TPU v7x, 32 devices: a whole 2x2x4 slice. The times are simulated.
32 devices in a mesh: parts: 2 (over x), group: 16 (over z, y, core).
Axes of the slice: x: 2, y: 2, z: 4, core: 2. Of those that a mesh axis runs over, the one named last changes fastest.
Arguments:
- solve_cols: bfloat16 [64, 512, 512], P(('parts', 'group')), parts along dimension 0
- region_groups: int32 [32, 4], P('group'), may hold values from 0 to 15, as said below
Outputs:
- schur: float32 [32, 7, 128, 128], P(('parts', 'group')), parts along dimension 0
There are 2 independent parts, one for each index of `parts`. A program takes and returns all parts, laid end to end along the dimension named above; an argument that names none is the same for every part. Nothing has to cross between parts.
Inputs may be any that keep to these rules, and one draw needn't show every extreme that they name: `region_groups`: the 4 groups of a region are 4 consecutive groups modulo 16, in any order. The 2 regions of one device together name 8 consecutive groups modulo 16, each once, so the slots of one device name one group at most 1 times, and exactly 1 times for some group.
All inputs are finite; a program needn't handle non-finite values.
Results may differ from a plain program's by a relative error of at most 0.00048.
Values may be sent and summed in bfloat16 or wider, within the bound.
No kernel may reach another device: no remote copies, remote signals or barrier semaphores. Data moves between devices by JAX's collectives and lax.ppermute only.
A program may use at most 128 MiB of HBM per device.

v0:
```python
import functools

import jax
import jax.numpy as jnp
from jax import lax
from jax.experimental import pallas as pl
from jax.experimental.pallas import tpu as pltpu
from jax.sharding import PartitionSpec as P

VMEM_BYTES = 48 * 1024 * 1024
LEAST_POWER = -100.0
TOP_POWER = 13.0
CHUNKS = 2
CORES = 2
COPIES = 2
TILE = 16


def packed_rows(width):
    return width // 2 + TILE


def unit_rows(width, slot_count):
    return packed_rows(width) + (slot_count - 1) * width


def parts_of(chunk, slot_count):
    halves = [(turn, at) for turn in range(1, slot_count) for at in range(2)]
    size = len(halves) // CHUNKS
    return halves[chunk * size : (chunk + 1) * size]


def row_range(chunk, width, slot_count):
    size = len(parts_of(chunk, slot_count)) * (width // 2)
    first = packed_rows(width) + chunk * size
    return (0 if chunk == 0 else first), first + size


def sum_rows(chunk, width, slot_count):
    count = 2 * len(parts_of(chunk, slot_count)) * (width // 2)
    return count + (packed_rows(width) if chunk == 0 else 0)


def half_iota(width):
    shape = (width // 2, width)
    return (
        lax.broadcasted_iota(jnp.int32, shape, 0),
        lax.broadcasted_iota(jnp.int32, shape, 1),
    )


def pack(block, tag):
    width = block.shape[1]
    half = width // 2
    row, col = half_iota(width)
    lower = pltpu.roll(block[half:], half, 1)
    packed = jnp.where((col >= half) | (row <= col), block[:half], lower)
    diagonal = jnp.sum(jnp.where(row == col, lower, 0.0), axis=0, keepdims=True)
    rest = jnp.where(col[:1] < half, diagonal, tag)
    return packed, jnp.broadcast_to(rest, (TILE, width))


def unpack(packed, diagonal):
    half, width = packed.shape
    row, col = half_iota(width)
    turned = jnp.concatenate([packed, jnp.zeros_like(packed)], axis=0).T
    upper = jnp.where((col >= half) | (row <= col), packed, turned[:half])
    last = jnp.where(row > col, packed, jnp.where(row < col, turned[:half], diagonal))
    return upper, jnp.where(col < half, turned[half:], pltpu.roll(last, half, 1))


def gram_kernel(total_groups, half, groups_hbm, cols_hbm, *refs):
    groups_ref, cols_ref, rows_ref, groups_sem, cols_sems = refs[-5:]
    send_refs = refs[:-5]
    region_count, slot_count = groups_ref.shape
    width = cols_ref.shape[2] // slot_count
    me = lax.axis_index("group")
    my_half, my_slot = me // half, lax.rem(me, half)
    groups_copy = pltpu.make_async_copy(groups_hbm, groups_ref, groups_sem)
    groups_copy.start()

    depth = cols_ref.shape[1] // COPIES

    def cols_copy(region, part):
        rows = pl.ds(part * depth, depth)
        return pltpu.make_async_copy(
            cols_hbm.at[region, rows], cols_ref.at[region, rows], cols_sems.at[region, part]
        )

    for region in range(region_count):
        for part in range(COPIES):
            cols_copy(region, part).start()
    groups_copy.wait()
    packed = packed_rows(width)

    def add_region(region, carry):
        for part in range(COPIES):
            cols_copy(region, part).wait()
        cols = cols_ref[region]
        gram = lax.dot_general(
            cols, cols, (((0,), (0,)), ((), ())), preferred_element_type=jnp.float32
        )
        groups = [groups_ref[region, s] for s in range(slot_count)]

        def ahead(s, t):
            return lax.rem(groups[t] - groups[s] + total_groups, total_groups)

        for s in range(slot_count):
            place = 0
            for t in range(slot_count):
                if t != s:
                    place = place + (ahead(t, s) < slot_count).astype(jnp.int32)
            away = (groups[s] // half != my_half).astype(jnp.int32)
            tag = (place + slot_count * away).astype(jnp.float32)
            slot = lax.rem(groups[s], half) ^ my_slot
            for t in range(slot_count):
                block = gram[s * width : (s + 1) * width, t * width : (t + 1) * width]
                if t == s:
                    block, rest = pack(block, tag)
                    rows_ref[slot, : width // 2] = block.astype(rows_ref.dtype)
                    rows_ref[slot, width // 2 : packed] = rest.astype(rows_ref.dtype)
                else:
                    gap = ahead(s, t)
                    turn = jnp.where(gap < slot_count, gap, gap - total_groups + slot_count)
                    at = pl.multiple_of(packed + (turn - 1) * width, TILE)
                    rows_ref[slot, pl.ds(at, width)] = block.astype(rows_ref.dtype)
        return carry

    lax.fori_loop(0, region_count, add_region, 0, unroll=region_count <= 2)
    for at, send_ref in enumerate(send_refs):
        first, last = row_range(at // CORES, width, slot_count)
        for pair in range(send_ref.shape[0]):
            send_ref[pair] = rows_ref[CORES * pair + at % CORES, first:last]


def sum_kernel(chunk, slot_count, *refs):
    arrays, (sums_ref, scaled_ref) = refs[:-2], refs[-2:]
    width = sums_ref.shape[1]
    half, packed = width // 2, packed_rows(width)
    count = sum_rows(chunk, width, slot_count)
    base = packed if chunk == 0 else 0
    sums_ref[...] = jnp.zeros_like(sums_ref)

    def units(arrays):
        return [(arrays[0], 0), (arrays[1], 0)] + [
            (x, core) for x in arrays[2:] for core in range(CORES)
        ]

    array_count = len(arrays) if chunk == 0 else len(arrays) // 2
    tags = [
        jnp.max(ref[at, half:packed].astype(jnp.float32)[TILE - 1 :, width - 1 :]).astype(
            jnp.int32
        )
        for ref, at in units(arrays[:array_count])
    ]
    for tag, (ref, at) in zip(tags, units(arrays[-array_count:])):
        away = tag // slot_count
        place = tag - slot_count * away
        if chunk == 0:
            to = pl.ds(pl.multiple_of(count * away, TILE), packed)
            sums_ref[to] += ref[at, :packed].astype(jnp.float32)
        for part, (turn, _) in enumerate(parts_of(chunk, slot_count)):
            wraps = (place + turn >= slot_count).astype(jnp.int32)
            to = count * away + base + (2 * part + wraps) * half
            block = ref[at, base + part * half : base + (part + 1) * half]
            sums_ref[pl.ds(pl.multiple_of(to, TILE), half)] += block.astype(jnp.float32)

    if chunk == 0:
        col = lax.broadcasted_iota(jnp.int32, (TILE, width), 1)
        for at in (half, count + half):
            sums_ref[at : at + TILE] = jnp.where(col < half, sums_ref[at : at + TILE], 0.0)

    tops = jnp.max(jnp.abs(sums_ref[count:]), axis=0, keepdims=True)
    largest = jnp.max(jnp.broadcast_to(tops, (8, width)), axis=1, keepdims=True)
    power = jnp.floor(jnp.log2(jnp.maximum(largest, 2.0**LEAST_POWER))) - TOP_POWER
    scaled_ref[:count] = sums_ref[count:] * jnp.exp2(-power)[0:1]
    scaled_ref[count:] = jnp.broadcast_to(power[0:1], (TILE, width))


def merge_kernel(keep_ref, got_ref, *refs):
    after_ref, send_refs = refs[0], refs[1:]
    pair_count = keep_ref.shape[0]
    for at in range(1, pair_count):
        send_refs[at - 1][0] = keep_ref[at]
        send_refs[at - 1][1] = got_ref[at]
    if len(send_refs) == pair_count:
        send_refs[-1][...] = after_ref[...]


def join_kernel(slot_count, *refs):
    out_hbm, joined_ref, sems = refs[-3:]
    width = joined_ref.shape[1]
    half, packed = width // 2, packed_rows(width)
    for chunk in range(CHUNKS):
        sums_ref, far_ref = refs[2 * chunk : 2 * chunk + 2]
        count = sum_rows(chunk, width, slot_count)
        factor = jnp.exp2(far_ref[count : count + 1])

        def joined(first, size):
            return sums_ref[first : first + size] + far_ref[first : first + size] * factor

        if chunk == 0:
            blocks = unpack(joined(0, half), joined(half, 8)[:1])
            for at, block in enumerate(blocks):
                joined_ref[slot_count - 1, at * half : (at + 1) * half] = block
        base = packed if chunk == 0 else 0
        for part, (turn, at) in enumerate(parts_of(chunk, slot_count)):
            for wraps in range(2):
                to = turn - slot_count * wraps + slot_count - 1
                joined_ref[to, at * half : (at + 1) * half] = joined(
                    base + (2 * part + wraps) * half, half
                )
    copies = [
        pltpu.make_async_copy(joined_ref.at[to], out_hbm.at[to], sems.at[to])
        for to in range(joined_ref.shape[0])
    ]
    for copy in copies:
        copy.start()
    for copy in copies:
        copy.wait()


def shards(solve_cols, region_groups):
    region_count, row_count, col_count = solve_cols.shape
    slot_count = region_groups.shape[1]
    width = col_count // slot_count
    total_groups = lax.axis_size("group")
    half = region_count * slot_count
    span_count = 2 * slot_count - 1
    pair_count = half // CORES
    params = pltpu.CompilerParams(vmem_limit_bytes=VMEM_BYTES)
    light = pl.CostEstimate(flops=0, bytes_accessed=0, transcendentals=0)
    vmem = pl.BlockSpec(memory_space=pltpu.VMEM)
    hbm = pl.BlockSpec(memory_space=pltpu.HBM)

    def permute(values, step):
        pairs = [(d, d ^ step) for d in range(total_groups)]
        return lax.ppermute(values, "group", pairs)

    def blocks(count, chunk):
        first, last = row_range(chunk, width, slot_count)
        return jax.ShapeDtypeStruct((count, last - first, width), solve_cols.dtype)

    sends = pl.pallas_call(
        functools.partial(gram_kernel, total_groups, half),
        in_specs=[hbm] * 2,
        out_specs=[vmem] * (CHUNKS * CORES),
        out_shape=[blocks(pair_count, chunk) for chunk in range(CHUNKS) for _ in range(CORES)],
        scratch_shapes=[
            pltpu.SMEM(region_groups.shape, region_groups.dtype),
            pltpu.VMEM(solve_cols.shape, solve_cols.dtype),
            pltpu.VMEM((half, unit_rows(width, slot_count), width), solve_cols.dtype),
            pltpu.SemaphoreType.DMA,
            pltpu.SemaphoreType.DMA((region_count, COPIES)),
        ],
        cost_estimate=light,
        compiler_params=params,
        name="gram_rows",
    )(
        pltpu.with_memory_space_constraint(region_groups, pltpu.HBM),
        pltpu.with_memory_space_constraint(solve_cols, pltpu.HBM),
    )

    pieces, tagged = [], []
    for chunk in range(CHUNKS):
        keep, give = sends[CORES * chunk : CORES * (chunk + 1)]
        gots = [keep, permute(give if chunk == 0 else later, 1)]
        after = sends[CORES + 1] if chunk == 0 else tagged[CORES]
        merged = pl.pallas_call(
            merge_kernel,
            out_shape=[blocks(CORES, chunk)] * (pair_count - 1)
            + ([blocks(pair_count, 1)] if chunk == 0 else []),
            cost_estimate=light,
            compiler_params=params,
            name="merge_units",
        )(*gots, after)
        later = merged[-1]
        for pair in range(pair_count - 1, 0, -1):
            gots.append(permute(merged[pair - 1], CORES * pair))
        tagged = tagged or gots
        count = sum_rows(chunk, width, slot_count)
        sums, scaled = pl.pallas_call(
            functools.partial(sum_kernel, chunk, slot_count),
            out_shape=(
                jax.ShapeDtypeStruct((2 * count, width), jnp.float32),
                jax.ShapeDtypeStruct((count + TILE, width), jnp.float32),
            ),
            cost_estimate=light,
            compiler_params=params,
            name="sum_offsets",
        )(*(tagged if chunk == 0 else tagged + gots))
        far = permute(scaled.astype(jnp.float16), half)
        pieces += [sums, far.astype(jnp.float32)]

    return pl.pallas_call(
        functools.partial(join_kernel, slot_count),
        in_specs=[vmem] * len(pieces),
        out_specs=hbm,
        out_shape=jax.ShapeDtypeStruct((span_count, width, width), jnp.float32),
        scratch_shapes=[
            pltpu.VMEM((span_count, width, width), jnp.float32),
            pltpu.SemaphoreType.DMA((span_count,)),
        ],
        cost_estimate=light,
        compiler_params=params,
        name="join_offsets",
    )(*pieces)[None]


def solution(mesh):
    return jax.shard_map(
        shards,
        mesh=mesh,
        in_specs=(P(("parts", "group"), None, None), P("group", None)),
        out_specs=P(("parts", "group"), None, None, None),
        check_vma=False,
    )
```

profile of v0, /device:TPU:0, one launch (start us, length us, event | category | flops | bytes accessed | tf_op | source)
XLA Modules:
  0.0 30.2 jit_solution(4744995821669380280)
XLA Ops:
  0.0 2.2 %gram_rows.1 = (bf16[4,272,128]{2,1,0:T(8,128)(2,1)S(1)}, bf16[4,272,128]{2,1,0:T(8,128)(2,1)S(1)}, bf16[4,192,128]{2,1,0:T(8,128)(2,1)S(1)}, bf16[4,192,128]{2,1,0:T(8,128)(2,1)S(1)}) custom-call(s32[2,4]{1,0:T(2,128)} %groups_hbm.1, bf16[2,512,512]{2,1,0:T(8,128)(2,1)} %cols_hbm.1), custom_call_target="tpu_custom_call" | custom-call | tf_op jit(solution)/shard_map/gram_rows/pallas_call | solution.py:244
  2.2 0.5 %collective-permute-start = (bf16[4,272,128]{2,1,0:T(8,128)(2,1)S(1)}, bf16[4,272,128]{2,1,0:T(8,128)(2,1)S(1)}, u32[]{:S(2)}, u32[]{:S(2)}) collective-permute-start(bf16[4,272,128]{2,1,0:T(8,128)(2,1)S(1)} %get-tuple-element.21), channel_id=1, source_target_pairs={{0,1},{1,0},{2,3},{3,2},{4,5},{5,4},{6,7},{7,6},{8,9},{9,8},{10,11... | collective-permute-start | bytes 835592 | tf_op jit(solution)/shard_map/ppermute | solution.py:238
  2.8 1.2 %collective-permute-done.got_ref.refs_1_ = bf16[4,272,128]{2,1,0:T(8,128)(2,1)S(1)} collective-permute-done((bf16[4,272,128]{2,1,0:T(8,128)(2,1)S(1)}, bf16[4,272,128]{2,1,0:T(8,128)(2,1)S(1)}, u32[]{:S(2)}, u32[]{:S(2)}) %collective-permute-start) | collective-permute-done | bytes 278560 | tf_op jit(solution)/shard_map/ppermute | solution.py:238
  4.0 0.4 %collective-permute-start.5 = (bf16[4,192,128]{2,1,0:T(8,128)(2,1)S(1)}, bf16[4,192,128]{2,1,0:T(8,128)(2,1)S(1)}, u32[]{:S(2)}, u32[]{:S(2)}) collective-permute-start(bf16[4,192,128]{2,1,0:T(8,128)(2,1)S(1)} %get-tuple-element.29), channel_id=1, source_target_pairs={{0,1},{1,0},{2,3},{3,2},{4,5},{5,4},{6,7},{7,6},{8,9},{9,8},{10,11... | collective-permute-start | bytes 589832 | tf_op jit(solution)/shard_map/ppermute | solution.py:238
  4.4 3.7 %collective-permute-start.1 = (bf16[2,272,128]{2,1,0:T(8,128)(2,1)S(1)}, bf16[2,272,128]{2,1,0:T(8,128)(2,1)S(1)}, u32[]{:S(2)}, u32[]{:S(2)}) collective-permute-start(bf16[2,272,128]{2,1,0:T(8,128)(2,1)S(1)} %get-tuple-element.23), channel_id=1, source_target_pairs={{0,6},{1,7},{2,4},{3,5},{4,2},{5,3},{6,0},{7,1},{8,14},{9,15},{10,... | collective-permute-start | bytes 417800 | tf_op jit(solution)/shard_map/ppermute | solution.py:238
  8.1 0.4 %collective-permute-start.2 = (bf16[2,272,128]{2,1,0:T(8,128)(2,1)S(1)}, bf16[2,272,128]{2,1,0:T(8,128)(2,1)S(1)}, u32[]{:S(2)}, u32[]{:S(2)}) collective-permute-start(bf16[2,272,128]{2,1,0:T(8,128)(2,1)S(1)} %get-tuple-element.24), channel_id=1, source_target_pairs={{0,4},{1,5},{2,6},{3,7},{4,0},{5,1},{6,2},{7,3},{8,12},{9,13},{10,... | collective-permute-start | bytes 417800 | tf_op jit(solution)/shard_map/ppermute | solution.py:238
  8.5 0.1 collective-permute-start.3
  8.7 3.9 %collective-permute-done.1.refs_2_.refs_0_ = bf16[2,272,128]{2,1,0:T(8,128)(2,1)S(1)} collective-permute-done((bf16[2,272,128]{2,1,0:T(8,128)(2,1)S(1)}, bf16[2,272,128]{2,1,0:T(8,128)(2,1)S(1)}, u32[]{:S(2)}, u32[]{:S(2)}) %collective-permute-start.1) | collective-permute-done | bytes 139296 | tf_op jit(solution)/shard_map/ppermute | solution.py:238
  12.6 0.0 collective-permute-done.5.got_ref.refs_6_
  12.6 3.0 %collective-permute-start.6 = (bf16[2,192,128]{2,1,0:T(8,128)(2,1)S(1)}, bf16[2,192,128]{2,1,0:T(8,128)(2,1)S(1)}, u32[]{:S(2)}, u32[]{:S(2)}) collective-permute-start(bf16[2,192,128]{2,1,0:T(8,128)(2,1)S(1)} %get-tuple-element.30), channel_id=1, source_target_pairs={{0,6},{1,7},{2,4},{3,5},{4,2},{5,3},{6,0},{7,1},{8,14},{9,15},{10,... | collective-permute-start | bytes 294920 | tf_op jit(solution)/shard_map/ppermute | solution.py:238
  15.6 0.4 %collective-permute-start.7 = (bf16[2,192,128]{2,1,0:T(8,128)(2,1)S(1)}, bf16[2,192,128]{2,1,0:T(8,128)(2,1)S(1)}, u32[]{:S(2)}, u32[]{:S(2)}) collective-permute-start(bf16[2,192,128]{2,1,0:T(8,128)(2,1)S(1)} %get-tuple-element.31), channel_id=1, source_target_pairs={{0,4},{1,5},{2,6},{3,7},{4,0},{5,1},{6,2},{7,3},{8,12},{9,13},{10,... | collective-permute-start | bytes 294920 | tf_op jit(solution)/shard_map/ppermute | solution.py:238
  16.1 0.2 collective-permute-start.8
  16.3 0.0 collective-permute-done.2.refs_3_
  16.3 0.0 collective-permute-done.3.refs_4_
  16.3 0.4 %sum_offsets.2 = (f32[928,128]{1,0:T(8,128)S(1)}, f32[480,128]{1,0:T(8,128)S(1)}) custom-call(bf16[4,272,128]{2,1,0:T(8,128)(2,1)S(1)} %get-tuple-element.20.keep_ref.refs_0_, bf16[4,272,128]{2,1,0:T(8,128)(2,1)S(1)} %collective-permute-done.got_ref.refs_1_, bf16[2,272,128]{2,1,0:T(8,128)(2,1)S(1)} %collective-permute-done.1.refs_2_.refs_0_, ...), custom_call_target="tpu_custom_call" | custom-call | tf_op jit(solution)/shard_map/sum_offsets/pallas_call | solution.py:282
  16.7 2.9 %collective-permute-start.4 = (f16[480,128]{1,0:T(8,128)(2,1)S(1)}, f16[480,128]{1,0:T(8,128)(2,1)S(1)}, u32[]{:S(2)}, u32[]{:S(2)}) collective-permute-start(f16[480,128]{1,0:T(8,128)(2,1)S(1)} %convert_element_type.12), channel_id=1, source_target_pairs={{0,8},{1,9},{2,10},{3,11},{4,12},{5,13},{6,14},{7,15},{8,0},{9,1},... | collective-permute-start | bytes 368648 | tf_op jit(solution)/shard_map/ppermute | solution.py:238
  19.6 0.0 collective-permute-done.6.refs_7_
  19.6 2.3 %collective-permute-done.7.refs_8_ = bf16[2,192,128]{2,1,0:T(8,128)(2,1)S(1)} collective-permute-done((bf16[2,192,128]{2,1,0:T(8,128)(2,1)S(1)}, bf16[2,192,128]{2,1,0:T(8,128)(2,1)S(1)}, u32[]{:S(2)}, u32[]{:S(2)}) %collective-permute-start.7) | collective-permute-done | bytes 98336 | tf_op jit(solution)/shard_map/ppermute | solution.py:238
  21.9 0.0 collective-permute-done.8.refs_9_
  21.9 0.4 %sum_offsets.3 = (f32[768,128]{1,0:T(8,128)S(1)}, f32[400,128]{1,0:T(8,128)S(1)}) custom-call(bf16[4,272,128]{2,1,0:T(8,128)(2,1)S(1)} %get-tuple-element.20.keep_ref.refs_0_, bf16[4,272,128]{2,1,0:T(8,128)(2,1)S(1)} %collective-permute-done.got_ref.refs_1_, bf16[2,272,128]{2,1,0:T(8,128)(2,1)S(1)} %collective-permute-done.1.refs_2_.refs_0_, ...), custom_call_target="tpu_custom_call" | custom-call | tf_op jit(solution)/shard_map/sum_offsets/pallas_call | solution.py:282
  22.3 2.2 %collective-permute-start.9 = (f16[400,128]{1,0:T(8,128)(2,1)S(1)}, f16[400,128]{1,0:T(8,128)(2,1)S(1)}, u32[]{:S(2)}, u32[]{:S(2)}) collective-permute-start(f16[400,128]{1,0:T(8,128)(2,1)S(1)} %convert_element_type.14), channel_id=1, source_target_pairs={{0,8},{1,9},{2,10},{3,11},{4,12},{5,13},{6,14},{7,15},{8,0},{9,1},... | collective-permute-start | bytes 307208 | tf_op jit(solution)/shard_map/ppermute | solution.py:238
  24.5 1.6 %collective-permute-done.4 = f16[480,128]{1,0:T(8,128)(2,1)S(1)} collective-permute-done((f16[480,128]{1,0:T(8,128)(2,1)S(1)}, f16[480,128]{1,0:T(8,128)(2,1)S(1)}, u32[]{:S(2)}, u32[]{:S(2)}) %collective-permute-start.4) | collective-permute-done | bytes 122912 | tf_op jit(solution)/shard_map/ppermute | solution.py:238
  26.1 3.1 %collective-permute-done.9 = f16[400,128]{1,0:T(8,128)(2,1)S(1)} collective-permute-done((f16[400,128]{1,0:T(8,128)(2,1)S(1)}, f16[400,128]{1,0:T(8,128)(2,1)S(1)}, u32[]{:S(2)}, u32[]{:S(2)}) %collective-permute-start.9) | collective-permute-done | bytes 102432 | tf_op jit(solution)/shard_map/ppermute | solution.py:238
  29.2 1.0 %join_offsets.1 = f32[7,128,128]{2,1,0:T(8,128)} custom-call(f32[928,128]{1,0:T(8,128)S(1)} %get-tuple-element.26.refs_0_, f32[480,128]{1,0:T(8,128)S(1)} %convert_element_type.13.refs_1_, f32[768,128]{1,0:T(8,128)S(1)} %get-tuple-element.33.refs_2_, f32[400,128]{1,0:T(8,128)S(1)} %convert_element_type.15.refs_3_), custom_call_target="tpu_custom_call" | custom-call | tf_op jit(solution)/shard_map/join_offsets/pallas_call | solution.py:295
  (6 shorter events, 0.1 us)
Async XLA Ops:
  2.2 1.7 %collective-permute-start = (bf16[4,272,128]{2,1,0:T(8,128)(2,1)S(1)}, bf16[4,272,128]{2,1,0:T(8,128)(2,1)S(1)}, u32[]{:S(2)}, u32[]{:S(2)}) collective-permute-start(bf16[4,272,128]{2,1,0:T(8,128)(2,1)S(1)} %get-tuple-element.21), channel_id=1, source_target_pairs={{0,1},{1,0},{2,3},{3,2},{4,5},{5,4},{6,7},{7,6},{8,9},{9,8},{10,11... | collective-permute-start | bytes 835592 | tf_op jit(solution)/shard_map/ppermute | solution.py:238
  4.0 8.6 %collective-permute-start.5 = (bf16[4,192,128]{2,1,0:T(8,128)(2,1)S(1)}, bf16[4,192,128]{2,1,0:T(8,128)(2,1)S(1)}, u32[]{:S(2)}, u32[]{:S(2)}) collective-permute-start(bf16[4,192,128]{2,1,0:T(8,128)(2,1)S(1)} %get-tuple-element.29), channel_id=1, source_target_pairs={{0,1},{1,0},{2,3},{3,2},{4,5},{5,4},{6,7},{7,6},{8,9},{9,8},{10,11... | collective-permute-start | bytes 589832 | tf_op jit(solution)/shard_map/ppermute | solution.py:238
  4.4 8.2 %collective-permute-start.1 = (bf16[2,272,128]{2,1,0:T(8,128)(2,1)S(1)}, bf16[2,272,128]{2,1,0:T(8,128)(2,1)S(1)}, u32[]{:S(2)}, u32[]{:S(2)}) collective-permute-start(bf16[2,272,128]{2,1,0:T(8,128)(2,1)S(1)} %get-tuple-element.23), channel_id=1, source_target_pairs={{0,6},{1,7},{2,4},{3,5},{4,2},{5,3},{6,0},{7,1},{8,14},{9,15},{10,... | collective-permute-start | bytes 417800 | tf_op jit(solution)/shard_map/ppermute | solution.py:238
  8.1 8.2 %collective-permute-start.2 = (bf16[2,272,128]{2,1,0:T(8,128)(2,1)S(1)}, bf16[2,272,128]{2,1,0:T(8,128)(2,1)S(1)}, u32[]{:S(2)}, u32[]{:S(2)}) collective-permute-start(bf16[2,272,128]{2,1,0:T(8,128)(2,1)S(1)} %get-tuple-element.24), channel_id=1, source_target_pairs={{0,4},{1,5},{2,6},{3,7},{4,0},{5,1},{6,2},{7,3},{8,12},{9,13},{10,... | collective-permute-start | bytes 417800 | tf_op jit(solution)/shard_map/ppermute | solution.py:238
  8.5 7.7 %collective-permute-start.3 = (bf16[2,272,128]{2,1,0:T(8,128)(2,1)S(1)}, bf16[2,272,128]{2,1,0:T(8,128)(2,1)S(1)}, u32[]{:S(2)}, u32[]{:S(2)}) collective-permute-start(bf16[2,272,128]{2,1,0:T(8,128)(2,1)S(1)} %get-tuple-element.25), channel_id=1, source_target_pairs={{0,2},{1,3},{2,0},{3,1},{4,6},{5,7},{6,4},{7,5},{8,10},{9,11},{10,... | collective-permute-start | bytes 417800 | tf_op jit(solution)/shard_map/ppermute | solution.py:238
  12.6 7.0 %collective-permute-start.6 = (bf16[2,192,128]{2,1,0:T(8,128)(2,1)S(1)}, bf16[2,192,128]{2,1,0:T(8,128)(2,1)S(1)}, u32[]{:S(2)}, u32[]{:S(2)}) collective-permute-start(bf16[2,192,128]{2,1,0:T(8,128)(2,1)S(1)} %get-tuple-element.30), channel_id=1, source_target_pairs={{0,6},{1,7},{2,4},{3,5},{4,2},{5,3},{6,0},{7,1},{8,14},{9,15},{10,... | collective-permute-start | bytes 294920 | tf_op jit(solution)/shard_map/ppermute | solution.py:238
  15.6 6.3 %collective-permute-start.7 = (bf16[2,192,128]{2,1,0:T(8,128)(2,1)S(1)}, bf16[2,192,128]{2,1,0:T(8,128)(2,1)S(1)}, u32[]{:S(2)}, u32[]{:S(2)}) collective-permute-start(bf16[2,192,128]{2,1,0:T(8,128)(2,1)S(1)} %get-tuple-element.31), channel_id=1, source_target_pairs={{0,4},{1,5},{2,6},{3,7},{4,0},{5,1},{6,2},{7,3},{8,12},{9,13},{10,... | collective-permute-start | bytes 294920 | tf_op jit(solution)/shard_map/ppermute | solution.py:238
  16.1 5.8 %collective-permute-start.8 = (bf16[2,192,128]{2,1,0:T(8,128)(2,1)S(1)}, bf16[2,192,128]{2,1,0:T(8,128)(2,1)S(1)}, u32[]{:S(2)}, u32[]{:S(2)}) collective-permute-start(bf16[2,192,128]{2,1,0:T(8,128)(2,1)S(1)} %get-tuple-element.32), channel_id=1, source_target_pairs={{0,2},{1,3},{2,0},{3,1},{4,6},{5,7},{6,4},{7,5},{8,10},{9,11},{10,... | collective-permute-start | bytes 294920 | tf_op jit(solution)/shard_map/ppermute | solution.py:238
  16.7 9.3 %collective-permute-start.4 = (f16[480,128]{1,0:T(8,128)(2,1)S(1)}, f16[480,128]{1,0:T(8,128)(2,1)S(1)}, u32[]{:S(2)}, u32[]{:S(2)}) collective-permute-start(f16[480,128]{1,0:T(8,128)(2,1)S(1)} %convert_element_type.12), channel_id=1, source_target_pairs={{0,8},{1,9},{2,10},{3,11},{4,12},{5,13},{6,14},{7,15},{8,0},{9,1},... | collective-permute-start | bytes 368648 | tf_op jit(solution)/shard_map/ppermute | solution.py:238
  22.3 6.9 %collective-permute-start.9 = (f16[400,128]{1,0:T(8,128)(2,1)S(1)}, f16[400,128]{1,0:T(8,128)(2,1)S(1)}, u32[]{:S(2)}, u32[]{:S(2)}) collective-permute-start(f16[400,128]{1,0:T(8,128)(2,1)S(1)} %convert_element_type.14), channel_id=1, source_target_pairs={{0,8},{1,9},{2,10},{3,11},{4,12},{5,13},{6,14},{7,15},{8,0},{9,1},... | collective-permute-start | bytes 307208 | tf_op jit(solution)/shard_map/ppermute | solution.py:238
where the time goes:
time: 30.3 us; the launch traced here: 30.2 us
  starting transfers between devices  13.9 us (46%)
  waiting for transfers between devices  12.1 us (40%)
  Pallas kernels  4.02 us (13%)
    ppermute x10, starting transfers between devices, permute(): return lax.ppermute(values, 'group', pairs)  13.9 us
    ppermute x10, waiting for transfers between devices, permute(): return lax.ppermute(values, 'group', pairs)  12.1 us
    pallas_call x1, Pallas kernels, shards(): pl.pallas_call(functools.partial(gram_kernel, total_groups, half), in_spe...  2.22 us
    pallas_call x1, Pallas kernels, shards(): pl.pallas_call(functools.partial(join_kernel, slot_count), in_specs=[vmem...  0.99 us
    pallas_call x2, Pallas kernels, shards(): pl.pallas_call(functools.partial(sum_kernel, chunk, slot_count), out_shap...  0.75 us
  transfers between devices with their start and end apart: 10, of which 5 were waited for; matrix products, arithmetic and copies ran while one was open for 0% of the time, Pallas kernels for 3%

commit v1 on v0

--- a/solution.py
+++ b/solution.py
@@ -187,35 +187,38 @@
         send_refs[-1][...] = after_ref[...]
 
 
-def join_kernel(slot_count, *refs):
+def join_kernel(chunk, slot_count, sums_ref, far_ref, *refs):
     out_hbm, joined_ref, sems = refs[-3:]
-    width = joined_ref.shape[1]
+    width = joined_ref.shape[2]
     half, packed = width // 2, packed_rows(width)
-    for chunk in range(CHUNKS):
-        sums_ref, far_ref = refs[2 * chunk : 2 * chunk + 2]
-        count = sum_rows(chunk, width, slot_count)
-        factor = jnp.exp2(far_ref[count : count + 1])
-
-        def joined(first, size):
-            return sums_ref[first : first + size] + far_ref[first : first + size] * factor
-
-        if chunk == 0:
-            blocks = unpack(joined(0, half), joined(half, 8)[:1])
-            for at, block in enumerate(blocks):
-                joined_ref[slot_count - 1, at * half : (at + 1) * half] = block
-        base = packed if chunk == 0 else 0
-        for part, (turn, at) in enumerate(parts_of(chunk, slot_count)):
-            for wraps in range(2):
-                to = turn - slot_count * wraps + slot_count - 1
-                joined_ref[to, at * half : (at + 1) * half] = joined(
-                    base + (2 * part + wraps) * half, half
-                )
-    copies = [
-        pltpu.make_async_copy(joined_ref.at[to], out_hbm.at[to], sems.at[to])
-        for to in range(joined_ref.shape[0])
-    ]
-    for copy in copies:
-        copy.start()
+    count = sum_rows(chunk, width, slot_count)
+    factor = jnp.exp2(far_ref[count : count + 1])
+    copies = []
+
+    def joined(first, size):
+        return sums_ref[first : first + size] + far_ref[first : first + size] * factor
+
+    def put(block, offset, at):
+        place = len(copies)
+        joined_ref[place] = block
+        copies.append(
+            pltpu.make_async_copy(
+                joined_ref.at[place],
+                out_hbm.at[offset + slot_count - 1, at * half : (at + 1) * half],
+                sems.at[place],
+            )
+        )
+        copies[-1].start()
+
+    base = 0
+    if chunk == 0:
+        base = packed
+        for at, block in enumerate(unpack(joined(0, half), joined(half, 8)[:1])):
+            put(block, 0, at)
+    for part, (turn, at) in enumerate(parts_of(chunk, slot_count)):
+        for wraps in range(2):
+            first = base + (2 * part + wraps) * half
+            put(joined(first, half), turn - slot_count * wraps, at)
     for copy in copies:
         copy.wait()
 
@@ -254,7 +257,9 @@
             pltpu.SemaphoreType.DMA((region_count, COPIES)),
         ],
         cost_estimate=light,
-        compiler_params=params,
+        compiler_params=pltpu.CompilerParams(
+            vmem_limit_bytes=VMEM_BYTES, fuse_transposed_lhs_in_matmul=True
+        ),
         name="gram_rows",
     )(
         pltpu.with_memory_space_constraint(region_groups, pltpu.HBM),
@@ -290,21 +295,28 @@
             name="sum_offsets",
         )(*(tagged if chunk == 0 else tagged + gots))
         far = permute(scaled.astype(jnp.float16), half)
-        pieces += [sums, far.astype(jnp.float32)]
-
-    return pl.pallas_call(
-        functools.partial(join_kernel, slot_count),
-        in_specs=[vmem] * len(pieces),
-        out_specs=hbm,
-        out_shape=jax.ShapeDtypeStruct((span_count, width, width), jnp.float32),
-        scratch_shapes=[
-            pltpu.VMEM((span_count, width, width), jnp.float32),
-            pltpu.SemaphoreType.DMA((span_count,)),
-        ],
-        cost_estimate=light,
-        compiler_params=params,
-        name="join_offsets",
-    )(*pieces)[None]
+        pieces.append((sums, far.astype(jnp.float32)))
+
+    schur = ()
+    for chunk in range(CHUNKS):
+        count = 2 * len(parts_of(chunk, slot_count)) + (2 if chunk == 0 else 0)
+        schur = (
+            pl.pallas_call(
+                functools.partial(join_kernel, chunk, slot_count),
+                in_specs=[vmem] * 2 + [hbm] * len(schur),
+                out_specs=hbm,
+                out_shape=jax.ShapeDtypeStruct((span_count, width, width), jnp.float32),
+                input_output_aliases={2: 0} if schur else {},
+                scratch_shapes=[
+                    pltpu.VMEM((count, width // 2, width), jnp.float32),
+                    pltpu.SemaphoreType.DMA((count,)),
+                ],
+                cost_estimate=light,
+                compiler_params=params,
+                name="join_offsets",
+            )(*pieces[chunk], *schur),
+        )
+    return schur[0][None]
 
 
 def solution(mesh):

time: 30.3 us -> 30.5 us (level)
  Pallas kernels: 4.02 us -> 5.09 us
  waiting for transfers between devices: 12.1 us -> 11.2 us
    ppermute x10, waiting for transfers between devices: 12.1 us -> 11.2 us  [permute(): return lax.ppermute(values, 'group', pairs)]
    pallas_call x1 -> x2, Pallas kernels: 0.99 us -> 1.65 us  [shards(): pl.pallas_call(functools.partial(join_kernel, chunk, slot_count), in_spec...]
    pallas_call x1, Pallas kernels: 2.22 us -> 2.63 us  [shards(): pl.pallas_call(functools.partial(gram_kernel, total_groups, half), in_spe...]
  transfers between devices with their start and end apart: 10 -> 10, of which waited for: 5 -> 5; matrix products, arithmetic and copies ran while one was open for 0% -> 0% of each run, Pallas kernels for 3% -> 6%
where the time goes in v1:
time: 30.5 us; the launch traced here: 30.3 us
  starting transfers between devices  13.9 us (46%)
  waiting for transfers between devices  11.2 us (37%)
  Pallas kernels  5.09 us (17%)
    ppermute x10, starting transfers between devices, permute(): return lax.ppermute(values, 'group', pairs)  13.9 us
    ppermute x10, waiting for transfers between devices, permute(): return lax.ppermute(values, 'group', pairs)  11.2 us
    pallas_call x1, Pallas kernels, shards(): pl.pallas_call(functools.partial(gram_kernel, total_groups, half), in_spe...  2.63 us
    pallas_call x2, Pallas kernels, shards(): pl.pallas_call(functools.partial(join_kernel, chunk, slot_count), in_spec...  1.65 us
    pallas_call x2, Pallas kernels, shards(): pl.pallas_call(functools.partial(sum_kernel, chunk, slot_count), out_shap...  0.75 us
  transfers between devices with their start and end apart: 10, of which 5 were waited for; matrix products, arithmetic and copies ran while one was open for 0% of the time, Pallas kernels for 6%

profile of v1, /device:TPU:0, one launch (start us, length us, event | category | flops | bytes accessed | tf_op | source)
XLA Modules:
  0.0 30.3 jit_solution(11250103991945713619)
XLA Ops:
  0.0 2.6 %gram_rows.1 = (bf16[4,272,128]{2,1,0:T(8,128)(2,1)S(1)}, bf16[4,272,128]{2,1,0:T(8,128)(2,1)S(1)}, bf16[4,192,128]{2,1,0:T(8,128)(2,1)S(1)}, bf16[4,192,128]{2,1,0:T(8,128)(2,1)S(1)}) custom-call(s32[2,4]{1,0:T(2,128)} %groups_hbm.1, bf16[2,512,512]{2,1,0:T(8,128)(2,1)} %cols_hbm.1), custom_call_target="tpu_custom_call" | custom-call | tf_op jit(solution)/shard_map/gram_rows/pallas_call | solution.py:247
  2.6 0.5 %collective-permute-start = (bf16[4,272,128]{2,1,0:T(8,128)(2,1)S(1)}, bf16[4,272,128]{2,1,0:T(8,128)(2,1)S(1)}, u32[]{:S(2)}, u32[]{:S(2)}) collective-permute-start(bf16[4,272,128]{2,1,0:T(8,128)(2,1)S(1)} %get-tuple-element.21), channel_id=1, source_target_pairs={{0,1},{1,0},{2,3},{3,2},{4,5},{5,4},{6,7},{7,6},{8,9},{9,8},{10,11... | collective-permute-start | bytes 835592 | tf_op jit(solution)/shard_map/ppermute | solution.py:241
  3.1 1.2 %collective-permute-done.got_ref.refs_1_ = bf16[4,272,128]{2,1,0:T(8,128)(2,1)S(1)} collective-permute-done((bf16[4,272,128]{2,1,0:T(8,128)(2,1)S(1)}, bf16[4,272,128]{2,1,0:T(8,128)(2,1)S(1)}, u32[]{:S(2)}, u32[]{:S(2)}) %collective-permute-start) | collective-permute-done | bytes 278560 | tf_op jit(solution)/shard_map/ppermute | solution.py:241
  4.4 0.4 %collective-permute-start.4 = (bf16[4,192,128]{2,1,0:T(8,128)(2,1)S(1)}, bf16[4,192,128]{2,1,0:T(8,128)(2,1)S(1)}, u32[]{:S(2)}, u32[]{:S(2)}) collective-permute-start(bf16[4,192,128]{2,1,0:T(8,128)(2,1)S(1)} %get-tuple-element.27), channel_id=1, source_target_pairs={{0,1},{1,0},{2,3},{3,2},{4,5},{5,4},{6,7},{7,6},{8,9},{9,8},{10,11... | collective-permute-start | bytes 589832 | tf_op jit(solution)/shard_map/ppermute | solution.py:241
  4.8 3.7 %collective-permute-start.1 = (bf16[2,272,128]{2,1,0:T(8,128)(2,1)S(1)}, bf16[2,272,128]{2,1,0:T(8,128)(2,1)S(1)}, u32[]{:S(2)}, u32[]{:S(2)}) collective-permute-start(bf16[2,272,128]{2,1,0:T(8,128)(2,1)S(1)} %get-tuple-element.23), channel_id=1, source_target_pairs={{0,6},{1,7},{2,4},{3,5},{4,2},{5,3},{6,0},{7,1},{8,14},{9,15},{10,... | collective-permute-start | bytes 417800 | tf_op jit(solution)/shard_map/ppermute | solution.py:241
  8.5 0.4 %collective-permute-start.2 = (bf16[2,272,128]{2,1,0:T(8,128)(2,1)S(1)}, bf16[2,272,128]{2,1,0:T(8,128)(2,1)S(1)}, u32[]{:S(2)}, u32[]{:S(2)}) collective-permute-start(bf16[2,272,128]{2,1,0:T(8,128)(2,1)S(1)} %get-tuple-element.24), channel_id=1, source_target_pairs={{0,4},{1,5},{2,6},{3,7},{4,0},{5,1},{6,2},{7,3},{8,12},{9,13},{10,... | collective-permute-start | bytes 417800 | tf_op jit(solution)/shard_map/ppermute | solution.py:241
  8.9 0.1 collective-permute-start.3
  9.1 3.9 %collective-permute-done.1.refs_0_.refs_2_ = bf16[2,272,128]{2,1,0:T(8,128)(2,1)S(1)} collective-permute-done((bf16[2,272,128]{2,1,0:T(8,128)(2,1)S(1)}, bf16[2,272,128]{2,1,0:T(8,128)(2,1)S(1)}, u32[]{:S(2)}, u32[]{:S(2)}) %collective-permute-start.1) | collective-permute-done | bytes 139296 | tf_op jit(solution)/shard_map/ppermute | solution.py:241
  13.0 0.0 collective-permute-done.4.got_ref.refs_6_
  13.0 3.0 %collective-permute-start.5 = (bf16[2,192,128]{2,1,0:T(8,128)(2,1)S(1)}, bf16[2,192,128]{2,1,0:T(8,128)(2,1)S(1)}, u32[]{:S(2)}, u32[]{:S(2)}) collective-permute-start(bf16[2,192,128]{2,1,0:T(8,128)(2,1)S(1)} %get-tuple-element.28), channel_id=1, source_target_pairs={{0,6},{1,7},{2,4},{3,5},{4,2},{5,3},{6,0},{7,1},{8,14},{9,15},{10,... | collective-permute-start | bytes 294920 | tf_op jit(solution)/shard_map/ppermute | solution.py:241
  16.0 0.4 %collective-permute-start.6 = (bf16[2,192,128]{2,1,0:T(8,128)(2,1)S(1)}, bf16[2,192,128]{2,1,0:T(8,128)(2,1)S(1)}, u32[]{:S(2)}, u32[]{:S(2)}) collective-permute-start(bf16[2,192,128]{2,1,0:T(8,128)(2,1)S(1)} %get-tuple-element.29), channel_id=1, source_target_pairs={{0,4},{1,5},{2,6},{3,7},{4,0},{5,1},{6,2},{7,3},{8,12},{9,13},{10,... | collective-permute-start | bytes 294920 | tf_op jit(solution)/shard_map/ppermute | solution.py:241
  16.5 0.2 collective-permute-start.7
  16.7 0.0 collective-permute-done.2.refs_3_
  16.7 0.0 collective-permute-done.3.refs_4_
  16.7 0.4 %sum_offsets.3 = (f32[928,128]{1,0:T(8,128)S(1)}, f32[480,128]{1,0:T(8,128)S(1)}) custom-call(bf16[4,272,128]{2,1,0:T(8,128)(2,1)S(1)} %get-tuple-element.20.keep_ref.refs_0_, bf16[4,272,128]{2,1,0:T(8,128)(2,1)S(1)} %collective-permute-done.got_ref.refs_1_, bf16[2,272,128]{2,1,0:T(8,128)(2,1)S(1)} %collective-permute-done.1.refs_0_.refs_2_, ...), custom_call_target="tpu_custom_call" | custom-call | tf_op jit(solution)/shard_map/sum_offsets/pallas_call | solution.py:287
  17.1 2.9 %collective-permute-start.9 = (f16[480,128]{1,0:T(8,128)(2,1)S(1)}, f16[480,128]{1,0:T(8,128)(2,1)S(1)}, u32[]{:S(2)}, u32[]{:S(2)}) collective-permute-start(f16[480,128]{1,0:T(8,128)(2,1)S(1)} %convert_element_type.14), channel_id=1, source_target_pairs={{0,8},{1,9},{2,10},{3,11},{4,12},{5,13},{6,14},{7,15},{8,0},{9,1},... | collective-permute-start | bytes 368648 | tf_op jit(solution)/shard_map/ppermute | solution.py:241
  20.0 0.0 collective-permute-done.5.refs_7_
  20.0 2.2 %collective-permute-done.6.refs_8_ = bf16[2,192,128]{2,1,0:T(8,128)(2,1)S(1)} collective-permute-done((bf16[2,192,128]{2,1,0:T(8,128)(2,1)S(1)}, bf16[2,192,128]{2,1,0:T(8,128)(2,1)S(1)}, u32[]{:S(2)}, u32[]{:S(2)}) %collective-permute-start.6) | collective-permute-done | bytes 98336 | tf_op jit(solution)/shard_map/ppermute | solution.py:241
  22.3 0.0 collective-permute-done.7.refs_9_
  22.3 0.4 %sum_offsets.2 = (f32[768,128]{1,0:T(8,128)S(1)}, f32[400,128]{1,0:T(8,128)S(1)}) custom-call(bf16[4,272,128]{2,1,0:T(8,128)(2,1)S(1)} %get-tuple-element.20.keep_ref.refs_0_, bf16[4,272,128]{2,1,0:T(8,128)(2,1)S(1)} %collective-permute-done.got_ref.refs_1_, bf16[2,272,128]{2,1,0:T(8,128)(2,1)S(1)} %collective-permute-done.1.refs_0_.refs_2_, ...), custom_call_target="tpu_custom_call" | custom-call | tf_op jit(solution)/shard_map/sum_offsets/pallas_call | solution.py:287
  22.7 2.2 %collective-permute-start.8 = (f16[400,128]{1,0:T(8,128)(2,1)S(1)}, f16[400,128]{1,0:T(8,128)(2,1)S(1)}, u32[]{:S(2)}, u32[]{:S(2)}) collective-permute-start(f16[400,128]{1,0:T(8,128)(2,1)S(1)} %convert_element_type.12), channel_id=1, source_target_pairs={{0,8},{1,9},{2,10},{3,11},{4,12},{5,13},{6,14},{7,15},{8,0},{9,1},... | collective-permute-start | bytes 307208 | tf_op jit(solution)/shard_map/ppermute | solution.py:241
  24.9 1.6 %collective-permute-done.9 = f16[480,128]{1,0:T(8,128)(2,1)S(1)} collective-permute-done((f16[480,128]{1,0:T(8,128)(2,1)S(1)}, f16[480,128]{1,0:T(8,128)(2,1)S(1)}, u32[]{:S(2)}, u32[]{:S(2)}) %collective-permute-start.9) | collective-permute-done | bytes 122912 | tf_op jit(solution)/shard_map/ppermute | solution.py:241
  26.4 0.9 %join_offsets.2.refs_0_ = f32[7,128,128]{2,1,0:T(8,128)} custom-call(f32[928,128]{1,0:T(8,128)S(1)} %get-tuple-element.33.sums_ref, f32[480,128]{1,0:T(8,128)S(1)} %convert_element_type.15.far_ref), custom_call_target="tpu_custom_call" | custom-call | tf_op jit(solution)/shard_map/join_offsets/pallas_call | solution.py:304
  27.4 2.2 %collective-permute-done.8 = f16[400,128]{1,0:T(8,128)(2,1)S(1)} collective-permute-done((f16[400,128]{1,0:T(8,128)(2,1)S(1)}, f16[400,128]{1,0:T(8,128)(2,1)S(1)}, u32[]{:S(2)}, u32[]{:S(2)}) %collective-permute-start.8) | collective-permute-done | bytes 102432 | tf_op jit(solution)/shard_map/ppermute | solution.py:241
  29.6 0.7 %join_offsets.3 = f32[7,128,128]{2,1,0:T(8,128)} custom-call(f32[768,128]{1,0:T(8,128)S(1)} %get-tuple-element.31.sums_ref, f32[400,128]{1,0:T(8,128)S(1)} %convert_element_type.13.far_ref, f32[7,128,128]{2,1,0:T(8,128)} %join_offsets.2.refs_0_), custom_call_target="tpu_custom_call", output_to_operand_aliasing={{}: (2, {})} | custom-call | tf_op jit(solution)/shard_map/join_offsets/pallas_call | solution.py:304
  (6 shorter events, 0.1 us)
Async XLA Ops:
  2.6 1.7 %collective-permute-start = (bf16[4,272,128]{2,1,0:T(8,128)(2,1)S(1)}, bf16[4,272,128]{2,1,0:T(8,128)(2,1)S(1)}, u32[]{:S(2)}, u32[]{:S(2)}) collective-permute-start(bf16[4,272,128]{2,1,0:T(8,128)(2,1)S(1)} %get-tuple-element.21), channel_id=1, source_target_pairs={{0,1},{1,0},{2,3},{3,2},{4,5},{5,4},{6,7},{7,6},{8,9},{9,8},{10,11... | collective-permute-start | bytes 835592 | tf_op jit(solution)/shard_map/ppermute | solution.py:241
  4.4 8.6 %collective-permute-start.4 = (bf16[4,192,128]{2,1,0:T(8,128)(2,1)S(1)}, bf16[4,192,128]{2,1,0:T(8,128)(2,1)S(1)}, u32[]{:S(2)}, u32[]{:S(2)}) collective-permute-start(bf16[4,192,128]{2,1,0:T(8,128)(2,1)S(1)} %get-tuple-element.27), channel_id=1, source_target_pairs={{0,1},{1,0},{2,3},{3,2},{4,5},{5,4},{6,7},{7,6},{8,9},{9,8},{10,11... | collective-permute-start | bytes 589832 | tf_op jit(solution)/shard_map/ppermute | solution.py:241
  4.8 8.2 %collective-permute-start.1 = (bf16[2,272,128]{2,1,0:T(8,128)(2,1)S(1)}, bf16[2,272,128]{2,1,0:T(8,128)(2,1)S(1)}, u32[]{:S(2)}, u32[]{:S(2)}) collective-permute-start(bf16[2,272,128]{2,1,0:T(8,128)(2,1)S(1)} %get-tuple-element.23), channel_id=1, source_target_pairs={{0,6},{1,7},{2,4},{3,5},{4,2},{5,3},{6,0},{7,1},{8,14},{9,15},{10,... | collective-permute-start | bytes 417800 | tf_op jit(solution)/shard_map/ppermute | solution.py:241
  8.5 8.2 %collective-permute-start.2 = (bf16[2,272,128]{2,1,0:T(8,128)(2,1)S(1)}, bf16[2,272,128]{2,1,0:T(8,128)(2,1)S(1)}, u32[]{:S(2)}, u32[]{:S(2)}) collective-permute-start(bf16[2,272,128]{2,1,0:T(8,128)(2,1)S(1)} %get-tuple-element.24), channel_id=1, source_target_pairs={{0,4},{1,5},{2,6},{3,7},{4,0},{5,1},{6,2},{7,3},{8,12},{9,13},{10,... | collective-permute-start | bytes 417800 | tf_op jit(solution)/shard_map/ppermute | solution.py:241
  8.9 7.7 %collective-permute-start.3 = (bf16[2,272,128]{2,1,0:T(8,128)(2,1)S(1)}, bf16[2,272,128]{2,1,0:T(8,128)(2,1)S(1)}, u32[]{:S(2)}, u32[]{:S(2)}) collective-permute-start(bf16[2,272,128]{2,1,0:T(8,128)(2,1)S(1)} %get-tuple-element.25), channel_id=1, source_target_pairs={{0,2},{1,3},{2,0},{3,1},{4,6},{5,7},{6,4},{7,5},{8,10},{9,11},{10,... | collective-permute-start | bytes 417800 | tf_op jit(solution)/shard_map/ppermute | solution.py:241
  13.0 7.0 %collective-permute-start.5 = (bf16[2,192,128]{2,1,0:T(8,128)(2,1)S(1)}, bf16[2,192,128]{2,1,0:T(8,128)(2,1)S(1)}, u32[]{:S(2)}, u32[]{:S(2)}) collective-permute-start(bf16[2,192,128]{2,1,0:T(8,128)(2,1)S(1)} %get-tuple-element.28), channel_id=1, source_target_pairs={{0,6},{1,7},{2,4},{3,5},{4,2},{5,3},{6,0},{7,1},{8,14},{9,15},{10,... | collective-permute-start | bytes 294920 | tf_op jit(solution)/shard_map/ppermute | solution.py:241
  16.0 6.3 %collective-permute-start.6 = (bf16[2,192,128]{2,1,0:T(8,128)(2,1)S(1)}, bf16[2,192,128]{2,1,0:T(8,128)(2,1)S(1)}, u32[]{:S(2)}, u32[]{:S(2)}) collective-permute-start(bf16[2,192,128]{2,1,0:T(8,128)(2,1)S(1)} %get-tuple-element.29), channel_id=1, source_target_pairs={{0,4},{1,5},{2,6},{3,7},{4,0},{5,1},{6,2},{7,3},{8,12},{9,13},{10,... | collective-permute-start | bytes 294920 | tf_op jit(solution)/shard_map/ppermute | solution.py:241
  16.5 5.8 %collective-permute-start.7 = (bf16[2,192,128]{2,1,0:T(8,128)(2,1)S(1)}, bf16[2,192,128]{2,1,0:T(8,128)(2,1)S(1)}, u32[]{:S(2)}, u32[]{:S(2)}) collective-permute-start(bf16[2,192,128]{2,1,0:T(8,128)(2,1)S(1)} %get-tuple-element.30), channel_id=1, source_target_pairs={{0,2},{1,3},{2,0},{3,1},{4,6},{5,7},{6,4},{7,5},{8,10},{9,11},{10,... | collective-permute-start | bytes 294920 | tf_op jit(solution)/shard_map/ppermute | solution.py:241
  17.1 9.3 %collective-permute-start.9 = (f16[480,128]{1,0:T(8,128)(2,1)S(1)}, f16[480,128]{1,0:T(8,128)(2,1)S(1)}, u32[]{:S(2)}, u32[]{:S(2)}) collective-permute-start(f16[480,128]{1,0:T(8,128)(2,1)S(1)} %convert_element_type.14), channel_id=1, source_target_pairs={{0,8},{1,9},{2,10},{3,11},{4,12},{5,13},{6,14},{7,15},{8,0},{9,1},... | collective-permute-start | bytes 368648 | tf_op jit(solution)/shard_map/ppermute | solution.py:241
  22.7 6.9 %collective-permute-start.8 = (f16[400,128]{1,0:T(8,128)(2,1)S(1)}, f16[400,128]{1,0:T(8,128)(2,1)S(1)}, u32[]{:S(2)}, u32[]{:S(2)}) collective-permute-start(f16[400,128]{1,0:T(8,128)(2,1)S(1)} %convert_element_type.12), channel_id=1, source_target_pairs={{0,8},{1,9},{2,10},{3,11},{4,12},{5,13},{6,14},{7,15},{8,0},{9,1},... | collective-permute-start | bytes 307208 | tf_op jit(solution)/shard_map/ppermute | solution.py:241

commit v2 on v1

--- a/solution.py
+++ b/solution.py
@@ -257,9 +257,7 @@
             pltpu.SemaphoreType.DMA((region_count, COPIES)),
         ],
         cost_estimate=light,
-        compiler_params=pltpu.CompilerParams(
-            vmem_limit_bytes=VMEM_BYTES, fuse_transposed_lhs_in_matmul=True
-        ),
+        compiler_params=params,
         name="gram_rows",
     )(
         pltpu.with_memory_space_constraint(region_groups, pltpu.HBM),
@@ -280,7 +278,7 @@
             name="merge_units",
         )(*gots, after)
         later = merged[-1]
-        for pair in range(pair_count - 1, 0, -1):
+        for pair in sorted(range(1, pair_count), key=lambda p: (p.bit_count(), -p)):
             gots.append(permute(merged[pair - 1], CORES * pair))
         tagged = tagged or gots
         count = sum_rows(chunk, width, slot_count)

time: 30.5 us -> 29.5 us (0.967)
  Pallas kernels: 5.09 us -> 4.68 us
    pallas_call x1, Pallas kernels: 2.63 us -> 2.22 us  [shards(): pl.pallas_call(functools.partial(gram_kernel, total_groups, half), in_spe...]
    ppermute x10, starting transfers between devices: 13.9 us -> 13.6 us  [permute(): return lax.ppermute(values, 'group', pairs)]
  transfers between devices with their start and end apart: 10 -> 10, of which waited for: 5 -> 8; matrix products, arithmetic and copies ran while one was open for 0% -> 0% of each run, Pallas kernels for 6% -> 6%
where the time goes in v2:
time: 29.5 us; the launch traced here: 29.4 us
  starting transfers between devices  13.6 us (46%)
  waiting for transfers between devices  10.9 us (37%)
  Pallas kernels  4.68 us (16%)
    ppermute x10, starting transfers between devices, permute(): return lax.ppermute(values, 'group', pairs)  13.6 us
    ppermute x10, waiting for transfers between devices, permute(): return lax.ppermute(values, 'group', pairs)  10.9 us
    pallas_call x1, Pallas kernels, shards(): pl.pallas_call(functools.partial(gram_kernel, total_groups, half), in_spe...  2.22 us
    pallas_call x2, Pallas kernels, shards(): pl.pallas_call(functools.partial(join_kernel, chunk, slot_count), in_spec...  1.65 us
    pallas_call x2, Pallas kernels, shards(): pl.pallas_call(functools.partial(sum_kernel, chunk, slot_count), out_shap...  0.75 us
  transfers between devices with their start and end apart: 10, of which 8 were waited for; matrix products, arithmetic and copies ran while one was open for 0% of the time, Pallas kernels for 6%

profile of v2, /device:TPU:0, one launch (start us, length us, event | category | flops | bytes accessed | tf_op | source)
XLA Modules:
  0.0 29.4 jit_solution(14145006037922171748)
XLA Ops:
  0.0 2.2 %gram_rows.1 = (bf16[4,272,128]{2,1,0:T(8,128)(2,1)S(1)}, bf16[4,272,128]{2,1,0:T(8,128)(2,1)S(1)}, bf16[4,192,128]{2,1,0:T(8,128)(2,1)S(1)}, bf16[4,192,128]{2,1,0:T(8,128)(2,1)S(1)}) custom-call(s32[2,4]{1,0:T(2,128)} %groups_hbm.1, bf16[2,512,512]{2,1,0:T(8,128)(2,1)} %cols_hbm.1), custom_call_target="tpu_custom_call" | custom-call | tf_op jit(solution)/shard_map/gram_rows/pallas_call | solution.py:247
  2.2 0.5 %collective-permute-start = (bf16[4,272,128]{2,1,0:T(8,128)(2,1)S(1)}, bf16[4,272,128]{2,1,0:T(8,128)(2,1)S(1)}, u32[]{:S(2)}, u32[]{:S(2)}) collective-permute-start(bf16[4,272,128]{2,1,0:T(8,128)(2,1)S(1)} %get-tuple-element.21), channel_id=1, source_target_pairs={{0,1},{1,0},{2,3},{3,2},{4,5},{5,4},{6,7},{7,6},{8,9},{9,8},{10,11... | collective-permute-start | bytes 835592 | tf_op jit(solution)/shard_map/ppermute | solution.py:241
  2.8 1.2 %collective-permute-done.got_ref.refs_1_ = bf16[4,272,128]{2,1,0:T(8,128)(2,1)S(1)} collective-permute-done((bf16[4,272,128]{2,1,0:T(8,128)(2,1)S(1)}, bf16[4,272,128]{2,1,0:T(8,128)(2,1)S(1)}, u32[]{:S(2)}, u32[]{:S(2)}) %collective-permute-start) | collective-permute-done | bytes 278560 | tf_op jit(solution)/shard_map/ppermute | solution.py:241
  4.0 0.4 %collective-permute-start.4 = (bf16[4,192,128]{2,1,0:T(8,128)(2,1)S(1)}, bf16[4,192,128]{2,1,0:T(8,128)(2,1)S(1)}, u32[]{:S(2)}, u32[]{:S(2)}) collective-permute-start(bf16[4,192,128]{2,1,0:T(8,128)(2,1)S(1)} %get-tuple-element.27), channel_id=1, source_target_pairs={{0,1},{1,0},{2,3},{3,2},{4,5},{5,4},{6,7},{7,6},{8,9},{9,8},{10,11... | collective-permute-start | bytes 589832 | tf_op jit(solution)/shard_map/ppermute | solution.py:241
  4.4 2.7 %collective-permute-start.1 = (bf16[2,272,128]{2,1,0:T(8,128)(2,1)S(1)}, bf16[2,272,128]{2,1,0:T(8,128)(2,1)S(1)}, u32[]{:S(2)}, u32[]{:S(2)}) collective-permute-start(bf16[2,272,128]{2,1,0:T(8,128)(2,1)S(1)} %get-tuple-element.23), channel_id=1, source_target_pairs={{0,4},{1,5},{2,6},{3,7},{4,0},{5,1},{6,2},{7,3},{8,12},{9,13},{10,... | collective-permute-start | bytes 417800 | tf_op jit(solution)/shard_map/ppermute | solution.py:241
  7.1 1.5 %collective-permute-start.2 = (bf16[2,272,128]{2,1,0:T(8,128)(2,1)S(1)}, bf16[2,272,128]{2,1,0:T(8,128)(2,1)S(1)}, u32[]{:S(2)}, u32[]{:S(2)}) collective-permute-start(bf16[2,272,128]{2,1,0:T(8,128)(2,1)S(1)} %get-tuple-element.24), channel_id=1, source_target_pairs={{0,2},{1,3},{2,0},{3,1},{4,6},{5,7},{6,4},{7,5},{8,10},{9,11},{10,... | collective-permute-start | bytes 417800 | tf_op jit(solution)/shard_map/ppermute | solution.py:241
  8.7 0.0 collective-permute-start.3
  8.7 3.0 %collective-permute-done.1.refs_0_.refs_2_ = bf16[2,272,128]{2,1,0:T(8,128)(2,1)S(1)} collective-permute-done((bf16[2,272,128]{2,1,0:T(8,128)(2,1)S(1)}, bf16[2,272,128]{2,1,0:T(8,128)(2,1)S(1)}, u32[]{:S(2)}, u32[]{:S(2)}) %collective-permute-start.1) | collective-permute-done | bytes 139296 | tf_op jit(solution)/shard_map/ppermute | solution.py:241
  11.6 0.0 collective-permute-done.4.got_ref.refs_6_
  11.7 2.0 %collective-permute-start.5 = (bf16[2,192,128]{2,1,0:T(8,128)(2,1)S(1)}, bf16[2,192,128]{2,1,0:T(8,128)(2,1)S(1)}, u32[]{:S(2)}, u32[]{:S(2)}) collective-permute-start(bf16[2,192,128]{2,1,0:T(8,128)(2,1)S(1)} %get-tuple-element.28), channel_id=1, source_target_pairs={{0,4},{1,5},{2,6},{3,7},{4,0},{5,1},{6,2},{7,3},{8,12},{9,13},{10,... | collective-permute-start | bytes 294920 | tf_op jit(solution)/shard_map/ppermute | solution.py:241
  13.7 1.5 %collective-permute-start.6 = (bf16[2,192,128]{2,1,0:T(8,128)(2,1)S(1)}, bf16[2,192,128]{2,1,0:T(8,128)(2,1)S(1)}, u32[]{:S(2)}, u32[]{:S(2)}) collective-permute-start(bf16[2,192,128]{2,1,0:T(8,128)(2,1)S(1)} %get-tuple-element.29), channel_id=1, source_target_pairs={{0,2},{1,3},{2,0},{3,1},{4,6},{5,7},{6,4},{7,5},{8,10},{9,11},{10,... | collective-permute-start | bytes 294920 | tf_op jit(solution)/shard_map/ppermute | solution.py:241
  15.3 0.0 collective-permute-start.7
  15.3 0.3 %collective-permute-done.2.refs_3_ = bf16[2,272,128]{2,1,0:T(8,128)(2,1)S(1)} collective-permute-done((bf16[2,272,128]{2,1,0:T(8,128)(2,1)S(1)}, bf16[2,272,128]{2,1,0:T(8,128)(2,1)S(1)}, u32[]{:S(2)}, u32[]{:S(2)}) %collective-permute-start.2) | collective-permute-done | bytes 139296 | tf_op jit(solution)/shard_map/ppermute | solution.py:241
  15.6 0.6 %collective-permute-done.3.refs_4_ = bf16[2,272,128]{2,1,0:T(8,128)(2,1)S(1)} collective-permute-done((bf16[2,272,128]{2,1,0:T(8,128)(2,1)S(1)}, bf16[2,272,128]{2,1,0:T(8,128)(2,1)S(1)}, u32[]{:S(2)}, u32[]{:S(2)}) %collective-permute-start.3) | collective-permute-done | bytes 139296 | tf_op jit(solution)/shard_map/ppermute | solution.py:241
  16.2 0.4 %sum_offsets.3 = (f32[928,128]{1,0:T(8,128)S(1)}, f32[480,128]{1,0:T(8,128)S(1)}) custom-call(bf16[4,272,128]{2,1,0:T(8,128)(2,1)S(1)} %get-tuple-element.20.keep_ref.refs_0_, bf16[4,272,128]{2,1,0:T(8,128)(2,1)S(1)} %collective-permute-done.got_ref.refs_1_, bf16[2,272,128]{2,1,0:T(8,128)(2,1)S(1)} %collective-permute-done.1.refs_0_.refs_2_, ...), custom_call_target="tpu_custom_call" | custom-call | tf_op jit(solution)/shard_map/sum_offsets/pallas_call | solution.py:285
  16.6 2.6 %collective-permute-start.9 = (f16[480,128]{1,0:T(8,128)(2,1)S(1)}, f16[480,128]{1,0:T(8,128)(2,1)S(1)}, u32[]{:S(2)}, u32[]{:S(2)}) collective-permute-start(f16[480,128]{1,0:T(8,128)(2,1)S(1)} %convert_element_type.14), channel_id=1, source_target_pairs={{0,8},{1,9},{2,10},{3,11},{4,12},{5,13},{6,14},{7,15},{8,0},{9,1},... | collective-permute-start | bytes 368648 | tf_op jit(solution)/shard_map/ppermute | solution.py:241
  19.3 0.0 collective-permute-done.5.refs_7_
  19.3 0.1 collective-permute-done.6.refs_8_
  19.3 2.3 %collective-permute-done.7.refs_9_ = bf16[2,192,128]{2,1,0:T(8,128)(2,1)S(1)} collective-permute-done((bf16[2,192,128]{2,1,0:T(8,128)(2,1)S(1)}, bf16[2,192,128]{2,1,0:T(8,128)(2,1)S(1)}, u32[]{:S(2)}, u32[]{:S(2)}) %collective-permute-start.7) | collective-permute-done | bytes 98336 | tf_op jit(solution)/shard_map/ppermute | solution.py:241
  21.6 0.4 %sum_offsets.2 = (f32[768,128]{1,0:T(8,128)S(1)}, f32[400,128]{1,0:T(8,128)S(1)}) custom-call(bf16[4,272,128]{2,1,0:T(8,128)(2,1)S(1)} %get-tuple-element.20.keep_ref.refs_0_, bf16[4,272,128]{2,1,0:T(8,128)(2,1)S(1)} %collective-permute-done.got_ref.refs_1_, bf16[2,272,128]{2,1,0:T(8,128)(2,1)S(1)} %collective-permute-done.1.refs_0_.refs_2_, ...), custom_call_target="tpu_custom_call" | custom-call | tf_op jit(solution)/shard_map/sum_offsets/pallas_call | solution.py:285
  22.0 2.1 %collective-permute-start.8 = (f16[400,128]{1,0:T(8,128)(2,1)S(1)}, f16[400,128]{1,0:T(8,128)(2,1)S(1)}, u32[]{:S(2)}, u32[]{:S(2)}) collective-permute-start(f16[400,128]{1,0:T(8,128)(2,1)S(1)} %convert_element_type.12), channel_id=1, source_target_pairs={{0,8},{1,9},{2,10},{3,11},{4,12},{5,13},{6,14},{7,15},{8,0},{9,1},... | collective-permute-start | bytes 307208 | tf_op jit(solution)/shard_map/ppermute | solution.py:241
  24.1 1.6 %collective-permute-done.9 = f16[480,128]{1,0:T(8,128)(2,1)S(1)} collective-permute-done((f16[480,128]{1,0:T(8,128)(2,1)S(1)}, f16[480,128]{1,0:T(8,128)(2,1)S(1)}, u32[]{:S(2)}, u32[]{:S(2)}) %collective-permute-start.9) | collective-permute-done | bytes 122912 | tf_op jit(solution)/shard_map/ppermute | solution.py:241
  25.7 0.9 %join_offsets.2.refs_0_ = f32[7,128,128]{2,1,0:T(8,128)} custom-call(f32[928,128]{1,0:T(8,128)S(1)} %get-tuple-element.33.sums_ref, f32[480,128]{1,0:T(8,128)S(1)} %convert_element_type.15.far_ref), custom_call_target="tpu_custom_call" | custom-call | tf_op jit(solution)/shard_map/join_offsets/pallas_call | solution.py:302
  26.6 2.0 %collective-permute-done.8 = f16[400,128]{1,0:T(8,128)(2,1)S(1)} collective-permute-done((f16[400,128]{1,0:T(8,128)(2,1)S(1)}, f16[400,128]{1,0:T(8,128)(2,1)S(1)}, u32[]{:S(2)}, u32[]{:S(2)}) %collective-permute-start.8) | collective-permute-done | bytes 102432 | tf_op jit(solution)/shard_map/ppermute | solution.py:241
  28.6 0.7 %join_offsets.3 = f32[7,128,128]{2,1,0:T(8,128)} custom-call(f32[768,128]{1,0:T(8,128)S(1)} %get-tuple-element.31.sums_ref, f32[400,128]{1,0:T(8,128)S(1)} %convert_element_type.13.far_ref, f32[7,128,128]{2,1,0:T(8,128)} %join_offsets.2.refs_0_), custom_call_target="tpu_custom_call", output_to_operand_aliasing={{}: (2, {})} | custom-call | tf_op jit(solution)/shard_map/join_offsets/pallas_call | solution.py:302
  (6 shorter events, 0.1 us)
Async XLA Ops:
  2.2 1.7 %collective-permute-start = (bf16[4,272,128]{2,1,0:T(8,128)(2,1)S(1)}, bf16[4,272,128]{2,1,0:T(8,128)(2,1)S(1)}, u32[]{:S(2)}, u32[]{:S(2)}) collective-permute-start(bf16[4,272,128]{2,1,0:T(8,128)(2,1)S(1)} %get-tuple-element.21), channel_id=1, source_target_pairs={{0,1},{1,0},{2,3},{3,2},{4,5},{5,4},{6,7},{7,6},{8,9},{9,8},{10,11... | collective-permute-start | bytes 835592 | tf_op jit(solution)/shard_map/ppermute | solution.py:241
  4.0 7.7 %collective-permute-start.4 = (bf16[4,192,128]{2,1,0:T(8,128)(2,1)S(1)}, bf16[4,192,128]{2,1,0:T(8,128)(2,1)S(1)}, u32[]{:S(2)}, u32[]{:S(2)}) collective-permute-start(bf16[4,192,128]{2,1,0:T(8,128)(2,1)S(1)} %get-tuple-element.27), channel_id=1, source_target_pairs={{0,1},{1,0},{2,3},{3,2},{4,5},{5,4},{6,7},{7,6},{8,9},{9,8},{10,11... | collective-permute-start | bytes 589832 | tf_op jit(solution)/shard_map/ppermute | solution.py:241
  4.4 7.2 %collective-permute-start.1 = (bf16[2,272,128]{2,1,0:T(8,128)(2,1)S(1)}, bf16[2,272,128]{2,1,0:T(8,128)(2,1)S(1)}, u32[]{:S(2)}, u32[]{:S(2)}) collective-permute-start(bf16[2,272,128]{2,1,0:T(8,128)(2,1)S(1)} %get-tuple-element.23), channel_id=1, source_target_pairs={{0,4},{1,5},{2,6},{3,7},{4,0},{5,1},{6,2},{7,3},{8,12},{9,13},{10,... | collective-permute-start | bytes 417800 | tf_op jit(solution)/shard_map/ppermute | solution.py:241
  7.1 8.4 %collective-permute-start.2 = (bf16[2,272,128]{2,1,0:T(8,128)(2,1)S(1)}, bf16[2,272,128]{2,1,0:T(8,128)(2,1)S(1)}, u32[]{:S(2)}, u32[]{:S(2)}) collective-permute-start(bf16[2,272,128]{2,1,0:T(8,128)(2,1)S(1)} %get-tuple-element.24), channel_id=1, source_target_pairs={{0,2},{1,3},{2,0},{3,1},{4,6},{5,7},{6,4},{7,5},{8,10},{9,11},{10,... | collective-permute-start | bytes 417800 | tf_op jit(solution)/shard_map/ppermute | solution.py:241
  8.7 7.5 %collective-permute-start.3 = (bf16[2,272,128]{2,1,0:T(8,128)(2,1)S(1)}, bf16[2,272,128]{2,1,0:T(8,128)(2,1)S(1)}, u32[]{:S(2)}, u32[]{:S(2)}) collective-permute-start(bf16[2,272,128]{2,1,0:T(8,128)(2,1)S(1)} %get-tuple-element.25), channel_id=1, source_target_pairs={{0,6},{1,7},{2,4},{3,5},{4,2},{5,3},{6,0},{7,1},{8,14},{9,15},{10,... | collective-permute-start | bytes 417800 | tf_op jit(solution)/shard_map/ppermute | solution.py:241
  11.7 7.6 %collective-permute-start.5 = (bf16[2,192,128]{2,1,0:T(8,128)(2,1)S(1)}, bf16[2,192,128]{2,1,0:T(8,128)(2,1)S(1)}, u32[]{:S(2)}, u32[]{:S(2)}) collective-permute-start(bf16[2,192,128]{2,1,0:T(8,128)(2,1)S(1)} %get-tuple-element.28), channel_id=1, source_target_pairs={{0,4},{1,5},{2,6},{3,7},{4,0},{5,1},{6,2},{7,3},{8,12},{9,13},{10,... | collective-permute-start | bytes 294920 | tf_op jit(solution)/shard_map/ppermute | solution.py:241
  13.7 5.6 %collective-permute-start.6 = (bf16[2,192,128]{2,1,0:T(8,128)(2,1)S(1)}, bf16[2,192,128]{2,1,0:T(8,128)(2,1)S(1)}, u32[]{:S(2)}, u32[]{:S(2)}) collective-permute-start(bf16[2,192,128]{2,1,0:T(8,128)(2,1)S(1)} %get-tuple-element.29), channel_id=1, source_target_pairs={{0,2},{1,3},{2,0},{3,1},{4,6},{5,7},{6,4},{7,5},{8,10},{9,11},{10,... | collective-permute-start | bytes 294920 | tf_op jit(solution)/shard_map/ppermute | solution.py:241
  15.3 6.3 %collective-permute-start.7 = (bf16[2,192,128]{2,1,0:T(8,128)(2,1)S(1)}, bf16[2,192,128]{2,1,0:T(8,128)(2,1)S(1)}, u32[]{:S(2)}, u32[]{:S(2)}) collective-permute-start(bf16[2,192,128]{2,1,0:T(8,128)(2,1)S(1)} %get-tuple-element.30), channel_id=1, source_target_pairs={{0,6},{1,7},{2,4},{3,5},{4,2},{5,3},{6,0},{7,1},{8,14},{9,15},{10,... | collective-permute-start | bytes 294920 | tf_op jit(solution)/shard_map/ppermute | solution.py:241
  16.6 9.1 %collective-permute-start.9 = (f16[480,128]{1,0:T(8,128)(2,1)S(1)}, f16[480,128]{1,0:T(8,128)(2,1)S(1)}, u32[]{:S(2)}, u32[]{:S(2)}) collective-permute-start(f16[480,128]{1,0:T(8,128)(2,1)S(1)} %convert_element_type.14), channel_id=1, source_target_pairs={{0,8},{1,9},{2,10},{3,11},{4,12},{5,13},{6,14},{7,15},{8,0},{9,1},... | collective-permute-start | bytes 368648 | tf_op jit(solution)/shard_map/ppermute | solution.py:241
  22.0 6.6 %collective-permute-start.8 = (f16[400,128]{1,0:T(8,128)(2,1)S(1)}, f16[400,128]{1,0:T(8,128)(2,1)S(1)}, u32[]{:S(2)}, u32[]{:S(2)}) collective-permute-start(f16[400,128]{1,0:T(8,128)(2,1)S(1)} %convert_element_type.12), channel_id=1, source_target_pairs={{0,8},{1,9},{2,10},{3,11},{4,12},{5,13},{6,14},{7,15},{8,0},{9,1},... | collective-permute-start | bytes 307208 | tf_op jit(solution)/shard_map/ppermute | solution.py:241

commit v3 on v2

--- a/solution.py
+++ b/solution.py
@@ -14,6 +14,7 @@
 CORES = 2
 COPIES = 2
 TILE = 16
+PRODUCTS = 2
 
 
 def packed_rows(width):
@@ -97,9 +98,16 @@
         for part in range(COPIES):
             cols_copy(region, part).wait()
         cols = cols_ref[region]
-        gram = lax.dot_general(
-            cols, cols, (((0,), (0,)), ((), ())), preferred_element_type=jnp.float32
-        )
+        depth = cols.shape[1] // PRODUCTS
+        grams = [
+            lax.dot_general(
+                cols[:, at * depth : (at + 1) * depth],
+                cols,
+                (((0,), (0,)), ((), ())),
+                preferred_element_type=jnp.float32,
+            )
+            for at in range(PRODUCTS)
+        ]
         groups = [groups_ref[region, s] for s in range(slot_count)]
 
         def ahead(s, t):
@@ -114,7 +122,8 @@
             tag = (place + slot_count * away).astype(jnp.float32)
             slot = lax.rem(groups[s], half) ^ my_slot
             for t in range(slot_count):
-                block = gram[s * width : (s + 1) * width, t * width : (t + 1) * width]
+                at = s * width % depth
+                block = grams[s * width // depth][at : at + width, t * width : (t + 1) * width]
                 if t == s:
                     block, rest = pack(block, tag)
                     rows_ref[slot, : width // 2] = block.astype(rows_ref.dtype)
@@ -178,13 +187,10 @@
 
 
 def merge_kernel(keep_ref, got_ref, *refs):
-    after_ref, send_refs = refs[0], refs[1:]
     pair_count = keep_ref.shape[0]
-    for at in range(1, pair_count):
-        send_refs[at - 1][0] = keep_ref[at]
-        send_refs[at - 1][1] = got_ref[at]
-    if len(send_refs) == pair_count:
-        send_refs[-1][...] = after_ref[...]
+    for at, send_ref in enumerate(refs[1 - pair_count :], 1):
+        send_ref[0] = keep_ref[at]
+        send_ref[1] = got_ref[at]
 
 
 def join_kernel(chunk, slot_count, sums_ref, far_ref, *refs):
@@ -267,17 +273,14 @@
     pieces, tagged = [], []
     for chunk in range(CHUNKS):
         keep, give = sends[CORES * chunk : CORES * (chunk + 1)]
-        gots = [keep, permute(give if chunk == 0 else later, 1)]
-        after = sends[CORES + 1] if chunk == 0 else tagged[CORES]
+        gots = [keep, permute(give, 1)]
         merged = pl.pallas_call(
             merge_kernel,
-            out_shape=[blocks(CORES, chunk)] * (pair_count - 1)
-            + ([blocks(pair_count, 1)] if chunk == 0 else []),
+            out_shape=[blocks(CORES, chunk)] * (pair_count - 1),
             cost_estimate=light,
             compiler_params=params,
             name="merge_units",
-        )(*gots, after)
-        later = merged[-1]
+        )(*gots, *tagged[CORES : CORES + chunk])
         for pair in sorted(range(1, pair_count), key=lambda p: (p.bit_count(), -p)):
             gots.append(permute(merged[pair - 1], CORES * pair))
         tagged = tagged or gots

time: 29.5 us -> 28.9 us (0.980)
  waiting for transfers between devices: 10.9 us -> 10.2 us
    ppermute x10, waiting for transfers between devices: 10.9 us -> 10.2 us  [permute(): return lax.ppermute(values, 'group', pairs)]
  transfers between devices with their start and end apart: 10 -> 10, of which waited for: 8 -> 7; matrix products, arithmetic and copies ran while one was open for 0% -> 0% of each run, Pallas kernels for 6% -> 6%
where the time goes in v3:
time: 28.9 us; the launch traced here: 28.8 us
  starting transfers between devices  13.7 us (47%)
  waiting for transfers between devices  10.2 us (35%)
  Pallas kernels  4.67 us (16%)
    ppermute x10, starting transfers between devices, permute(): return lax.ppermute(values, 'group', pairs)  13.7 us
    ppermute x10, waiting for transfers between devices, permute(): return lax.ppermute(values, 'group', pairs)  10.2 us
    pallas_call x1, Pallas kernels, shards(): pl.pallas_call(functools.partial(gram_kernel, total_groups, half), in_spe...  2.23 us
    pallas_call x2, Pallas kernels, shards(): pl.pallas_call(functools.partial(join_kernel, chunk, slot_count), in_spec...  1.65 us
    pallas_call x2, Pallas kernels, shards(): pl.pallas_call(functools.partial(sum_kernel, chunk, slot_count), out_shap...  0.75 us
  transfers between devices with their start and end apart: 10, of which 7 were waited for; matrix products, arithmetic and copies ran while one was open for 0% of the time, Pallas kernels for 6%

profile of v3, /device:TPU:0, one launch (start us, length us, event | category | flops | bytes accessed | tf_op | source)
XLA Modules:
  0.0 28.8 jit_solution(18093013667437389578)
XLA Ops:
  0.0 2.2 %gram_rows.1 = (bf16[4,272,128]{2,1,0:T(8,128)(2,1)S(1)}, bf16[4,272,128]{2,1,0:T(8,128)(2,1)S(1)}, bf16[4,192,128]{2,1,0:T(8,128)(2,1)S(1)}, bf16[4,192,128]{2,1,0:T(8,128)(2,1)S(1)}) custom-call(s32[2,4]{1,0:T(2,128)} %groups_hbm.1, bf16[2,512,512]{2,1,0:T(8,128)(2,1)} %cols_hbm.1), custom_call_target="tpu_custom_call" | custom-call | tf_op jit(solution)/shard_map/gram_rows/pallas_call | solution.py:253
  2.2 0.5 %collective-permute-start = (bf16[4,272,128]{2,1,0:T(8,128)(2,1)S(1)}, bf16[4,272,128]{2,1,0:T(8,128)(2,1)S(1)}, u32[]{:S(2)}, u32[]{:S(2)}) collective-permute-start(bf16[4,272,128]{2,1,0:T(8,128)(2,1)S(1)} %get-tuple-element.20), channel_id=1, source_target_pairs={{0,1},{1,0},{2,3},{3,2},{4,5},{5,4},{6,7},{7,6},{8,9},{9,8},{10,11... | collective-permute-start | bytes 835592 | tf_op jit(solution)/shard_map/ppermute | solution.py:247
  2.8 0.1 collective-permute-start.4
  2.8 1.1 %collective-permute-done.got_ref.refs_1_ = bf16[4,272,128]{2,1,0:T(8,128)(2,1)S(1)} collective-permute-done((bf16[4,272,128]{2,1,0:T(8,128)(2,1)S(1)}, bf16[4,272,128]{2,1,0:T(8,128)(2,1)S(1)}, u32[]{:S(2)}, u32[]{:S(2)}) %collective-permute-start) | collective-permute-done | bytes 278560 | tf_op jit(solution)/shard_map/ppermute | solution.py:247
  4.0 3.0 %collective-permute-start.1 = (bf16[2,272,128]{2,1,0:T(8,128)(2,1)S(1)}, bf16[2,272,128]{2,1,0:T(8,128)(2,1)S(1)}, u32[]{:S(2)}, u32[]{:S(2)}) collective-permute-start(bf16[2,272,128]{2,1,0:T(8,128)(2,1)S(1)} %get-tuple-element.21), channel_id=1, source_target_pairs={{0,4},{1,5},{2,6},{3,7},{4,0},{5,1},{6,2},{7,3},{8,12},{9,13},{10,... | collective-permute-start | bytes 417800 | tf_op jit(solution)/shard_map/ppermute | solution.py:247
  7.0 1.5 %collective-permute-start.2 = (bf16[2,272,128]{2,1,0:T(8,128)(2,1)S(1)}, bf16[2,272,128]{2,1,0:T(8,128)(2,1)S(1)}, u32[]{:S(2)}, u32[]{:S(2)}) collective-permute-start(bf16[2,272,128]{2,1,0:T(8,128)(2,1)S(1)} %get-tuple-element.22), channel_id=1, source_target_pairs={{0,2},{1,3},{2,0},{3,1},{4,6},{5,7},{6,4},{7,5},{8,10},{9,11},{10,... | collective-permute-start | bytes 417800 | tf_op jit(solution)/shard_map/ppermute | solution.py:247
  8.5 0.0 collective-permute-start.3
  8.5 0.0 collective-permute-done.4.got_ref.refs_6_
  8.5 2.7 %collective-permute-done.1.refs_0_.refs_2_ = bf16[2,272,128]{2,1,0:T(8,128)(2,1)S(1)} collective-permute-done((bf16[2,272,128]{2,1,0:T(8,128)(2,1)S(1)}, bf16[2,272,128]{2,1,0:T(8,128)(2,1)S(1)}, u32[]{:S(2)}, u32[]{:S(2)}) %collective-permute-start.1) | collective-permute-done | bytes 139296 | tf_op jit(solution)/shard_map/ppermute | solution.py:247
  11.3 2.3 %collective-permute-start.5 = (bf16[2,192,128]{2,1,0:T(8,128)(2,1)S(1)}, bf16[2,192,128]{2,1,0:T(8,128)(2,1)S(1)}, u32[]{:S(2)}, u32[]{:S(2)}) collective-permute-start(bf16[2,192,128]{2,1,0:T(8,128)(2,1)S(1)} %get-tuple-element.26), channel_id=1, source_target_pairs={{0,4},{1,5},{2,6},{3,7},{4,0},{5,1},{6,2},{7,3},{8,12},{9,13},{10,... | collective-permute-start | bytes 294920 | tf_op jit(solution)/shard_map/ppermute | solution.py:247
  13.6 1.5 %collective-permute-start.6 = (bf16[2,192,128]{2,1,0:T(8,128)(2,1)S(1)}, bf16[2,192,128]{2,1,0:T(8,128)(2,1)S(1)}, u32[]{:S(2)}, u32[]{:S(2)}) collective-permute-start(bf16[2,192,128]{2,1,0:T(8,128)(2,1)S(1)} %get-tuple-element.27), channel_id=1, source_target_pairs={{0,2},{1,3},{2,0},{3,1},{4,6},{5,7},{6,4},{7,5},{8,10},{9,11},{10,... | collective-permute-start | bytes 294920 | tf_op jit(solution)/shard_map/ppermute | solution.py:247
  15.1 0.0 collective-permute-start.7
  15.1 0.4 %collective-permute-done.2.refs_3_ = bf16[2,272,128]{2,1,0:T(8,128)(2,1)S(1)} collective-permute-done((bf16[2,272,128]{2,1,0:T(8,128)(2,1)S(1)}, bf16[2,272,128]{2,1,0:T(8,128)(2,1)S(1)}, u32[]{:S(2)}, u32[]{:S(2)}) %collective-permute-start.2) | collective-permute-done | bytes 139296 | tf_op jit(solution)/shard_map/ppermute | solution.py:247
  15.5 0.5 %collective-permute-done.3.refs_4_ = bf16[2,272,128]{2,1,0:T(8,128)(2,1)S(1)} collective-permute-done((bf16[2,272,128]{2,1,0:T(8,128)(2,1)S(1)}, bf16[2,272,128]{2,1,0:T(8,128)(2,1)S(1)}, u32[]{:S(2)}, u32[]{:S(2)}) %collective-permute-start.3) | collective-permute-done | bytes 139296 | tf_op jit(solution)/shard_map/ppermute | solution.py:247
  16.0 0.4 %sum_offsets.3 = (f32[928,128]{1,0:T(8,128)S(1)}, f32[480,128]{1,0:T(8,128)S(1)}) custom-call(bf16[4,272,128]{2,1,0:T(8,128)(2,1)S(1)} %get-tuple-element.19.keep_ref.refs_0_, bf16[4,272,128]{2,1,0:T(8,128)(2,1)S(1)} %collective-permute-done.got_ref.refs_1_, bf16[2,272,128]{2,1,0:T(8,128)(2,1)S(1)} %collective-permute-done.1.refs_0_.refs_2_, ...), custom_call_target="tpu_custom_call" | custom-call | tf_op jit(solution)/shard_map/sum_offsets/pallas_call | solution.py:288
  16.5 2.7 %collective-permute-start.9 = (f16[480,128]{1,0:T(8,128)(2,1)S(1)}, f16[480,128]{1,0:T(8,128)(2,1)S(1)}, u32[]{:S(2)}, u32[]{:S(2)}) collective-permute-start(f16[480,128]{1,0:T(8,128)(2,1)S(1)} %convert_element_type.14), channel_id=1, source_target_pairs={{0,8},{1,9},{2,10},{3,11},{4,12},{5,13},{6,14},{7,15},{8,0},{9,1},... | collective-permute-start | bytes 368648 | tf_op jit(solution)/shard_map/ppermute | solution.py:247
  19.1 0.0 collective-permute-done.5.refs_7_
  19.1 0.0 collective-permute-done.6.refs_8_
  19.1 2.2 %collective-permute-done.7.refs_9_ = bf16[2,192,128]{2,1,0:T(8,128)(2,1)S(1)} collective-permute-done((bf16[2,192,128]{2,1,0:T(8,128)(2,1)S(1)}, bf16[2,192,128]{2,1,0:T(8,128)(2,1)S(1)}, u32[]{:S(2)}, u32[]{:S(2)}) %collective-permute-start.7) | collective-permute-done | bytes 98336 | tf_op jit(solution)/shard_map/ppermute | solution.py:247
  21.3 0.4 %sum_offsets.2 = (f32[768,128]{1,0:T(8,128)S(1)}, f32[400,128]{1,0:T(8,128)S(1)}) custom-call(bf16[4,272,128]{2,1,0:T(8,128)(2,1)S(1)} %get-tuple-element.19.keep_ref.refs_0_, bf16[4,272,128]{2,1,0:T(8,128)(2,1)S(1)} %collective-permute-done.got_ref.refs_1_, bf16[2,272,128]{2,1,0:T(8,128)(2,1)S(1)} %collective-permute-done.1.refs_0_.refs_2_, ...), custom_call_target="tpu_custom_call" | custom-call | tf_op jit(solution)/shard_map/sum_offsets/pallas_call | solution.py:288
  21.7 2.1 %collective-permute-start.8 = (f16[400,128]{1,0:T(8,128)(2,1)S(1)}, f16[400,128]{1,0:T(8,128)(2,1)S(1)}, u32[]{:S(2)}, u32[]{:S(2)}) collective-permute-start(f16[400,128]{1,0:T(8,128)(2,1)S(1)} %convert_element_type.12), channel_id=1, source_target_pairs={{0,8},{1,9},{2,10},{3,11},{4,12},{5,13},{6,14},{7,15},{8,0},{9,1},... | collective-permute-start | bytes 307208 | tf_op jit(solution)/shard_map/ppermute | solution.py:247
  23.8 1.3 %collective-permute-done.9 = f16[480,128]{1,0:T(8,128)(2,1)S(1)} collective-permute-done((f16[480,128]{1,0:T(8,128)(2,1)S(1)}, f16[480,128]{1,0:T(8,128)(2,1)S(1)}, u32[]{:S(2)}, u32[]{:S(2)}) %collective-permute-start.9) | collective-permute-done | bytes 122912 | tf_op jit(solution)/shard_map/ppermute | solution.py:247
  25.1 0.9 %join_offsets.2.refs_0_ = f32[7,128,128]{2,1,0:T(8,128)} custom-call(f32[928,128]{1,0:T(8,128)S(1)} %get-tuple-element.31.sums_ref, f32[480,128]{1,0:T(8,128)S(1)} %convert_element_type.15.far_ref), custom_call_target="tpu_custom_call" | custom-call | tf_op jit(solution)/shard_map/join_offsets/pallas_call | solution.py:305
  26.0 2.0 %collective-permute-done.8 = f16[400,128]{1,0:T(8,128)(2,1)S(1)} collective-permute-done((f16[400,128]{1,0:T(8,128)(2,1)S(1)}, f16[400,128]{1,0:T(8,128)(2,1)S(1)}, u32[]{:S(2)}, u32[]{:S(2)}) %collective-permute-start.8) | collective-permute-done | bytes 102432 | tf_op jit(solution)/shard_map/ppermute | solution.py:247
  28.0 0.7 %join_offsets.3 = f32[7,128,128]{2,1,0:T(8,128)} custom-call(f32[768,128]{1,0:T(8,128)S(1)} %get-tuple-element.29.sums_ref, f32[400,128]{1,0:T(8,128)S(1)} %convert_element_type.13.far_ref, f32[7,128,128]{2,1,0:T(8,128)} %join_offsets.2.refs_0_), custom_call_target="tpu_custom_call", output_to_operand_aliasing={{}: (2, {})} | custom-call | tf_op jit(solution)/shard_map/join_offsets/pallas_call | solution.py:305
  (6 shorter events, 0.1 us)
Async XLA Ops:
  2.2 1.7 %collective-permute-start = (bf16[4,272,128]{2,1,0:T(8,128)(2,1)S(1)}, bf16[4,272,128]{2,1,0:T(8,128)(2,1)S(1)}, u32[]{:S(2)}, u32[]{:S(2)}) collective-permute-start(bf16[4,272,128]{2,1,0:T(8,128)(2,1)S(1)} %get-tuple-element.20), channel_id=1, source_target_pairs={{0,1},{1,0},{2,3},{3,2},{4,5},{5,4},{6,7},{7,6},{8,9},{9,8},{10,11... | collective-permute-start | bytes 835592 | tf_op jit(solution)/shard_map/ppermute | solution.py:247
  2.8 5.8 %collective-permute-start.4 = (bf16[4,192,128]{2,1,0:T(8,128)(2,1)S(1)}, bf16[4,192,128]{2,1,0:T(8,128)(2,1)S(1)}, u32[]{:S(2)}, u32[]{:S(2)}) collective-permute-start(bf16[4,192,128]{2,1,0:T(8,128)(2,1)S(1)} %get-tuple-element.25), channel_id=1, source_target_pairs={{0,1},{1,0},{2,3},{3,2},{4,5},{5,4},{6,7},{7,6},{8,9},{9,8},{10,11... | collective-permute-start | bytes 589832 | tf_op jit(solution)/shard_map/ppermute | solution.py:247
  4.0 7.3 %collective-permute-start.1 = (bf16[2,272,128]{2,1,0:T(8,128)(2,1)S(1)}, bf16[2,272,128]{2,1,0:T(8,128)(2,1)S(1)}, u32[]{:S(2)}, u32[]{:S(2)}) collective-permute-start(bf16[2,272,128]{2,1,0:T(8,128)(2,1)S(1)} %get-tuple-element.21), channel_id=1, source_target_pairs={{0,4},{1,5},{2,6},{3,7},{4,0},{5,1},{6,2},{7,3},{8,12},{9,13},{10,... | collective-permute-start | bytes 417800 | tf_op jit(solution)/shard_map/ppermute | solution.py:247
  7.0 8.5 %collective-permute-start.2 = (bf16[2,272,128]{2,1,0:T(8,128)(2,1)S(1)}, bf16[2,272,128]{2,1,0:T(8,128)(2,1)S(1)}, u32[]{:S(2)}, u32[]{:S(2)}) collective-permute-start(bf16[2,272,128]{2,1,0:T(8,128)(2,1)S(1)} %get-tuple-element.22), channel_id=1, source_target_pairs={{0,2},{1,3},{2,0},{3,1},{4,6},{5,7},{6,4},{7,5},{8,10},{9,11},{10,... | collective-permute-start | bytes 417800 | tf_op jit(solution)/shard_map/ppermute | solution.py:247
  8.5 7.5 %collective-permute-start.3 = (bf16[2,272,128]{2,1,0:T(8,128)(2,1)S(1)}, bf16[2,272,128]{2,1,0:T(8,128)(2,1)S(1)}, u32[]{:S(2)}, u32[]{:S(2)}) collective-permute-start(bf16[2,272,128]{2,1,0:T(8,128)(2,1)S(1)} %get-tuple-element.23), channel_id=1, source_target_pairs={{0,6},{1,7},{2,4},{3,5},{4,2},{5,3},{6,0},{7,1},{8,14},{9,15},{10,... | collective-permute-start | bytes 417800 | tf_op jit(solution)/shard_map/ppermute | solution.py:247
  11.3 7.9 %collective-permute-start.5 = (bf16[2,192,128]{2,1,0:T(8,128)(2,1)S(1)}, bf16[2,192,128]{2,1,0:T(8,128)(2,1)S(1)}, u32[]{:S(2)}, u32[]{:S(2)}) collective-permute-start(bf16[2,192,128]{2,1,0:T(8,128)(2,1)S(1)} %get-tuple-element.26), channel_id=1, source_target_pairs={{0,4},{1,5},{2,6},{3,7},{4,0},{5,1},{6,2},{7,3},{8,12},{9,13},{10,... | collective-permute-start | bytes 294920 | tf_op jit(solution)/shard_map/ppermute | solution.py:247
  13.6 5.6 %collective-permute-start.6 = (bf16[2,192,128]{2,1,0:T(8,128)(2,1)S(1)}, bf16[2,192,128]{2,1,0:T(8,128)(2,1)S(1)}, u32[]{:S(2)}, u32[]{:S(2)}) collective-permute-start(bf16[2,192,128]{2,1,0:T(8,128)(2,1)S(1)} %get-tuple-element.27), channel_id=1, source_target_pairs={{0,2},{1,3},{2,0},{3,1},{4,6},{5,7},{6,4},{7,5},{8,10},{9,11},{10,... | collective-permute-start | bytes 294920 | tf_op jit(solution)/shard_map/ppermute | solution.py:247
  15.1 6.2 %collective-permute-start.7 = (bf16[2,192,128]{2,1,0:T(8,128)(2,1)S(1)}, bf16[2,192,128]{2,1,0:T(8,128)(2,1)S(1)}, u32[]{:S(2)}, u32[]{:S(2)}) collective-permute-start(bf16[2,192,128]{2,1,0:T(8,128)(2,1)S(1)} %get-tuple-element.28), channel_id=1, source_target_pairs={{0,6},{1,7},{2,4},{3,5},{4,2},{5,3},{6,0},{7,1},{8,14},{9,15},{10,... | collective-permute-start | bytes 294920 | tf_op jit(solution)/shard_map/ppermute | solution.py:247
  16.5 8.6 %collective-permute-start.9 = (f16[480,128]{1,0:T(8,128)(2,1)S(1)}, f16[480,128]{1,0:T(8,128)(2,1)S(1)}, u32[]{:S(2)}, u32[]{:S(2)}) collective-permute-start(f16[480,128]{1,0:T(8,128)(2,1)S(1)} %convert_element_type.14), channel_id=1, source_target_pairs={{0,8},{1,9},{2,10},{3,11},{4,12},{5,13},{6,14},{7,15},{8,0},{9,1},... | collective-permute-start | bytes 368648 | tf_op jit(solution)/shard_map/ppermute | solution.py:247
  21.7 6.3 %collective-permute-start.8 = (f16[400,128]{1,0:T(8,128)(2,1)S(1)}, f16[400,128]{1,0:T(8,128)(2,1)S(1)}, u32[]{:S(2)}, u32[]{:S(2)}) collective-permute-start(f16[400,128]{1,0:T(8,128)(2,1)S(1)} %convert_element_type.12), channel_id=1, source_target_pairs={{0,8},{1,9},{2,10},{3,11},{4,12},{5,13},{6,14},{7,15},{8,0},{9,1},... | collective-permute-start | bytes 307208 | tf_op jit(solution)/shard_map/ppermute | solution.py:247

commit v4 on v3

--- a/solution.py
+++ b/solution.py
@@ -229,6 +229,10 @@
         copy.wait()
 
 
+def order_of(chunk, pair):
+    return (0 if chunk == 0 else -(pair.bit_length()), pair.bit_count(), -pair)
+
+
 def shards(solve_cols, region_groups):
     region_count, row_count, col_count = solve_cols.shape
     slot_count = region_groups.shape[1]
@@ -281,8 +285,13 @@
             compiler_params=params,
             name="merge_units",
         )(*gots, *tagged[CORES : CORES + chunk])
-        for pair in sorted(range(1, pair_count), key=lambda p: (p.bit_count(), -p)):
-            gots.append(permute(merged[pair - 1], CORES * pair))
+        chips = {}
+        for pair in sorted(range(1, pair_count), key=functools.partial(order_of, chunk)):
+            chips[pair] = permute(merged[pair - 1], CORES * pair)
+        gots += [
+            chips[pair]
+            for pair in sorted(range(1, pair_count), key=functools.partial(order_of, 0))
+        ]
         tagged = tagged or gots
         count = sum_rows(chunk, width, slot_count)
         sums, scaled = pl.pallas_call(

time: 28.9 us -> 28.9 us (level)
  no operation moved by 1% of the time
where the time goes in v4:
time: 28.9 us; the launch traced here: 28.8 us
  starting transfers between devices  13.7 us (47%)
  waiting for transfers between devices  10.2 us (35%)
  Pallas kernels  4.68 us (16%)
    ppermute x10, starting transfers between devices, permute(): return lax.ppermute(values, 'group', pairs)  13.7 us
    ppermute x10, waiting for transfers between devices, permute(): return lax.ppermute(values, 'group', pairs)  10.2 us
    pallas_call x1, Pallas kernels, shards(): pl.pallas_call(functools.partial(gram_kernel, total_groups, half), in_spe...  2.23 us
    pallas_call x2, Pallas kernels, shards(): pl.pallas_call(functools.partial(join_kernel, chunk, slot_count), in_spec...  1.65 us
    pallas_call x2, Pallas kernels, shards(): pl.pallas_call(functools.partial(sum_kernel, chunk, slot_count), out_shap...  0.75 us
  transfers between devices with their start and end apart: 10, of which 7 were waited for; matrix products, arithmetic and copies ran while one was open for 0% of the time, Pallas kernels for 6%

profile of v4, /device:TPU:0, one launch (start us, length us, event | category | flops | bytes accessed | tf_op | source)
XLA Modules:
  0.0 28.8 jit_solution(18093013667437389578)
XLA Ops:
  0.0 2.2 %gram_rows.1 = (bf16[4,272,128]{2,1,0:T(8,128)(2,1)S(1)}, bf16[4,272,128]{2,1,0:T(8,128)(2,1)S(1)}, bf16[4,192,128]{2,1,0:T(8,128)(2,1)S(1)}, bf16[4,192,128]{2,1,0:T(8,128)(2,1)S(1)}) custom-call(s32[2,4]{1,0:T(2,128)} %groups_hbm.1, bf16[2,512,512]{2,1,0:T(8,128)(2,1)} %cols_hbm.1), custom_call_target="tpu_custom_call" | custom-call | tf_op jit(solution)/shard_map/gram_rows/pallas_call | solution.py:257
  2.2 0.5 %collective-permute-start = (bf16[4,272,128]{2,1,0:T(8,128)(2,1)S(1)}, bf16[4,272,128]{2,1,0:T(8,128)(2,1)S(1)}, u32[]{:S(2)}, u32[]{:S(2)}) collective-permute-start(bf16[4,272,128]{2,1,0:T(8,128)(2,1)S(1)} %get-tuple-element.20), channel_id=1, source_target_pairs={{0,1},{1,0},{2,3},{3,2},{4,5},{5,4},{6,7},{7,6},{8,9},{9,8},{10,11... | collective-permute-start | bytes 835592 | tf_op jit(solution)/shard_map/ppermute | solution.py:251
  2.8 0.1 collective-permute-start.4
  2.8 1.1 %collective-permute-done.got_ref.refs_1_ = bf16[4,272,128]{2,1,0:T(8,128)(2,1)S(1)} collective-permute-done((bf16[4,272,128]{2,1,0:T(8,128)(2,1)S(1)}, bf16[4,272,128]{2,1,0:T(8,128)(2,1)S(1)}, u32[]{:S(2)}, u32[]{:S(2)}) %collective-permute-start) | collective-permute-done | bytes 278560 | tf_op jit(solution)/shard_map/ppermute | solution.py:251
  4.0 3.0 %collective-permute-start.1 = (bf16[2,272,128]{2,1,0:T(8,128)(2,1)S(1)}, bf16[2,272,128]{2,1,0:T(8,128)(2,1)S(1)}, u32[]{:S(2)}, u32[]{:S(2)}) collective-permute-start(bf16[2,272,128]{2,1,0:T(8,128)(2,1)S(1)} %get-tuple-element.21), channel_id=1, source_target_pairs={{0,4},{1,5},{2,6},{3,7},{4,0},{5,1},{6,2},{7,3},{8,12},{9,13},{10,... | collective-permute-start | bytes 417800 | tf_op jit(solution)/shard_map/ppermute | solution.py:251
  7.0 1.5 %collective-permute-start.2 = (bf16[2,272,128]{2,1,0:T(8,128)(2,1)S(1)}, bf16[2,272,128]{2,1,0:T(8,128)(2,1)S(1)}, u32[]{:S(2)}, u32[]{:S(2)}) collective-permute-start(bf16[2,272,128]{2,1,0:T(8,128)(2,1)S(1)} %get-tuple-element.22), channel_id=1, source_target_pairs={{0,2},{1,3},{2,0},{3,1},{4,6},{5,7},{6,4},{7,5},{8,10},{9,11},{10,... | collective-permute-start | bytes 417800 | tf_op jit(solution)/shard_map/ppermute | solution.py:251
  8.5 0.0 collective-permute-start.3
  8.5 0.0 collective-permute-done.4.got_ref.refs_6_
  8.5 2.7 %collective-permute-done.1.refs_0_.refs_2_ = bf16[2,272,128]{2,1,0:T(8,128)(2,1)S(1)} collective-permute-done((bf16[2,272,128]{2,1,0:T(8,128)(2,1)S(1)}, bf16[2,272,128]{2,1,0:T(8,128)(2,1)S(1)}, u32[]{:S(2)}, u32[]{:S(2)}) %collective-permute-start.1) | collective-permute-done | bytes 139296 | tf_op jit(solution)/shard_map/ppermute | solution.py:251
  11.3 2.3 %collective-permute-start.5 = (bf16[2,192,128]{2,1,0:T(8,128)(2,1)S(1)}, bf16[2,192,128]{2,1,0:T(8,128)(2,1)S(1)}, u32[]{:S(2)}, u32[]{:S(2)}) collective-permute-start(bf16[2,192,128]{2,1,0:T(8,128)(2,1)S(1)} %get-tuple-element.26), channel_id=1, source_target_pairs={{0,4},{1,5},{2,6},{3,7},{4,0},{5,1},{6,2},{7,3},{8,12},{9,13},{10,... | collective-permute-start | bytes 294920 | tf_op jit(solution)/shard_map/ppermute | solution.py:251
  13.6 1.5 %collective-permute-start.6 = (bf16[2,192,128]{2,1,0:T(8,128)(2,1)S(1)}, bf16[2,192,128]{2,1,0:T(8,128)(2,1)S(1)}, u32[]{:S(2)}, u32[]{:S(2)}) collective-permute-start(bf16[2,192,128]{2,1,0:T(8,128)(2,1)S(1)} %get-tuple-element.27), channel_id=1, source_target_pairs={{0,2},{1,3},{2,0},{3,1},{4,6},{5,7},{6,4},{7,5},{8,10},{9,11},{10,... | collective-permute-start | bytes 294920 | tf_op jit(solution)/shard_map/ppermute | solution.py:251
  15.1 0.0 collective-permute-start.7
  15.1 0.4 %collective-permute-done.2.refs_3_ = bf16[2,272,128]{2,1,0:T(8,128)(2,1)S(1)} collective-permute-done((bf16[2,272,128]{2,1,0:T(8,128)(2,1)S(1)}, bf16[2,272,128]{2,1,0:T(8,128)(2,1)S(1)}, u32[]{:S(2)}, u32[]{:S(2)}) %collective-permute-start.2) | collective-permute-done | bytes 139296 | tf_op jit(solution)/shard_map/ppermute | solution.py:251
  15.5 0.5 %collective-permute-done.3.refs_4_ = bf16[2,272,128]{2,1,0:T(8,128)(2,1)S(1)} collective-permute-done((bf16[2,272,128]{2,1,0:T(8,128)(2,1)S(1)}, bf16[2,272,128]{2,1,0:T(8,128)(2,1)S(1)}, u32[]{:S(2)}, u32[]{:S(2)}) %collective-permute-start.3) | collective-permute-done | bytes 139296 | tf_op jit(solution)/shard_map/ppermute | solution.py:251
  16.0 0.4 %sum_offsets.3 = (f32[928,128]{1,0:T(8,128)S(1)}, f32[480,128]{1,0:T(8,128)S(1)}) custom-call(bf16[4,272,128]{2,1,0:T(8,128)(2,1)S(1)} %get-tuple-element.19.keep_ref.refs_0_, bf16[4,272,128]{2,1,0:T(8,128)(2,1)S(1)} %collective-permute-done.got_ref.refs_1_, bf16[2,272,128]{2,1,0:T(8,128)(2,1)S(1)} %collective-permute-done.1.refs_0_.refs_2_, ...), custom_call_target="tpu_custom_call" | custom-call | tf_op jit(solution)/shard_map/sum_offsets/pallas_call | solution.py:297
  16.5 2.7 %collective-permute-start.9 = (f16[480,128]{1,0:T(8,128)(2,1)S(1)}, f16[480,128]{1,0:T(8,128)(2,1)S(1)}, u32[]{:S(2)}, u32[]{:S(2)}) collective-permute-start(f16[480,128]{1,0:T(8,128)(2,1)S(1)} %convert_element_type.14), channel_id=1, source_target_pairs={{0,8},{1,9},{2,10},{3,11},{4,12},{5,13},{6,14},{7,15},{8,0},{9,1},... | collective-permute-start | bytes 368648 | tf_op jit(solution)/shard_map/ppermute | solution.py:251
  19.1 0.0 collective-permute-done.5.refs_7_
  19.1 0.0 collective-permute-done.6.refs_8_
  19.1 2.2 %collective-permute-done.7.refs_9_ = bf16[2,192,128]{2,1,0:T(8,128)(2,1)S(1)} collective-permute-done((bf16[2,192,128]{2,1,0:T(8,128)(2,1)S(1)}, bf16[2,192,128]{2,1,0:T(8,128)(2,1)S(1)}, u32[]{:S(2)}, u32[]{:S(2)}) %collective-permute-start.7) | collective-permute-done | bytes 98336 | tf_op jit(solution)/shard_map/ppermute | solution.py:251
  21.4 0.4 %sum_offsets.2 = (f32[768,128]{1,0:T(8,128)S(1)}, f32[400,128]{1,0:T(8,128)S(1)}) custom-call(bf16[4,272,128]{2,1,0:T(8,128)(2,1)S(1)} %get-tuple-element.19.keep_ref.refs_0_, bf16[4,272,128]{2,1,0:T(8,128)(2,1)S(1)} %collective-permute-done.got_ref.refs_1_, bf16[2,272,128]{2,1,0:T(8,128)(2,1)S(1)} %collective-permute-done.1.refs_0_.refs_2_, ...), custom_call_target="tpu_custom_call" | custom-call | tf_op jit(solution)/shard_map/sum_offsets/pallas_call | solution.py:297
  21.7 2.1 %collective-permute-start.8 = (f16[400,128]{1,0:T(8,128)(2,1)S(1)}, f16[400,128]{1,0:T(8,128)(2,1)S(1)}, u32[]{:S(2)}, u32[]{:S(2)}) collective-permute-start(f16[400,128]{1,0:T(8,128)(2,1)S(1)} %convert_element_type.12), channel_id=1, source_target_pairs={{0,8},{1,9},{2,10},{3,11},{4,12},{5,13},{6,14},{7,15},{8,0},{9,1},... | collective-permute-start | bytes 307208 | tf_op jit(solution)/shard_map/ppermute | solution.py:251
  23.8 1.3 %collective-permute-done.9 = f16[480,128]{1,0:T(8,128)(2,1)S(1)} collective-permute-done((f16[480,128]{1,0:T(8,128)(2,1)S(1)}, f16[480,128]{1,0:T(8,128)(2,1)S(1)}, u32[]{:S(2)}, u32[]{:S(2)}) %collective-permute-start.9) | collective-permute-done | bytes 122912 | tf_op jit(solution)/shard_map/ppermute | solution.py:251
  25.1 0.9 %join_offsets.2.refs_0_ = f32[7,128,128]{2,1,0:T(8,128)} custom-call(f32[928,128]{1,0:T(8,128)S(1)} %get-tuple-element.31.sums_ref, f32[480,128]{1,0:T(8,128)S(1)} %convert_element_type.15.far_ref), custom_call_target="tpu_custom_call" | custom-call | tf_op jit(solution)/shard_map/join_offsets/pallas_call | solution.py:314
  26.1 2.0 %collective-permute-done.8 = f16[400,128]{1,0:T(8,128)(2,1)S(1)} collective-permute-done((f16[400,128]{1,0:T(8,128)(2,1)S(1)}, f16[400,128]{1,0:T(8,128)(2,1)S(1)}, u32[]{:S(2)}, u32[]{:S(2)}) %collective-permute-start.8) | collective-permute-done | bytes 102432 | tf_op jit(solution)/shard_map/ppermute | solution.py:251
  28.0 0.7 %join_offsets.3 = f32[7,128,128]{2,1,0:T(8,128)} custom-call(f32[768,128]{1,0:T(8,128)S(1)} %get-tuple-element.29.sums_ref, f32[400,128]{1,0:T(8,128)S(1)} %convert_element_type.13.far_ref, f32[7,128,128]{2,1,0:T(8,128)} %join_offsets.2.refs_0_), custom_call_target="tpu_custom_call", output_to_operand_aliasing={{}: (2, {})} | custom-call | tf_op jit(solution)/shard_map/join_offsets/pallas_call | solution.py:314
  (6 shorter events, 0.1 us)
Async XLA Ops:
  2.2 1.7 %collective-permute-start = (bf16[4,272,128]{2,1,0:T(8,128)(2,1)S(1)}, bf16[4,272,128]{2,1,0:T(8,128)(2,1)S(1)}, u32[]{:S(2)}, u32[]{:S(2)}) collective-permute-start(bf16[4,272,128]{2,1,0:T(8,128)(2,1)S(1)} %get-tuple-element.20), channel_id=1, source_target_pairs={{0,1},{1,0},{2,3},{3,2},{4,5},{5,4},{6,7},{7,6},{8,9},{9,8},{10,11... | collective-permute-start | bytes 835592 | tf_op jit(solution)/shard_map/ppermute | solution.py:251
  2.8 5.8 %collective-permute-start.4 = (bf16[4,192,128]{2,1,0:T(8,128)(2,1)S(1)}, bf16[4,192,128]{2,1,0:T(8,128)(2,1)S(1)}, u32[]{:S(2)}, u32[]{:S(2)}) collective-permute-start(bf16[4,192,128]{2,1,0:T(8,128)(2,1)S(1)} %get-tuple-element.25), channel_id=1, source_target_pairs={{0,1},{1,0},{2,3},{3,2},{4,5},{5,4},{6,7},{7,6},{8,9},{9,8},{10,11... | collective-permute-start | bytes 589832 | tf_op jit(solution)/shard_map/ppermute | solution.py:251
  4.0 7.3 %collective-permute-start.1 = (bf16[2,272,128]{2,1,0:T(8,128)(2,1)S(1)}, bf16[2,272,128]{2,1,0:T(8,128)(2,1)S(1)}, u32[]{:S(2)}, u32[]{:S(2)}) collective-permute-start(bf16[2,272,128]{2,1,0:T(8,128)(2,1)S(1)} %get-tuple-element.21), channel_id=1, source_target_pairs={{0,4},{1,5},{2,6},{3,7},{4,0},{5,1},{6,2},{7,3},{8,12},{9,13},{10,... | collective-permute-start | bytes 417800 | tf_op jit(solution)/shard_map/ppermute | solution.py:251
  7.0 8.5 %collective-permute-start.2 = (bf16[2,272,128]{2,1,0:T(8,128)(2,1)S(1)}, bf16[2,272,128]{2,1,0:T(8,128)(2,1)S(1)}, u32[]{:S(2)}, u32[]{:S(2)}) collective-permute-start(bf16[2,272,128]{2,1,0:T(8,128)(2,1)S(1)} %get-tuple-element.22), channel_id=1, source_target_pairs={{0,2},{1,3},{2,0},{3,1},{4,6},{5,7},{6,4},{7,5},{8,10},{9,11},{10,... | collective-permute-start | bytes 417800 | tf_op jit(solution)/shard_map/ppermute | solution.py:251
  8.5 7.5 %collective-permute-start.3 = (bf16[2,272,128]{2,1,0:T(8,128)(2,1)S(1)}, bf16[2,272,128]{2,1,0:T(8,128)(2,1)S(1)}, u32[]{:S(2)}, u32[]{:S(2)}) collective-permute-start(bf16[2,272,128]{2,1,0:T(8,128)(2,1)S(1)} %get-tuple-element.23), channel_id=1, source_target_pairs={{0,6},{1,7},{2,4},{3,5},{4,2},{5,3},{6,0},{7,1},{8,14},{9,15},{10,... | collective-permute-start | bytes 417800 | tf_op jit(solution)/shard_map/ppermute | solution.py:251
  11.3 7.9 %collective-permute-start.5 = (bf16[2,192,128]{2,1,0:T(8,128)(2,1)S(1)}, bf16[2,192,128]{2,1,0:T(8,128)(2,1)S(1)}, u32[]{:S(2)}, u32[]{:S(2)}) collective-permute-start(bf16[2,192,128]{2,1,0:T(8,128)(2,1)S(1)} %get-tuple-element.26), channel_id=1, source_target_pairs={{0,4},{1,5},{2,6},{3,7},{4,0},{5,1},{6,2},{7,3},{8,12},{9,13},{10,... | collective-permute-start | bytes 294920 | tf_op jit(solution)/shard_map/ppermute | solution.py:251
  13.6 5.6 %collective-permute-start.6 = (bf16[2,192,128]{2,1,0:T(8,128)(2,1)S(1)}, bf16[2,192,128]{2,1,0:T(8,128)(2,1)S(1)}, u32[]{:S(2)}, u32[]{:S(2)}) collective-permute-start(bf16[2,192,128]{2,1,0:T(8,128)(2,1)S(1)} %get-tuple-element.27), channel_id=1, source_target_pairs={{0,2},{1,3},{2,0},{3,1},{4,6},{5,7},{6,4},{7,5},{8,10},{9,11},{10,... | collective-permute-start | bytes 294920 | tf_op jit(solution)/shard_map/ppermute | solution.py:251
  15.1 6.2 %collective-permute-start.7 = (bf16[2,192,128]{2,1,0:T(8,128)(2,1)S(1)}, bf16[2,192,128]{2,1,0:T(8,128)(2,1)S(1)}, u32[]{:S(2)}, u32[]{:S(2)}) collective-permute-start(bf16[2,192,128]{2,1,0:T(8,128)(2,1)S(1)} %get-tuple-element.28), channel_id=1, source_target_pairs={{0,6},{1,7},{2,4},{3,5},{4,2},{5,3},{6,0},{7,1},{8,14},{9,15},{10,... | collective-permute-start | bytes 294920 | tf_op jit(solution)/shard_map/ppermute | solution.py:251
  16.5 8.6 %collective-permute-start.9 = (f16[480,128]{1,0:T(8,128)(2,1)S(1)}, f16[480,128]{1,0:T(8,128)(2,1)S(1)}, u32[]{:S(2)}, u32[]{:S(2)}) collective-permute-start(f16[480,128]{1,0:T(8,128)(2,1)S(1)} %convert_element_type.14), channel_id=1, source_target_pairs={{0,8},{1,9},{2,10},{3,11},{4,12},{5,13},{6,14},{7,15},{8,0},{9,1},... | collective-permute-start | bytes 368648 | tf_op jit(solution)/shard_map/ppermute | solution.py:251
  21.7 6.3 %collective-permute-start.8 = (f16[400,128]{1,0:T(8,128)(2,1)S(1)}, f16[400,128]{1,0:T(8,128)(2,1)S(1)}, u32[]{:S(2)}, u32[]{:S(2)}) collective-permute-start(f16[400,128]{1,0:T(8,128)(2,1)S(1)} %convert_element_type.12), channel_id=1, source_target_pairs={{0,8},{1,9},{2,10},{3,11},{4,12},{5,13},{6,14},{7,15},{8,0},{9,1},... | collective-permute-start | bytes 307208 | tf_op jit(solution)/shard_map/ppermute | solution.py:251

commit v5 on v3

--- a/solution.py
+++ b/solution.py
@@ -142,6 +142,13 @@
             send_ref[pair] = rows_ref[CORES * pair + at % CORES, first:last]
 
 
+def order_of(chunk, pair_count):
+    def key(pair):
+        return (0 if chunk == 0 else -pair.bit_length(), pair.bit_count(), -pair)
+
+    return sorted(range(1, pair_count), key=key)
+
+
 def sum_kernel(chunk, slot_count, *refs):
     arrays, (sums_ref, scaled_ref) = refs[:-2], refs[-2:]
     width = sums_ref.shape[1]
@@ -150,19 +157,21 @@
     base = packed if chunk == 0 else 0
     sums_ref[...] = jnp.zeros_like(sums_ref)
 
-    def units(arrays):
-        return [(arrays[0], 0), (arrays[1], 0)] + [
-            (x, core) for x in arrays[2:] for core in range(CORES)
-        ]
+    def units(chunk, arrays):
+        found = {(0, core): (arrays[core], 0) for core in range(CORES)}
+        for pair, ref in zip(order_of(chunk, len(arrays) - CORES + 1), arrays[CORES:]):
+            found.update({(pair, core): (ref, core) for core in range(CORES)})
+        return found
 
     array_count = len(arrays) if chunk == 0 else len(arrays) // 2
-    tags = [
-        jnp.max(ref[at, half:packed].astype(jnp.float32)[TILE - 1 :, width - 1 :]).astype(
-            jnp.int32
-        )
-        for ref, at in units(arrays[:array_count])
-    ]
-    for tag, (ref, at) in zip(tags, units(arrays[-array_count:])):
+    tags = {
+        unit: jnp.max(
+            ref[at, half:packed].astype(jnp.float32)[TILE - 1 :, width - 1 :]
+        ).astype(jnp.int32)
+        for unit, (ref, at) in units(0, arrays[:array_count]).items()
+    }
+    for unit, (ref, at) in units(chunk, arrays[-array_count:]).items():
+        tag = tags[unit]
         away = tag // slot_count
         place = tag - slot_count * away
         if chunk == 0:
@@ -281,7 +290,7 @@
             compiler_params=params,
             name="merge_units",
         )(*gots, *tagged[CORES : CORES + chunk])
-        for pair in sorted(range(1, pair_count), key=lambda p: (p.bit_count(), -p)):
+        for pair in order_of(chunk, pair_count):
             gots.append(permute(merged[pair - 1], CORES * pair))
         tagged = tagged or gots
         count = sum_rows(chunk, width, slot_count)

time: 28.9 us -> 29.1 us (level)
  starting transfers between devices: 13.7 us -> 14.1 us
    ppermute x10, starting transfers between devices: 13.7 us -> 14.1 us  [permute(): return lax.ppermute(values, 'group', pairs)]
where the time goes in v5:
time: 29.1 us; the launch traced here: 28.9 us
  starting transfers between devices  14.1 us (48%)
  waiting for transfers between devices  9.97 us (34%)
  Pallas kernels  4.68 us (16%)
    ppermute x10, starting transfers between devices, permute(): return lax.ppermute(values, 'group', pairs)  14.1 us
    ppermute x10, waiting for transfers between devices, permute(): return lax.ppermute(values, 'group', pairs)  9.97 us
    pallas_call x1, Pallas kernels, shards(): pl.pallas_call(functools.partial(gram_kernel, total_groups, half), in_spe...  2.23 us
    pallas_call x2, Pallas kernels, shards(): pl.pallas_call(functools.partial(join_kernel, chunk, slot_count), in_spec...  1.65 us
    pallas_call x2, Pallas kernels, shards(): pl.pallas_call(functools.partial(sum_kernel, chunk, slot_count), out_shap...  0.75 us
  transfers between devices with their start and end apart: 10, of which 7 were waited for; matrix products, arithmetic and copies ran while one was open for 0% of the time, Pallas kernels for 6%

profile of v5, /device:TPU:0, one launch (start us, length us, event | category | flops | bytes accessed | tf_op | source)
XLA Modules:
  0.0 28.9 jit_solution(8929513658323400293)
XLA Ops:
  0.0 2.2 %gram_rows.1 = (bf16[4,272,128]{2,1,0:T(8,128)(2,1)S(1)}, bf16[4,272,128]{2,1,0:T(8,128)(2,1)S(1)}, bf16[4,192,128]{2,1,0:T(8,128)(2,1)S(1)}, bf16[4,192,128]{2,1,0:T(8,128)(2,1)S(1)}) custom-call(s32[2,4]{1,0:T(2,128)} %groups_hbm.1, bf16[2,512,512]{2,1,0:T(8,128)(2,1)} %cols_hbm.1), custom_call_target="tpu_custom_call" | custom-call | tf_op jit(solution)/shard_map/gram_rows/pallas_call | solution.py:262
  2.2 0.5 %collective-permute-start = (bf16[4,272,128]{2,1,0:T(8,128)(2,1)S(1)}, bf16[4,272,128]{2,1,0:T(8,128)(2,1)S(1)}, u32[]{:S(2)}, u32[]{:S(2)}) collective-permute-start(bf16[4,272,128]{2,1,0:T(8,128)(2,1)S(1)} %get-tuple-element.20), channel_id=1, source_target_pairs={{0,1},{1,0},{2,3},{3,2},{4,5},{5,4},{6,7},{7,6},{8,9},{9,8},{10,11... | collective-permute-start | bytes 835592 | tf_op jit(solution)/shard_map/ppermute | solution.py:256
  2.8 0.1 collective-permute-start.4
  2.8 1.1 %collective-permute-done.got_ref.refs_1_ = bf16[4,272,128]{2,1,0:T(8,128)(2,1)S(1)} collective-permute-done((bf16[4,272,128]{2,1,0:T(8,128)(2,1)S(1)}, bf16[4,272,128]{2,1,0:T(8,128)(2,1)S(1)}, u32[]{:S(2)}, u32[]{:S(2)}) %collective-permute-start) | collective-permute-done | bytes 278560 | tf_op jit(solution)/shard_map/ppermute | solution.py:256
  4.0 3.0 %collective-permute-start.1 = (bf16[2,272,128]{2,1,0:T(8,128)(2,1)S(1)}, bf16[2,272,128]{2,1,0:T(8,128)(2,1)S(1)}, u32[]{:S(2)}, u32[]{:S(2)}) collective-permute-start(bf16[2,272,128]{2,1,0:T(8,128)(2,1)S(1)} %get-tuple-element.21), channel_id=1, source_target_pairs={{0,4},{1,5},{2,6},{3,7},{4,0},{5,1},{6,2},{7,3},{8,12},{9,13},{10,... | collective-permute-start | bytes 417800 | tf_op jit(solution)/shard_map/ppermute | solution.py:256
  7.0 1.5 %collective-permute-start.2 = (bf16[2,272,128]{2,1,0:T(8,128)(2,1)S(1)}, bf16[2,272,128]{2,1,0:T(8,128)(2,1)S(1)}, u32[]{:S(2)}, u32[]{:S(2)}) collective-permute-start(bf16[2,272,128]{2,1,0:T(8,128)(2,1)S(1)} %get-tuple-element.22), channel_id=1, source_target_pairs={{0,2},{1,3},{2,0},{3,1},{4,6},{5,7},{6,4},{7,5},{8,10},{9,11},{10,... | collective-permute-start | bytes 417800 | tf_op jit(solution)/shard_map/ppermute | solution.py:256
  8.5 0.0 collective-permute-start.3
  8.5 0.0 collective-permute-done.4.got_ref.refs_6_
  8.5 2.7 %collective-permute-done.1.refs_0_.refs_2_ = bf16[2,272,128]{2,1,0:T(8,128)(2,1)S(1)} collective-permute-done((bf16[2,272,128]{2,1,0:T(8,128)(2,1)S(1)}, bf16[2,272,128]{2,1,0:T(8,128)(2,1)S(1)}, u32[]{:S(2)}, u32[]{:S(2)}) %collective-permute-start.1) | collective-permute-done | bytes 139296 | tf_op jit(solution)/shard_map/ppermute | solution.py:256
  11.3 2.3 %collective-permute-start.5 = (bf16[2,192,128]{2,1,0:T(8,128)(2,1)S(1)}, bf16[2,192,128]{2,1,0:T(8,128)(2,1)S(1)}, u32[]{:S(2)}, u32[]{:S(2)}) collective-permute-start(bf16[2,192,128]{2,1,0:T(8,128)(2,1)S(1)} %get-tuple-element.26), channel_id=1, source_target_pairs={{0,4},{1,5},{2,6},{3,7},{4,0},{5,1},{6,2},{7,3},{8,12},{9,13},{10,... | collective-permute-start | bytes 294920 | tf_op jit(solution)/shard_map/ppermute | solution.py:256
  13.6 1.0 %collective-permute-start.6 = (bf16[2,192,128]{2,1,0:T(8,128)(2,1)S(1)}, bf16[2,192,128]{2,1,0:T(8,128)(2,1)S(1)}, u32[]{:S(2)}, u32[]{:S(2)}) collective-permute-start(bf16[2,192,128]{2,1,0:T(8,128)(2,1)S(1)} %get-tuple-element.27), channel_id=1, source_target_pairs={{0,6},{1,7},{2,4},{3,5},{4,2},{5,3},{6,0},{7,1},{8,14},{9,15},{10,... | collective-permute-start | bytes 294920 | tf_op jit(solution)/shard_map/ppermute | solution.py:256
  14.6 0.5 %collective-permute-start.7 = (bf16[2,192,128]{2,1,0:T(8,128)(2,1)S(1)}, bf16[2,192,128]{2,1,0:T(8,128)(2,1)S(1)}, u32[]{:S(2)}, u32[]{:S(2)}) collective-permute-start(bf16[2,192,128]{2,1,0:T(8,128)(2,1)S(1)} %get-tuple-element.28), channel_id=1, source_target_pairs={{0,2},{1,3},{2,0},{3,1},{4,6},{5,7},{6,4},{7,5},{8,10},{9,11},{10,... | collective-permute-start | bytes 294920 | tf_op jit(solution)/shard_map/ppermute | solution.py:256
  15.1 0.2 collective-permute-done.2.refs_3_
  15.3 0.7 %collective-permute-done.3.refs_4_ = bf16[2,272,128]{2,1,0:T(8,128)(2,1)S(1)} collective-permute-done((bf16[2,272,128]{2,1,0:T(8,128)(2,1)S(1)}, bf16[2,272,128]{2,1,0:T(8,128)(2,1)S(1)}, u32[]{:S(2)}, u32[]{:S(2)}) %collective-permute-start.3) | collective-permute-done | bytes 139296 | tf_op jit(solution)/shard_map/ppermute | solution.py:256
  16.0 0.4 %sum_offsets.3 = (f32[928,128]{1,0:T(8,128)S(1)}, f32[480,128]{1,0:T(8,128)S(1)}) custom-call(bf16[4,272,128]{2,1,0:T(8,128)(2,1)S(1)} %get-tuple-element.19.keep_ref.refs_0_, bf16[4,272,128]{2,1,0:T(8,128)(2,1)S(1)} %collective-permute-done.got_ref.refs_1_, bf16[2,272,128]{2,1,0:T(8,128)(2,1)S(1)} %collective-permute-done.1.refs_0_.refs_2_, ...), custom_call_target="tpu_custom_call" | custom-call | tf_op jit(solution)/shard_map/sum_offsets/pallas_call | solution.py:297
  16.5 2.7 %collective-permute-start.9 = (f16[480,128]{1,0:T(8,128)(2,1)S(1)}, f16[480,128]{1,0:T(8,128)(2,1)S(1)}, u32[]{:S(2)}, u32[]{:S(2)}) collective-permute-start(f16[480,128]{1,0:T(8,128)(2,1)S(1)} %convert_element_type.14), channel_id=1, source_target_pairs={{0,8},{1,9},{2,10},{3,11},{4,12},{5,13},{6,14},{7,15},{8,0},{9,1},... | collective-permute-start | bytes 368648 | tf_op jit(solution)/shard_map/ppermute | solution.py:256
  19.1 0.0 collective-permute-done.5.refs_7_
  19.1 1.5 %collective-permute-done.6.refs_8_ = bf16[2,192,128]{2,1,0:T(8,128)(2,1)S(1)} collective-permute-done((bf16[2,192,128]{2,1,0:T(8,128)(2,1)S(1)}, bf16[2,192,128]{2,1,0:T(8,128)(2,1)S(1)}, u32[]{:S(2)}, u32[]{:S(2)}) %collective-permute-start.6) | collective-permute-done | bytes 98336 | tf_op jit(solution)/shard_map/ppermute | solution.py:256
  20.6 0.0 collective-permute-done.7.refs_9_
  20.6 0.4 %sum_offsets.2 = (f32[768,128]{1,0:T(8,128)S(1)}, f32[400,128]{1,0:T(8,128)S(1)}) custom-call(bf16[4,272,128]{2,1,0:T(8,128)(2,1)S(1)} %get-tuple-element.19.keep_ref.refs_0_, bf16[4,272,128]{2,1,0:T(8,128)(2,1)S(1)} %collective-permute-done.got_ref.refs_1_, bf16[2,272,128]{2,1,0:T(8,128)(2,1)S(1)} %collective-permute-done.1.refs_0_.refs_2_, ...), custom_call_target="tpu_custom_call" | custom-call | tf_op jit(solution)/shard_map/sum_offsets/pallas_call | solution.py:297
  21.0 2.5 %collective-permute-start.8 = (f16[400,128]{1,0:T(8,128)(2,1)S(1)}, f16[400,128]{1,0:T(8,128)(2,1)S(1)}, u32[]{:S(2)}, u32[]{:S(2)}) collective-permute-start(f16[400,128]{1,0:T(8,128)(2,1)S(1)} %convert_element_type.12), channel_id=1, source_target_pairs={{0,8},{1,9},{2,10},{3,11},{4,12},{5,13},{6,14},{7,15},{8,0},{9,1},... | collective-permute-start | bytes 307208 | tf_op jit(solution)/shard_map/ppermute | solution.py:256
  23.5 1.9 %collective-permute-done.9 = f16[480,128]{1,0:T(8,128)(2,1)S(1)} collective-permute-done((f16[480,128]{1,0:T(8,128)(2,1)S(1)}, f16[480,128]{1,0:T(8,128)(2,1)S(1)}, u32[]{:S(2)}, u32[]{:S(2)}) %collective-permute-start.9) | collective-permute-done | bytes 122912 | tf_op jit(solution)/shard_map/ppermute | solution.py:256
  25.4 0.9 %join_offsets.2.refs_0_ = f32[7,128,128]{2,1,0:T(8,128)} custom-call(f32[928,128]{1,0:T(8,128)S(1)} %get-tuple-element.31.sums_ref, f32[480,128]{1,0:T(8,128)S(1)} %convert_element_type.15.far_ref), custom_call_target="tpu_custom_call" | custom-call | tf_op jit(solution)/shard_map/join_offsets/pallas_call | solution.py:314
  26.3 1.8 %collective-permute-done.8 = f16[400,128]{1,0:T(8,128)(2,1)S(1)} collective-permute-done((f16[400,128]{1,0:T(8,128)(2,1)S(1)}, f16[400,128]{1,0:T(8,128)(2,1)S(1)}, u32[]{:S(2)}, u32[]{:S(2)}) %collective-permute-start.8) | collective-permute-done | bytes 102432 | tf_op jit(solution)/shard_map/ppermute | solution.py:256
  28.2 0.7 %join_offsets.3 = f32[7,128,128]{2,1,0:T(8,128)} custom-call(f32[768,128]{1,0:T(8,128)S(1)} %get-tuple-element.29.sums_ref, f32[400,128]{1,0:T(8,128)S(1)} %convert_element_type.13.far_ref, f32[7,128,128]{2,1,0:T(8,128)} %join_offsets.2.refs_0_), custom_call_target="tpu_custom_call", output_to_operand_aliasing={{}: (2, {})} | custom-call | tf_op jit(solution)/shard_map/join_offsets/pallas_call | solution.py:314
  (6 shorter events, 0.1 us)
Async XLA Ops:
  2.2 1.7 %collective-permute-start = (bf16[4,272,128]{2,1,0:T(8,128)(2,1)S(1)}, bf16[4,272,128]{2,1,0:T(8,128)(2,1)S(1)}, u32[]{:S(2)}, u32[]{:S(2)}) collective-permute-start(bf16[4,272,128]{2,1,0:T(8,128)(2,1)S(1)} %get-tuple-element.20), channel_id=1, source_target_pairs={{0,1},{1,0},{2,3},{3,2},{4,5},{5,4},{6,7},{7,6},{8,9},{9,8},{10,11... | collective-permute-start | bytes 835592 | tf_op jit(solution)/shard_map/ppermute | solution.py:256
  2.8 5.8 %collective-permute-start.4 = (bf16[4,192,128]{2,1,0:T(8,128)(2,1)S(1)}, bf16[4,192,128]{2,1,0:T(8,128)(2,1)S(1)}, u32[]{:S(2)}, u32[]{:S(2)}) collective-permute-start(bf16[4,192,128]{2,1,0:T(8,128)(2,1)S(1)} %get-tuple-element.25), channel_id=1, source_target_pairs={{0,1},{1,0},{2,3},{3,2},{4,5},{5,4},{6,7},{7,6},{8,9},{9,8},{10,11... | collective-permute-start | bytes 589832 | tf_op jit(solution)/shard_map/ppermute | solution.py:256
  4.0 7.3 %collective-permute-start.1 = (bf16[2,272,128]{2,1,0:T(8,128)(2,1)S(1)}, bf16[2,272,128]{2,1,0:T(8,128)(2,1)S(1)}, u32[]{:S(2)}, u32[]{:S(2)}) collective-permute-start(bf16[2,272,128]{2,1,0:T(8,128)(2,1)S(1)} %get-tuple-element.21), channel_id=1, source_target_pairs={{0,4},{1,5},{2,6},{3,7},{4,0},{5,1},{6,2},{7,3},{8,12},{9,13},{10,... | collective-permute-start | bytes 417800 | tf_op jit(solution)/shard_map/ppermute | solution.py:256
  7.0 8.4 %collective-permute-start.2 = (bf16[2,272,128]{2,1,0:T(8,128)(2,1)S(1)}, bf16[2,272,128]{2,1,0:T(8,128)(2,1)S(1)}, u32[]{:S(2)}, u32[]{:S(2)}) collective-permute-start(bf16[2,272,128]{2,1,0:T(8,128)(2,1)S(1)} %get-tuple-element.22), channel_id=1, source_target_pairs={{0,2},{1,3},{2,0},{3,1},{4,6},{5,7},{6,4},{7,5},{8,10},{9,11},{10,... | collective-permute-start | bytes 417800 | tf_op jit(solution)/shard_map/ppermute | solution.py:256
  8.5 7.6 %collective-permute-start.3 = (bf16[2,272,128]{2,1,0:T(8,128)(2,1)S(1)}, bf16[2,272,128]{2,1,0:T(8,128)(2,1)S(1)}, u32[]{:S(2)}, u32[]{:S(2)}) collective-permute-start(bf16[2,272,128]{2,1,0:T(8,128)(2,1)S(1)} %get-tuple-element.23), channel_id=1, source_target_pairs={{0,6},{1,7},{2,4},{3,5},{4,2},{5,3},{6,0},{7,1},{8,14},{9,15},{10,... | collective-permute-start | bytes 417800 | tf_op jit(solution)/shard_map/ppermute | solution.py:256
  11.3 7.9 %collective-permute-start.5 = (bf16[2,192,128]{2,1,0:T(8,128)(2,1)S(1)}, bf16[2,192,128]{2,1,0:T(8,128)(2,1)S(1)}, u32[]{:S(2)}, u32[]{:S(2)}) collective-permute-start(bf16[2,192,128]{2,1,0:T(8,128)(2,1)S(1)} %get-tuple-element.26), channel_id=1, source_target_pairs={{0,4},{1,5},{2,6},{3,7},{4,0},{5,1},{6,2},{7,3},{8,12},{9,13},{10,... | collective-permute-start | bytes 294920 | tf_op jit(solution)/shard_map/ppermute | solution.py:256
  13.6 7.1 %collective-permute-start.6 = (bf16[2,192,128]{2,1,0:T(8,128)(2,1)S(1)}, bf16[2,192,128]{2,1,0:T(8,128)(2,1)S(1)}, u32[]{:S(2)}, u32[]{:S(2)}) collective-permute-start(bf16[2,192,128]{2,1,0:T(8,128)(2,1)S(1)} %get-tuple-element.27), channel_id=1, source_target_pairs={{0,6},{1,7},{2,4},{3,5},{4,2},{5,3},{6,0},{7,1},{8,14},{9,15},{10,... | collective-permute-start | bytes 294920 | tf_op jit(solution)/shard_map/ppermute | solution.py:256
  14.6 6.0 %collective-permute-start.7 = (bf16[2,192,128]{2,1,0:T(8,128)(2,1)S(1)}, bf16[2,192,128]{2,1,0:T(8,128)(2,1)S(1)}, u32[]{:S(2)}, u32[]{:S(2)}) collective-permute-start(bf16[2,192,128]{2,1,0:T(8,128)(2,1)S(1)} %get-tuple-element.28), channel_id=1, source_target_pairs={{0,2},{1,3},{2,0},{3,1},{4,6},{5,7},{6,4},{7,5},{8,10},{9,11},{10,... | collective-permute-start | bytes 294920 | tf_op jit(solution)/shard_map/ppermute | solution.py:256
  16.5 8.9 %collective-permute-start.9 = (f16[480,128]{1,0:T(8,128)(2,1)S(1)}, f16[480,128]{1,0:T(8,128)(2,1)S(1)}, u32[]{:S(2)}, u32[]{:S(2)}) collective-permute-start(f16[480,128]{1,0:T(8,128)(2,1)S(1)} %convert_element_type.14), channel_id=1, source_target_pairs={{0,8},{1,9},{2,10},{3,11},{4,12},{5,13},{6,14},{7,15},{8,0},{9,1},... | collective-permute-start | bytes 368648 | tf_op jit(solution)/shard_map/ppermute | solution.py:256
  21.0 7.1 %collective-permute-start.8 = (f16[400,128]{1,0:T(8,128)(2,1)S(1)}, f16[400,128]{1,0:T(8,128)(2,1)S(1)}, u32[]{:S(2)}, u32[]{:S(2)}) collective-permute-start(f16[400,128]{1,0:T(8,128)(2,1)S(1)} %convert_element_type.12), channel_id=1, source_target_pairs={{0,8},{1,9},{2,10},{3,11},{4,12},{5,13},{6,14},{7,15},{8,0},{9,1},... | collective-permute-start | bytes 307208 | tf_op jit(solution)/shard_map/ppermute | solution.py:256

commit v6 on v3

--- a/solution.py
+++ b/solution.py
@@ -142,20 +142,32 @@
             send_ref[pair] = rows_ref[CORES * pair + at % CORES, first:last]
 
 
-def sum_kernel(chunk, slot_count, *refs):
-    arrays, (sums_ref, scaled_ref) = refs[:-2], refs[-2:]
-    width = sums_ref.shape[1]
+def order_of(chunk, pair_count):
+    def key(pair):
+        return (0 if chunk == 0 else -pair.bit_length(), pair.bit_count(), -pair)
+
+    return sorted(range(1, pair_count), key=key)
+
+
+def sum_kernel(chunk, slot_count, last, *refs):
+    width = refs[-1].shape[1]
     half, packed = width // 2, packed_rows(width)
     count = sum_rows(chunk, width, slot_count)
     base = packed if chunk == 0 else 0
-    sums_ref[...] = jnp.zeros_like(sums_ref)
+    if last:
+        before_ref, *arrays, sums_ref, scaled_ref = refs
+        sums_ref[...] = before_ref[...]
+    else:
+        *arrays, sums_ref = refs
+        sums_ref[...] = jnp.zeros_like(sums_ref)
 
     def units(arrays):
-        return [(arrays[0], 0), (arrays[1], 0)] + [
-            (x, core) for x in arrays[2:] for core in range(CORES)
+        own = 0 if last else CORES
+        return [(ref, 0) for ref in arrays[:own]] + [
+            (ref, core) for ref in arrays[own:] for core in range(CORES)
         ]
 
-    array_count = len(arrays) if chunk == 0 else len(arrays) // 2
+    array_count = len(arrays) // (chunk + 1)
     tags = [
         jnp.max(ref[at, half:packed].astype(jnp.float32)[TILE - 1 :, width - 1 :]).astype(
             jnp.int32
@@ -174,6 +186,8 @@
             block = ref[at, base + part * half : base + (part + 1) * half]
             sums_ref[pl.ds(pl.multiple_of(to, TILE), half)] += block.astype(jnp.float32)
 
+    if not last:
+        return
     if chunk == 0:
         col = lax.broadcasted_iota(jnp.int32, (TILE, width), 1)
         for at in (half, count + half):
@@ -281,20 +295,24 @@
             compiler_params=params,
             name="merge_units",
         )(*gots, *tagged[CORES : CORES + chunk])
-        for pair in sorted(range(1, pair_count), key=lambda p: (p.bit_count(), -p)):
+        for pair in order_of(chunk, pair_count):
             gots.append(permute(merged[pair - 1], CORES * pair))
         tagged = tagged or gots
         count = sum_rows(chunk, width, slot_count)
-        sums, scaled = pl.pallas_call(
-            functools.partial(sum_kernel, chunk, slot_count),
-            out_shape=(
-                jax.ShapeDtypeStruct((2 * count, width), jnp.float32),
-                jax.ShapeDtypeStruct((count + TILE, width), jnp.float32),
-            ),
-            cost_estimate=light,
-            compiler_params=params,
-            name="sum_offsets",
-        )(*(tagged if chunk == 0 else tagged + gots))
+        shape = jax.ShapeDtypeStruct((2 * count, width), jnp.float32)
+        scaled = jax.ShapeDtypeStruct((count + TILE, width), jnp.float32)
+        by_chip = dict(zip(order_of(0, pair_count), tagged[CORES:]))
+        tags = tagged[:CORES] + [by_chip[pair] for pair in order_of(chunk, pair_count)]
+        sums = ()
+        for last, arrays in ((False, slice(0, -1)), (True, slice(-1, None))):
+            sums = pl.pallas_call(
+                functools.partial(sum_kernel, chunk, slot_count, last),
+                out_shape=(shape, scaled) if last else (shape,),
+                cost_estimate=light,
+                compiler_params=params,
+                name="sum_offsets",
+            )(*sums, *(tags[arrays] if chunk else ()), *gots[arrays])
+        sums, scaled = sums
         far = permute(scaled.astype(jnp.float16), half)
         pieces.append((sums, far.astype(jnp.float32)))
 

time: 28.9 us -> 28.9 us (level)
  waiting for transfers between devices: 10.2 us -> 9.54 us
  starting transfers between devices: 13.7 us -> 14.2 us
    ppermute x10, waiting for transfers between devices: 10.2 us -> 9.54 us  [permute(): return lax.ppermute(values, 'group', pairs)]
    ppermute x10, starting transfers between devices: 13.7 us -> 14.2 us  [permute(): return lax.ppermute(values, 'group', pairs)]
    pallas_call x2 -> x4, Pallas kernels: 0.75 us -> 0.96 us  [shards(): pl.pallas_call(functools.partial(sum_kernel, chunk, slot_count, last), ou...]
  transfers between devices with their start and end apart: 10 -> 10, of which waited for: 7 -> 7; matrix products, arithmetic and copies ran while one was open for 0% -> 0% of each run, Pallas kernels for 6% -> 7%
where the time goes in v6:
time: 28.9 us; the launch traced here: 28.8 us
  starting transfers between devices  14.2 us (49%)
  waiting for transfers between devices  9.54 us (33%)
  Pallas kernels  4.88 us (17%)
    ppermute x10, starting transfers between devices, permute(): return lax.ppermute(values, 'group', pairs)  14.2 us
    ppermute x10, waiting for transfers between devices, permute(): return lax.ppermute(values, 'group', pairs)  9.54 us
    pallas_call x1, Pallas kernels, shards(): pl.pallas_call(functools.partial(gram_kernel, total_groups, half), in_spe...  2.23 us
    pallas_call x2, Pallas kernels, shards(): pl.pallas_call(functools.partial(join_kernel, chunk, slot_count), in_spec...  1.65 us
    pallas_call x4, Pallas kernels, shards(): pl.pallas_call(functools.partial(sum_kernel, chunk, slot_count, last), ou...  0.96 us
  transfers between devices with their start and end apart: 10, of which 7 were waited for; matrix products, arithmetic and copies ran while one was open for 0% of the time, Pallas kernels for 7%

profile of v6, /device:TPU:0, one launch (start us, length us, event | category | flops | bytes accessed | tf_op | source)
XLA Modules:
  0.0 28.8 jit_solution(3710241013662209340)
XLA Ops:
  0.0 2.2 %gram_rows.1 = (bf16[4,272,128]{2,1,0:T(8,128)(2,1)S(1)}, bf16[4,272,128]{2,1,0:T(8,128)(2,1)S(1)}, bf16[4,192,128]{2,1,0:T(8,128)(2,1)S(1)}, bf16[4,192,128]{2,1,0:T(8,128)(2,1)S(1)}) custom-call(s32[2,4]{1,0:T(2,128)} %groups_hbm.1, bf16[2,512,512]{2,1,0:T(8,128)(2,1)} %cols_hbm.1), custom_call_target="tpu_custom_call" | custom-call | tf_op jit(solution)/shard_map/gram_rows/pallas_call | solution.py:267
  2.2 0.5 %collective-permute-start = (bf16[4,272,128]{2,1,0:T(8,128)(2,1)S(1)}, bf16[4,272,128]{2,1,0:T(8,128)(2,1)S(1)}, u32[]{:S(2)}, u32[]{:S(2)}) collective-permute-start(bf16[4,272,128]{2,1,0:T(8,128)(2,1)S(1)} %get-tuple-element.20), channel_id=1, source_target_pairs={{0,1},{1,0},{2,3},{3,2},{4,5},{5,4},{6,7},{7,6},{8,9},{9,8},{10,11... | collective-permute-start | bytes 835592 | tf_op jit(solution)/shard_map/ppermute | solution.py:261
  2.8 0.1 collective-permute-start.3
  2.8 1.1 %collective-permute-done.got_ref.refs_1_ = bf16[4,272,128]{2,1,0:T(8,128)(2,1)S(1)} collective-permute-done((bf16[4,272,128]{2,1,0:T(8,128)(2,1)S(1)}, bf16[4,272,128]{2,1,0:T(8,128)(2,1)S(1)}, u32[]{:S(2)}, u32[]{:S(2)}) %collective-permute-start) | collective-permute-done | bytes 278560 | tf_op jit(solution)/shard_map/ppermute | solution.py:261
  4.0 3.0 %collective-permute-start.1 = (bf16[2,272,128]{2,1,0:T(8,128)(2,1)S(1)}, bf16[2,272,128]{2,1,0:T(8,128)(2,1)S(1)}, u32[]{:S(2)}, u32[]{:S(2)}) collective-permute-start(bf16[2,272,128]{2,1,0:T(8,128)(2,1)S(1)} %get-tuple-element.21), channel_id=1, source_target_pairs={{0,4},{1,5},{2,6},{3,7},{4,0},{5,1},{6,2},{7,3},{8,12},{9,13},{10,... | collective-permute-start | bytes 417800 | tf_op jit(solution)/shard_map/ppermute | solution.py:261
  7.0 1.5 %collective-permute-start.6 = (bf16[2,272,128]{2,1,0:T(8,128)(2,1)S(1)}, bf16[2,272,128]{2,1,0:T(8,128)(2,1)S(1)}, u32[]{:S(2)}, u32[]{:S(2)}) collective-permute-start(bf16[2,272,128]{2,1,0:T(8,128)(2,1)S(1)} %get-tuple-element.27), channel_id=1, source_target_pairs={{0,2},{1,3},{2,0},{3,1},{4,6},{5,7},{6,4},{7,5},{8,10},{9,11},{10,... | collective-permute-start | bytes 417800 | tf_op jit(solution)/shard_map/ppermute | solution.py:261
  8.5 0.0 collective-permute-start.2
  8.5 0.0 collective-permute-done.3.got_ref.refs_5_
  8.5 2.7 %collective-permute-done.1.refs_0_.refs_2_ = bf16[2,272,128]{2,1,0:T(8,128)(2,1)S(1)} collective-permute-done((bf16[2,272,128]{2,1,0:T(8,128)(2,1)S(1)}, bf16[2,272,128]{2,1,0:T(8,128)(2,1)S(1)}, u32[]{:S(2)}, u32[]{:S(2)}) %collective-permute-start.1) | collective-permute-done | bytes 139296 | tf_op jit(solution)/shard_map/ppermute | solution.py:261
  11.3 2.3 %collective-permute-start.4 = (bf16[2,192,128]{2,1,0:T(8,128)(2,1)S(1)}, bf16[2,192,128]{2,1,0:T(8,128)(2,1)S(1)}, u32[]{:S(2)}, u32[]{:S(2)}) collective-permute-start(bf16[2,192,128]{2,1,0:T(8,128)(2,1)S(1)} %get-tuple-element.25), channel_id=1, source_target_pairs={{0,4},{1,5},{2,6},{3,7},{4,0},{5,1},{6,2},{7,3},{8,12},{9,13},{10,... | collective-permute-start | bytes 294920 | tf_op jit(solution)/shard_map/ppermute | solution.py:261
  13.6 1.0 %collective-permute-start.5 = (bf16[2,192,128]{2,1,0:T(8,128)(2,1)S(1)}, bf16[2,192,128]{2,1,0:T(8,128)(2,1)S(1)}, u32[]{:S(2)}, u32[]{:S(2)}) collective-permute-start(bf16[2,192,128]{2,1,0:T(8,128)(2,1)S(1)} %get-tuple-element.26), channel_id=1, source_target_pairs={{0,6},{1,7},{2,4},{3,5},{4,2},{5,3},{6,0},{7,1},{8,14},{9,15},{10,... | collective-permute-start | bytes 294920 | tf_op jit(solution)/shard_map/ppermute | solution.py:261
  14.6 0.5 %collective-permute-start.7 = (bf16[2,192,128]{2,1,0:T(8,128)(2,1)S(1)}, bf16[2,192,128]{2,1,0:T(8,128)(2,1)S(1)}, u32[]{:S(2)}, u32[]{:S(2)}) collective-permute-start(bf16[2,192,128]{2,1,0:T(8,128)(2,1)S(1)} %get-tuple-element.28), channel_id=1, source_target_pairs={{0,2},{1,3},{2,0},{3,1},{4,6},{5,7},{6,4},{7,5},{8,10},{9,11},{10,... | collective-permute-start | bytes 294920 | tf_op jit(solution)/shard_map/ppermute | solution.py:261
  15.1 0.2 collective-permute-done.6.refs_1_.refs_3_
  15.3 0.2 sum_offsets.6.refs_0_
  15.6 0.5 %collective-permute-done.2.refs_3_.refs_1_ = bf16[2,272,128]{2,1,0:T(8,128)(2,1)S(1)} collective-permute-done((bf16[2,272,128]{2,1,0:T(8,128)(2,1)S(1)}, bf16[2,272,128]{2,1,0:T(8,128)(2,1)S(1)}, u32[]{:S(2)}, u32[]{:S(2)}) %collective-permute-start.2) | collective-permute-done | bytes 139296 | tf_op jit(solution)/shard_map/ppermute | solution.py:261
  16.0 0.3 sum_offsets.7
  16.4 2.7 %collective-permute-start.9 = (f16[480,128]{1,0:T(8,128)(2,1)S(1)}, f16[480,128]{1,0:T(8,128)(2,1)S(1)}, u32[]{:S(2)}, u32[]{:S(2)}) collective-permute-start(f16[480,128]{1,0:T(8,128)(2,1)S(1)} %convert_element_type.14), channel_id=1, source_target_pairs={{0,8},{1,9},{2,10},{3,11},{4,12},{5,13},{6,14},{7,15},{8,0},{9,1},... | collective-permute-start | bytes 368648 | tf_op jit(solution)/shard_map/ppermute | solution.py:261
  19.0 0.0 collective-permute-done.4.refs_6_
  19.0 1.6 %collective-permute-done.5.refs_7_ = bf16[2,192,128]{2,1,0:T(8,128)(2,1)S(1)} collective-permute-done((bf16[2,192,128]{2,1,0:T(8,128)(2,1)S(1)}, bf16[2,192,128]{2,1,0:T(8,128)(2,1)S(1)}, u32[]{:S(2)}, u32[]{:S(2)}) %collective-permute-start.5) | collective-permute-done | bytes 98336 | tf_op jit(solution)/shard_map/ppermute | solution.py:261
  20.6 0.2 sum_offsets.4.refs_0_
  20.8 0.0 collective-permute-done.7.refs_2_
  20.8 0.3 sum_offsets.5
  21.1 2.5 %collective-permute-start.8 = (f16[400,128]{1,0:T(8,128)(2,1)S(1)}, f16[400,128]{1,0:T(8,128)(2,1)S(1)}, u32[]{:S(2)}, u32[]{:S(2)}) collective-permute-start(f16[400,128]{1,0:T(8,128)(2,1)S(1)} %convert_element_type.12), channel_id=1, source_target_pairs={{0,8},{1,9},{2,10},{3,11},{4,12},{5,13},{6,14},{7,15},{8,0},{9,1},... | collective-permute-start | bytes 307208 | tf_op jit(solution)/shard_map/ppermute | solution.py:261
  23.6 1.6 %collective-permute-done.9 = f16[480,128]{1,0:T(8,128)(2,1)S(1)} collective-permute-done((f16[480,128]{1,0:T(8,128)(2,1)S(1)}, f16[480,128]{1,0:T(8,128)(2,1)S(1)}, u32[]{:S(2)}, u32[]{:S(2)}) %collective-permute-start.9) | collective-permute-done | bytes 122912 | tf_op jit(solution)/shard_map/ppermute | solution.py:261
  25.2 0.9 %join_offsets.2.refs_0_ = f32[7,128,128]{2,1,0:T(8,128)} custom-call(f32[928,128]{1,0:T(8,128)S(1)} %get-tuple-element.31.sums_ref, f32[480,128]{1,0:T(8,128)S(1)} %convert_element_type.15.far_ref), custom_call_target="tpu_custom_call" | custom-call | tf_op jit(solution)/shard_map/join_offsets/pallas_call | solution.py:323
  26.2 1.9 %collective-permute-done.8 = f16[400,128]{1,0:T(8,128)(2,1)S(1)} collective-permute-done((f16[400,128]{1,0:T(8,128)(2,1)S(1)}, f16[400,128]{1,0:T(8,128)(2,1)S(1)}, u32[]{:S(2)}, u32[]{:S(2)}) %collective-permute-start.8) | collective-permute-done | bytes 102432 | tf_op jit(solution)/shard_map/ppermute | solution.py:261
  28.0 0.7 %join_offsets.3 = f32[7,128,128]{2,1,0:T(8,128)} custom-call(f32[768,128]{1,0:T(8,128)S(1)} %get-tuple-element.29.sums_ref, f32[400,128]{1,0:T(8,128)S(1)} %convert_element_type.13.far_ref, f32[7,128,128]{2,1,0:T(8,128)} %join_offsets.2.refs_0_), custom_call_target="tpu_custom_call", output_to_operand_aliasing={{}: (2, {})} | custom-call | tf_op jit(solution)/shard_map/join_offsets/pallas_call | solution.py:323
  (6 shorter events, 0.1 us)
Async XLA Ops:
  2.2 1.7 %collective-permute-start = (bf16[4,272,128]{2,1,0:T(8,128)(2,1)S(1)}, bf16[4,272,128]{2,1,0:T(8,128)(2,1)S(1)}, u32[]{:S(2)}, u32[]{:S(2)}) collective-permute-start(bf16[4,272,128]{2,1,0:T(8,128)(2,1)S(1)} %get-tuple-element.20), channel_id=1, source_target_pairs={{0,1},{1,0},{2,3},{3,2},{4,5},{5,4},{6,7},{7,6},{8,9},{9,8},{10,11... | collective-permute-start | bytes 835592 | tf_op jit(solution)/shard_map/ppermute | solution.py:261
  2.8 5.8 %collective-permute-start.3 = (bf16[4,192,128]{2,1,0:T(8,128)(2,1)S(1)}, bf16[4,192,128]{2,1,0:T(8,128)(2,1)S(1)}, u32[]{:S(2)}, u32[]{:S(2)}) collective-permute-start(bf16[4,192,128]{2,1,0:T(8,128)(2,1)S(1)} %get-tuple-element.24), channel_id=1, source_target_pairs={{0,1},{1,0},{2,3},{3,2},{4,5},{5,4},{6,7},{7,6},{8,9},{9,8},{10,11... | collective-permute-start | bytes 589832 | tf_op jit(solution)/shard_map/ppermute | solution.py:261
  4.0 7.3 %collective-permute-start.1 = (bf16[2,272,128]{2,1,0:T(8,128)(2,1)S(1)}, bf16[2,272,128]{2,1,0:T(8,128)(2,1)S(1)}, u32[]{:S(2)}, u32[]{:S(2)}) collective-permute-start(bf16[2,272,128]{2,1,0:T(8,128)(2,1)S(1)} %get-tuple-element.21), channel_id=1, source_target_pairs={{0,4},{1,5},{2,6},{3,7},{4,0},{5,1},{6,2},{7,3},{8,12},{9,13},{10,... | collective-permute-start | bytes 417800 | tf_op jit(solution)/shard_map/ppermute | solution.py:261
  7.0 8.4 %collective-permute-start.6 = (bf16[2,272,128]{2,1,0:T(8,128)(2,1)S(1)}, bf16[2,272,128]{2,1,0:T(8,128)(2,1)S(1)}, u32[]{:S(2)}, u32[]{:S(2)}) collective-permute-start(bf16[2,272,128]{2,1,0:T(8,128)(2,1)S(1)} %get-tuple-element.27), channel_id=1, source_target_pairs={{0,2},{1,3},{2,0},{3,1},{4,6},{5,7},{6,4},{7,5},{8,10},{9,11},{10,... | collective-permute-start | bytes 417800 | tf_op jit(solution)/shard_map/ppermute | solution.py:261
  8.5 7.6 %collective-permute-start.2 = (bf16[2,272,128]{2,1,0:T(8,128)(2,1)S(1)}, bf16[2,272,128]{2,1,0:T(8,128)(2,1)S(1)}, u32[]{:S(2)}, u32[]{:S(2)}) collective-permute-start(bf16[2,272,128]{2,1,0:T(8,128)(2,1)S(1)} %get-tuple-element.22), channel_id=1, source_target_pairs={{0,6},{1,7},{2,4},{3,5},{4,2},{5,3},{6,0},{7,1},{8,14},{9,15},{10,... | collective-permute-start | bytes 417800 | tf_op jit(solution)/shard_map/ppermute | solution.py:261
  11.3 7.8 %collective-permute-start.4 = (bf16[2,192,128]{2,1,0:T(8,128)(2,1)S(1)}, bf16[2,192,128]{2,1,0:T(8,128)(2,1)S(1)}, u32[]{:S(2)}, u32[]{:S(2)}) collective-permute-start(bf16[2,192,128]{2,1,0:T(8,128)(2,1)S(1)} %get-tuple-element.25), channel_id=1, source_target_pairs={{0,4},{1,5},{2,6},{3,7},{4,0},{5,1},{6,2},{7,3},{8,12},{9,13},{10,... | collective-permute-start | bytes 294920 | tf_op jit(solution)/shard_map/ppermute | solution.py:261
  13.6 7.0 %collective-permute-start.5 = (bf16[2,192,128]{2,1,0:T(8,128)(2,1)S(1)}, bf16[2,192,128]{2,1,0:T(8,128)(2,1)S(1)}, u32[]{:S(2)}, u32[]{:S(2)}) collective-permute-start(bf16[2,192,128]{2,1,0:T(8,128)(2,1)S(1)} %get-tuple-element.26), channel_id=1, source_target_pairs={{0,6},{1,7},{2,4},{3,5},{4,2},{5,3},{6,0},{7,1},{8,14},{9,15},{10,... | collective-permute-start | bytes 294920 | tf_op jit(solution)/shard_map/ppermute | solution.py:261
  14.6 6.2 %collective-permute-start.7 = (bf16[2,192,128]{2,1,0:T(8,128)(2,1)S(1)}, bf16[2,192,128]{2,1,0:T(8,128)(2,1)S(1)}, u32[]{:S(2)}, u32[]{:S(2)}) collective-permute-start(bf16[2,192,128]{2,1,0:T(8,128)(2,1)S(1)} %get-tuple-element.28), channel_id=1, source_target_pairs={{0,2},{1,3},{2,0},{3,1},{4,6},{5,7},{6,4},{7,5},{8,10},{9,11},{10,... | collective-permute-start | bytes 294920 | tf_op jit(solution)/shard_map/ppermute | solution.py:261
  16.4 8.9 %collective-permute-start.9 = (f16[480,128]{1,0:T(8,128)(2,1)S(1)}, f16[480,128]{1,0:T(8,128)(2,1)S(1)}, u32[]{:S(2)}, u32[]{:S(2)}) collective-permute-start(f16[480,128]{1,0:T(8,128)(2,1)S(1)} %convert_element_type.14), channel_id=1, source_target_pairs={{0,8},{1,9},{2,10},{3,11},{4,12},{5,13},{6,14},{7,15},{8,0},{9,1},... | collective-permute-start | bytes 368648 | tf_op jit(solution)/shard_map/ppermute | solution.py:261
  21.1 6.9 %collective-permute-start.8 = (f16[400,128]{1,0:T(8,128)(2,1)S(1)}, f16[400,128]{1,0:T(8,128)(2,1)S(1)}, u32[]{:S(2)}, u32[]{:S(2)}) collective-permute-start(f16[400,128]{1,0:T(8,128)(2,1)S(1)} %convert_element_type.12), channel_id=1, source_target_pairs={{0,8},{1,9},{2,10},{3,11},{4,12},{5,13},{6,14},{7,15},{8,0},{9,1},... | collective-permute-start | bytes 307208 | tf_op jit(solution)/shard_map/ppermute | solution.py:261

commit v7 on v6

--- a/solution.py
+++ b/solution.py
@@ -92,11 +92,12 @@
         for part in range(COPIES):
             cols_copy(region, part).start()
     groups_copy.wait()
-    packed = packed_rows(width)
-
-    def add_region(region, carry):
+    for region in range(region_count):
         for part in range(COPIES):
             cols_copy(region, part).wait()
+    packed = packed_rows(width)
+
+    def add_region(region, carry):
         cols = cols_ref[region]
         depth = cols.shape[1] // PRODUCTS
         grams = [
@@ -149,20 +150,18 @@
     return sorted(range(1, pair_count), key=key)
 
 
-def sum_kernel(chunk, slot_count, last, *refs):
+def sum_kernel(chunk, slot_count, first, last, *refs):
     width = refs[-1].shape[1]
     half, packed = width // 2, packed_rows(width)
     count = sum_rows(chunk, width, slot_count)
     base = packed if chunk == 0 else 0
-    if last:
-        before_ref, *arrays, sums_ref, scaled_ref = refs
-        sums_ref[...] = before_ref[...]
-    else:
-        *arrays, sums_ref = refs
-        sums_ref[...] = jnp.zeros_like(sums_ref)
+    arrays = list(refs)
+    scaled_ref = arrays.pop() if last else None
+    sums_ref = arrays.pop()
+    sums_ref[...] = jnp.zeros_like(sums_ref) if first else arrays.pop(0)[...]
 
     def units(arrays):
-        own = 0 if last else CORES
+        own = CORES if first else 0
         return [(ref, 0) for ref in arrays[:own]] + [
             (ref, core) for ref in arrays[own:] for core in range(CORES)
         ]
@@ -304,9 +303,11 @@
         by_chip = dict(zip(order_of(0, pair_count), tagged[CORES:]))
         tags = tagged[:CORES] + [by_chip[pair] for pair in order_of(chunk, pair_count)]
         sums = ()
-        for last, arrays in ((False, slice(0, -1)), (True, slice(-1, None))):
+        calls = [(0, -1), (-1, None)] if chunk == 0 else [(0, None)]
+        for begin, end in calls:
+            first, last, arrays = begin == 0, end is None, slice(begin, end)
             sums = pl.pallas_call(
-                functools.partial(sum_kernel, chunk, slot_count, last),
+                functools.partial(sum_kernel, chunk, slot_count, first, last),
                 out_shape=(shape, scaled) if last else (shape,),
                 cost_estimate=light,
                 compiler_params=params,

time: 28.9 us -> 28.8 us (level)
    pallas_call x4 -> x3, Pallas kernels: 0.96 us -> 0.85 us  [shards(): pl.pallas_call(functools.partial(sum_kernel, chunk, slot_count, first, la...]
  transfers between devices with their start and end apart: 10 -> 10, of which waited for: 7 -> 7; matrix products, arithmetic and copies ran while one was open for 0% -> 0% of each run, Pallas kernels for 7% -> 6%
where the time goes in v7:
time: 28.8 us; the launch traced here: 28.7 us
  starting transfers between devices  14.2 us (49%)
  waiting for transfers between devices  9.64 us (33%)
  Pallas kernels  4.67 us (16%)
    ppermute x10, starting transfers between devices, permute(): return lax.ppermute(values, 'group', pairs)  14.2 us
    ppermute x10, waiting for transfers between devices, permute(): return lax.ppermute(values, 'group', pairs)  9.64 us
    pallas_call x1, Pallas kernels, shards(): pl.pallas_call(functools.partial(gram_kernel, total_groups, half), in_spe...  2.12 us
    pallas_call x2, Pallas kernels, shards(): pl.pallas_call(functools.partial(join_kernel, chunk, slot_count), in_spec...  1.66 us
    pallas_call x3, Pallas kernels, shards(): pl.pallas_call(functools.partial(sum_kernel, chunk, slot_count, first, la...  0.85 us
  transfers between devices with their start and end apart: 10, of which 7 were waited for; matrix products, arithmetic and copies ran while one was open for 0% of the time, Pallas kernels for 6%

profile of v7, /device:TPU:0, one launch (start us, length us, event | category | flops | bytes accessed | tf_op | source)
XLA Modules:
  0.0 28.7 jit_solution(10700358157440869474)
XLA Ops:
  0.0 2.1 %gram_rows.1 = (bf16[4,272,128]{2,1,0:T(8,128)(2,1)S(1)}, bf16[4,272,128]{2,1,0:T(8,128)(2,1)S(1)}, bf16[4,192,128]{2,1,0:T(8,128)(2,1)S(1)}, bf16[4,192,128]{2,1,0:T(8,128)(2,1)S(1)}) custom-call(s32[2,4]{1,0:T(2,128)} %groups_hbm.1, bf16[2,512,512]{2,1,0:T(8,128)(2,1)} %cols_hbm.1), custom_call_target="tpu_custom_call" | custom-call | tf_op jit(solution)/shard_map/gram_rows/pallas_call | solution.py:266
  2.1 0.5 %collective-permute-start = (bf16[4,272,128]{2,1,0:T(8,128)(2,1)S(1)}, bf16[4,272,128]{2,1,0:T(8,128)(2,1)S(1)}, u32[]{:S(2)}, u32[]{:S(2)}) collective-permute-start(bf16[4,272,128]{2,1,0:T(8,128)(2,1)S(1)} %get-tuple-element.20), channel_id=1, source_target_pairs={{0,1},{1,0},{2,3},{3,2},{4,5},{5,4},{6,7},{7,6},{8,9},{9,8},{10,11... | collective-permute-start | bytes 835592 | tf_op jit(solution)/shard_map/ppermute | solution.py:260
  2.6 0.1 collective-permute-start.4
  2.7 1.1 %collective-permute-done.got_ref.refs_1_ = bf16[4,272,128]{2,1,0:T(8,128)(2,1)S(1)} collective-permute-done((bf16[4,272,128]{2,1,0:T(8,128)(2,1)S(1)}, bf16[4,272,128]{2,1,0:T(8,128)(2,1)S(1)}, u32[]{:S(2)}, u32[]{:S(2)}) %collective-permute-start) | collective-permute-done | bytes 278560 | tf_op jit(solution)/shard_map/ppermute | solution.py:260
  3.9 3.0 %collective-permute-start.1 = (bf16[2,272,128]{2,1,0:T(8,128)(2,1)S(1)}, bf16[2,272,128]{2,1,0:T(8,128)(2,1)S(1)}, u32[]{:S(2)}, u32[]{:S(2)}) collective-permute-start(bf16[2,272,128]{2,1,0:T(8,128)(2,1)S(1)} %get-tuple-element.21), channel_id=1, source_target_pairs={{0,4},{1,5},{2,6},{3,7},{4,0},{5,1},{6,2},{7,3},{8,12},{9,13},{10,... | collective-permute-start | bytes 417800 | tf_op jit(solution)/shard_map/ppermute | solution.py:260
  6.9 1.5 %collective-permute-start.3 = (bf16[2,272,128]{2,1,0:T(8,128)(2,1)S(1)}, bf16[2,272,128]{2,1,0:T(8,128)(2,1)S(1)}, u32[]{:S(2)}, u32[]{:S(2)}) collective-permute-start(bf16[2,272,128]{2,1,0:T(8,128)(2,1)S(1)} %get-tuple-element.23), channel_id=1, source_target_pairs={{0,2},{1,3},{2,0},{3,1},{4,6},{5,7},{6,4},{7,5},{8,10},{9,11},{10,... | collective-permute-start | bytes 417800 | tf_op jit(solution)/shard_map/ppermute | solution.py:260
  8.4 0.0 collective-permute-start.2
  8.4 0.0 collective-permute-done.4.got_ref.refs_6_
  8.4 2.7 %collective-permute-done.1.refs_0_.refs_2_ = bf16[2,272,128]{2,1,0:T(8,128)(2,1)S(1)} collective-permute-done((bf16[2,272,128]{2,1,0:T(8,128)(2,1)S(1)}, bf16[2,272,128]{2,1,0:T(8,128)(2,1)S(1)}, u32[]{:S(2)}, u32[]{:S(2)}) %collective-permute-start.1) | collective-permute-done | bytes 139296 | tf_op jit(solution)/shard_map/ppermute | solution.py:260
  11.1 2.3 %collective-permute-start.5 = (bf16[2,192,128]{2,1,0:T(8,128)(2,1)S(1)}, bf16[2,192,128]{2,1,0:T(8,128)(2,1)S(1)}, u32[]{:S(2)}, u32[]{:S(2)}) collective-permute-start(bf16[2,192,128]{2,1,0:T(8,128)(2,1)S(1)} %get-tuple-element.26), channel_id=1, source_target_pairs={{0,4},{1,5},{2,6},{3,7},{4,0},{5,1},{6,2},{7,3},{8,12},{9,13},{10,... | collective-permute-start | bytes 294920 | tf_op jit(solution)/shard_map/ppermute | solution.py:260
  13.5 1.0 %collective-permute-start.6 = (bf16[2,192,128]{2,1,0:T(8,128)(2,1)S(1)}, bf16[2,192,128]{2,1,0:T(8,128)(2,1)S(1)}, u32[]{:S(2)}, u32[]{:S(2)}) collective-permute-start(bf16[2,192,128]{2,1,0:T(8,128)(2,1)S(1)} %get-tuple-element.27), channel_id=1, source_target_pairs={{0,6},{1,7},{2,4},{3,5},{4,2},{5,3},{6,0},{7,1},{8,14},{9,15},{10,... | collective-permute-start | bytes 294920 | tf_op jit(solution)/shard_map/ppermute | solution.py:260
  14.5 0.5 %collective-permute-start.7 = (bf16[2,192,128]{2,1,0:T(8,128)(2,1)S(1)}, bf16[2,192,128]{2,1,0:T(8,128)(2,1)S(1)}, u32[]{:S(2)}, u32[]{:S(2)}) collective-permute-start(bf16[2,192,128]{2,1,0:T(8,128)(2,1)S(1)} %get-tuple-element.28), channel_id=1, source_target_pairs={{0,2},{1,3},{2,0},{3,1},{4,6},{5,7},{6,4},{7,5},{8,10},{9,11},{10,... | collective-permute-start | bytes 294920 | tf_op jit(solution)/shard_map/ppermute | solution.py:260
  15.0 0.2 collective-permute-done.3.refs_4_.refs_3_
  15.2 0.2 sum_offsets.4.refs_0_
  15.5 0.5 %collective-permute-done.2.refs_3_.refs_1_ = bf16[2,272,128]{2,1,0:T(8,128)(2,1)S(1)} collective-permute-done((bf16[2,272,128]{2,1,0:T(8,128)(2,1)S(1)}, bf16[2,272,128]{2,1,0:T(8,128)(2,1)S(1)}, u32[]{:S(2)}, u32[]{:S(2)}) %collective-permute-start.2) | collective-permute-done | bytes 139296 | tf_op jit(solution)/shard_map/ppermute | solution.py:260
  15.9 0.3 sum_offsets.5
  16.3 2.7 %collective-permute-start.9 = (f16[480,128]{1,0:T(8,128)(2,1)S(1)}, f16[480,128]{1,0:T(8,128)(2,1)S(1)}, u32[]{:S(2)}, u32[]{:S(2)}) collective-permute-start(f16[480,128]{1,0:T(8,128)(2,1)S(1)} %convert_element_type.14), channel_id=1, source_target_pairs={{0,8},{1,9},{2,10},{3,11},{4,12},{5,13},{6,14},{7,15},{8,0},{9,1},... | collective-permute-start | bytes 368648 | tf_op jit(solution)/shard_map/ppermute | solution.py:260
  18.9 0.0 collective-permute-done.5.refs_7_
  18.9 1.5 %collective-permute-done.6.refs_8_ = bf16[2,192,128]{2,1,0:T(8,128)(2,1)S(1)} collective-permute-done((bf16[2,192,128]{2,1,0:T(8,128)(2,1)S(1)}, bf16[2,192,128]{2,1,0:T(8,128)(2,1)S(1)}, u32[]{:S(2)}, u32[]{:S(2)}) %collective-permute-start.6) | collective-permute-done | bytes 98336 | tf_op jit(solution)/shard_map/ppermute | solution.py:260
  20.5 0.0 collective-permute-done.7.refs_9_
  20.5 0.4 %sum_offsets.3 = (f32[768,128]{1,0:T(8,128)S(1)}, f32[400,128]{1,0:T(8,128)S(1)}) custom-call(bf16[4,272,128]{2,1,0:T(8,128)(2,1)S(1)} %get-tuple-element.19.keep_ref.refs_0_, bf16[4,272,128]{2,1,0:T(8,128)(2,1)S(1)} %collective-permute-done.got_ref.refs_1_, bf16[2,272,128]{2,1,0:T(8,128)(2,1)S(1)} %collective-permute-done.1.refs_0_.refs_2_, ...), custom_call_target="tpu_custom_call" | custom-call | tf_op jit(solution)/shard_map/sum_offsets/pallas_call | solution.py:309
  20.8 2.5 %collective-permute-start.8 = (f16[400,128]{1,0:T(8,128)(2,1)S(1)}, f16[400,128]{1,0:T(8,128)(2,1)S(1)}, u32[]{:S(2)}, u32[]{:S(2)}) collective-permute-start(f16[400,128]{1,0:T(8,128)(2,1)S(1)} %convert_element_type.12), channel_id=1, source_target_pairs={{0,8},{1,9},{2,10},{3,11},{4,12},{5,13},{6,14},{7,15},{8,0},{9,1},... | collective-permute-start | bytes 307208 | tf_op jit(solution)/shard_map/ppermute | solution.py:260
  23.4 1.7 %collective-permute-done.9 = f16[480,128]{1,0:T(8,128)(2,1)S(1)} collective-permute-done((f16[480,128]{1,0:T(8,128)(2,1)S(1)}, f16[480,128]{1,0:T(8,128)(2,1)S(1)}, u32[]{:S(2)}, u32[]{:S(2)}) %collective-permute-start.9) | collective-permute-done | bytes 122912 | tf_op jit(solution)/shard_map/ppermute | solution.py:260
  25.1 0.9 %join_offsets.2.refs_0_ = f32[7,128,128]{2,1,0:T(8,128)} custom-call(f32[928,128]{1,0:T(8,128)S(1)} %get-tuple-element.31.sums_ref, f32[480,128]{1,0:T(8,128)S(1)} %convert_element_type.15.far_ref), custom_call_target="tpu_custom_call" | custom-call | tf_op jit(solution)/shard_map/join_offsets/pallas_call | solution.py:324
  26.1 1.8 %collective-permute-done.8 = f16[400,128]{1,0:T(8,128)(2,1)S(1)} collective-permute-done((f16[400,128]{1,0:T(8,128)(2,1)S(1)}, f16[400,128]{1,0:T(8,128)(2,1)S(1)}, u32[]{:S(2)}, u32[]{:S(2)}) %collective-permute-start.8) | collective-permute-done | bytes 102432 | tf_op jit(solution)/shard_map/ppermute | solution.py:260
  27.9 0.7 %join_offsets.3 = f32[7,128,128]{2,1,0:T(8,128)} custom-call(f32[768,128]{1,0:T(8,128)S(1)} %get-tuple-element.29.sums_ref, f32[400,128]{1,0:T(8,128)S(1)} %convert_element_type.13.far_ref, f32[7,128,128]{2,1,0:T(8,128)} %join_offsets.2.refs_0_), custom_call_target="tpu_custom_call", output_to_operand_aliasing={{}: (2, {})} | custom-call | tf_op jit(solution)/shard_map/join_offsets/pallas_call | solution.py:324
  (6 shorter events, 0.1 us)
Async XLA Ops:
  2.1 1.7 %collective-permute-start = (bf16[4,272,128]{2,1,0:T(8,128)(2,1)S(1)}, bf16[4,272,128]{2,1,0:T(8,128)(2,1)S(1)}, u32[]{:S(2)}, u32[]{:S(2)}) collective-permute-start(bf16[4,272,128]{2,1,0:T(8,128)(2,1)S(1)} %get-tuple-element.20), channel_id=1, source_target_pairs={{0,1},{1,0},{2,3},{3,2},{4,5},{5,4},{6,7},{7,6},{8,9},{9,8},{10,11... | collective-permute-start | bytes 835592 | tf_op jit(solution)/shard_map/ppermute | solution.py:260
  2.6 5.8 %collective-permute-start.4 = (bf16[4,192,128]{2,1,0:T(8,128)(2,1)S(1)}, bf16[4,192,128]{2,1,0:T(8,128)(2,1)S(1)}, u32[]{:S(2)}, u32[]{:S(2)}) collective-permute-start(bf16[4,192,128]{2,1,0:T(8,128)(2,1)S(1)} %get-tuple-element.25), channel_id=1, source_target_pairs={{0,1},{1,0},{2,3},{3,2},{4,5},{5,4},{6,7},{7,6},{8,9},{9,8},{10,11... | collective-permute-start | bytes 589832 | tf_op jit(solution)/shard_map/ppermute | solution.py:260
  3.9 7.3 %collective-permute-start.1 = (bf16[2,272,128]{2,1,0:T(8,128)(2,1)S(1)}, bf16[2,272,128]{2,1,0:T(8,128)(2,1)S(1)}, u32[]{:S(2)}, u32[]{:S(2)}) collective-permute-start(bf16[2,272,128]{2,1,0:T(8,128)(2,1)S(1)} %get-tuple-element.21), channel_id=1, source_target_pairs={{0,4},{1,5},{2,6},{3,7},{4,0},{5,1},{6,2},{7,3},{8,12},{9,13},{10,... | collective-permute-start | bytes 417800 | tf_op jit(solution)/shard_map/ppermute | solution.py:260
  6.9 8.4 %collective-permute-start.3 = (bf16[2,272,128]{2,1,0:T(8,128)(2,1)S(1)}, bf16[2,272,128]{2,1,0:T(8,128)(2,1)S(1)}, u32[]{:S(2)}, u32[]{:S(2)}) collective-permute-start(bf16[2,272,128]{2,1,0:T(8,128)(2,1)S(1)} %get-tuple-element.23), channel_id=1, source_target_pairs={{0,2},{1,3},{2,0},{3,1},{4,6},{5,7},{6,4},{7,5},{8,10},{9,11},{10,... | collective-permute-start | bytes 417800 | tf_op jit(solution)/shard_map/ppermute | solution.py:260
  8.4 7.5 %collective-permute-start.2 = (bf16[2,272,128]{2,1,0:T(8,128)(2,1)S(1)}, bf16[2,272,128]{2,1,0:T(8,128)(2,1)S(1)}, u32[]{:S(2)}, u32[]{:S(2)}) collective-permute-start(bf16[2,272,128]{2,1,0:T(8,128)(2,1)S(1)} %get-tuple-element.22), channel_id=1, source_target_pairs={{0,6},{1,7},{2,4},{3,5},{4,2},{5,3},{6,0},{7,1},{8,14},{9,15},{10,... | collective-permute-start | bytes 417800 | tf_op jit(solution)/shard_map/ppermute | solution.py:260
  11.1 7.8 %collective-permute-start.5 = (bf16[2,192,128]{2,1,0:T(8,128)(2,1)S(1)}, bf16[2,192,128]{2,1,0:T(8,128)(2,1)S(1)}, u32[]{:S(2)}, u32[]{:S(2)}) collective-permute-start(bf16[2,192,128]{2,1,0:T(8,128)(2,1)S(1)} %get-tuple-element.26), channel_id=1, source_target_pairs={{0,4},{1,5},{2,6},{3,7},{4,0},{5,1},{6,2},{7,3},{8,12},{9,13},{10,... | collective-permute-start | bytes 294920 | tf_op jit(solution)/shard_map/ppermute | solution.py:260
  13.5 7.0 %collective-permute-start.6 = (bf16[2,192,128]{2,1,0:T(8,128)(2,1)S(1)}, bf16[2,192,128]{2,1,0:T(8,128)(2,1)S(1)}, u32[]{:S(2)}, u32[]{:S(2)}) collective-permute-start(bf16[2,192,128]{2,1,0:T(8,128)(2,1)S(1)} %get-tuple-element.27), channel_id=1, source_target_pairs={{0,6},{1,7},{2,4},{3,5},{4,2},{5,3},{6,0},{7,1},{8,14},{9,15},{10,... | collective-permute-start | bytes 294920 | tf_op jit(solution)/shard_map/ppermute | solution.py:260
  14.5 5.9 %collective-permute-start.7 = (bf16[2,192,128]{2,1,0:T(8,128)(2,1)S(1)}, bf16[2,192,128]{2,1,0:T(8,128)(2,1)S(1)}, u32[]{:S(2)}, u32[]{:S(2)}) collective-permute-start(bf16[2,192,128]{2,1,0:T(8,128)(2,1)S(1)} %get-tuple-element.28), channel_id=1, source_target_pairs={{0,2},{1,3},{2,0},{3,1},{4,6},{5,7},{6,4},{7,5},{8,10},{9,11},{10,... | collective-permute-start | bytes 294920 | tf_op jit(solution)/shard_map/ppermute | solution.py:260
  16.3 8.9 %collective-permute-start.9 = (f16[480,128]{1,0:T(8,128)(2,1)S(1)}, f16[480,128]{1,0:T(8,128)(2,1)S(1)}, u32[]{:S(2)}, u32[]{:S(2)}) collective-permute-start(f16[480,128]{1,0:T(8,128)(2,1)S(1)} %convert_element_type.14), channel_id=1, source_target_pairs={{0,8},{1,9},{2,10},{3,11},{4,12},{5,13},{6,14},{7,15},{8,0},{9,1},... | collective-permute-start | bytes 368648 | tf_op jit(solution)/shard_map/ppermute | solution.py:260
  20.8 7.1 %collective-permute-start.8 = (f16[400,128]{1,0:T(8,128)(2,1)S(1)}, f16[400,128]{1,0:T(8,128)(2,1)S(1)}, u32[]{:S(2)}, u32[]{:S(2)}) collective-permute-start(f16[400,128]{1,0:T(8,128)(2,1)S(1)} %convert_element_type.12), channel_id=1, source_target_pairs={{0,8},{1,9},{2,10},{3,11},{4,12},{5,13},{6,14},{7,15},{8,0},{9,1},... | collective-permute-start | bytes 307208 | tf_op jit(solution)/shard_map/ppermute | solution.py:260

commit v8 on v3

--- a/solution.py
+++ b/solution.py
@@ -92,11 +92,12 @@
         for part in range(COPIES):
             cols_copy(region, part).start()
     groups_copy.wait()
-    packed = packed_rows(width)
-
-    def add_region(region, carry):
+    for region in range(region_count):
         for part in range(COPIES):
             cols_copy(region, part).wait()
+    packed = packed_rows(width)
+
+    def add_region(region, carry):
         cols = cols_ref[region]
         depth = cols.shape[1] // PRODUCTS
         grams = [
@@ -142,20 +143,27 @@
             send_ref[pair] = rows_ref[CORES * pair + at % CORES, first:last]
 
 
+def order_of(pair_count):
+    def key(pair):
+        return (-pair.bit_length(), pair.bit_count(), -pair)
+
+    return sorted(range(1, pair_count), key=key)
+
+
 def sum_kernel(chunk, slot_count, *refs):
-    arrays, (sums_ref, scaled_ref) = refs[:-2], refs[-2:]
-    width = sums_ref.shape[1]
+    width = refs[-1].shape[1]
     half, packed = width // 2, packed_rows(width)
     count = sum_rows(chunk, width, slot_count)
     base = packed if chunk == 0 else 0
+    *arrays, sums_ref, scaled_ref = refs
     sums_ref[...] = jnp.zeros_like(sums_ref)
 
     def units(arrays):
-        return [(arrays[0], 0), (arrays[1], 0)] + [
-            (x, core) for x in arrays[2:] for core in range(CORES)
+        return [(ref, 0) for ref in arrays[:CORES]] + [
+            (ref, core) for ref in arrays[CORES:] for core in range(CORES)
         ]
 
-    array_count = len(arrays) if chunk == 0 else len(arrays) // 2
+    array_count = len(arrays) // (chunk + 1)
     tags = [
         jnp.max(ref[at, half:packed].astype(jnp.float32)[TILE - 1 :, width - 1 :]).astype(
             jnp.int32
@@ -281,20 +289,19 @@
             compiler_params=params,
             name="merge_units",
         )(*gots, *tagged[CORES : CORES + chunk])
-        for pair in sorted(range(1, pair_count), key=lambda p: (p.bit_count(), -p)):
+        for pair in order_of(pair_count):
             gots.append(permute(merged[pair - 1], CORES * pair))
         tagged = tagged or gots
         count = sum_rows(chunk, width, slot_count)
+        shape = jax.ShapeDtypeStruct((2 * count, width), jnp.float32)
+        scaled = jax.ShapeDtypeStruct((count + TILE, width), jnp.float32)
         sums, scaled = pl.pallas_call(
             functools.partial(sum_kernel, chunk, slot_count),
-            out_shape=(
-                jax.ShapeDtypeStruct((2 * count, width), jnp.float32),
-                jax.ShapeDtypeStruct((count + TILE, width), jnp.float32),
-            ),
+            out_shape=(shape, scaled),
             cost_estimate=light,
             compiler_params=params,
             name="sum_offsets",
-        )(*(tagged if chunk == 0 else tagged + gots))
+        )(*(tagged if chunk else ()), *gots)
         far = permute(scaled.astype(jnp.float16), half)
         pieces.append((sums, far.astype(jnp.float32)))
 

time: 28.9 us -> 31.5 us (1.090)
  waiting for transfers between devices: 10.2 us -> 13.7 us
  starting transfers between devices: 13.7 us -> 13 us
    ppermute x10, waiting for transfers between devices: 10.2 us -> 13.7 us  [permute(): return lax.ppermute(values, 'group', pairs)]
    ppermute x10, starting transfers between devices: 13.7 us -> 13 us  [permute(): return lax.ppermute(values, 'group', pairs)]
  transfers between devices with their start and end apart: 10 -> 10, of which waited for: 7 -> 6; matrix products, arithmetic and copies ran while one was open for 0% -> 0% of each run, Pallas kernels for 6% -> 5%
where the time goes in v8:
time: 31.5 us; the launch traced here: 31.4 us
  waiting for transfers between devices  13.7 us (43%)
  starting transfers between devices  13 us (41%)
  Pallas kernels  4.57 us (15%)
    ppermute x10, waiting for transfers between devices, permute(): return lax.ppermute(values, 'group', pairs)  13.7 us
    ppermute x10, starting transfers between devices, permute(): return lax.ppermute(values, 'group', pairs)  13 us
    pallas_call x1, Pallas kernels, shards(): pl.pallas_call(functools.partial(gram_kernel, total_groups, half), in_spe...  2.12 us
    pallas_call x2, Pallas kernels, shards(): pl.pallas_call(functools.partial(join_kernel, chunk, slot_count), in_spec...  1.65 us
    pallas_call x2, Pallas kernels, shards(): pl.pallas_call(functools.partial(sum_kernel, chunk, slot_count), out_shap...  0.75 us
  transfers between devices with their start and end apart: 10, of which 6 were waited for; matrix products, arithmetic and copies ran while one was open for 0% of the time, Pallas kernels for 5%

profile of v8, /device:TPU:0, one launch (start us, length us, event | category | flops | bytes accessed | tf_op | source)
XLA Modules:
  0.0 31.4 jit_solution(14895302722527300450)
XLA Ops:
  0.0 2.1 %gram_rows.1 = (bf16[4,272,128]{2,1,0:T(8,128)(2,1)S(1)}, bf16[4,272,128]{2,1,0:T(8,128)(2,1)S(1)}, bf16[4,192,128]{2,1,0:T(8,128)(2,1)S(1)}, bf16[4,192,128]{2,1,0:T(8,128)(2,1)S(1)}) custom-call(s32[2,4]{1,0:T(2,128)} %groups_hbm.1, bf16[2,512,512]{2,1,0:T(8,128)(2,1)} %cols_hbm.1), custom_call_target="tpu_custom_call" | custom-call | tf_op jit(solution)/shard_map/gram_rows/pallas_call | solution.py:261
  2.1 0.5 %collective-permute-start = (bf16[4,272,128]{2,1,0:T(8,128)(2,1)S(1)}, bf16[4,272,128]{2,1,0:T(8,128)(2,1)S(1)}, u32[]{:S(2)}, u32[]{:S(2)}) collective-permute-start(bf16[4,272,128]{2,1,0:T(8,128)(2,1)S(1)} %get-tuple-element.20), channel_id=1, source_target_pairs={{0,1},{1,0},{2,3},{3,2},{4,5},{5,4},{6,7},{7,6},{8,9},{9,8},{10,11... | collective-permute-start | bytes 835592 | tf_op jit(solution)/shard_map/ppermute | solution.py:255
  2.6 0.1 collective-permute-start.4
  2.7 1.1 %collective-permute-done.got_ref.refs_1_ = bf16[4,272,128]{2,1,0:T(8,128)(2,1)S(1)} collective-permute-done((bf16[4,272,128]{2,1,0:T(8,128)(2,1)S(1)}, bf16[4,272,128]{2,1,0:T(8,128)(2,1)S(1)}, u32[]{:S(2)}, u32[]{:S(2)}) %collective-permute-start) | collective-permute-done | bytes 278560 | tf_op jit(solution)/shard_map/ppermute | solution.py:255
  3.9 3.0 %collective-permute-start.1 = (bf16[2,272,128]{2,1,0:T(8,128)(2,1)S(1)}, bf16[2,272,128]{2,1,0:T(8,128)(2,1)S(1)}, u32[]{:S(2)}, u32[]{:S(2)}) collective-permute-start(bf16[2,272,128]{2,1,0:T(8,128)(2,1)S(1)} %get-tuple-element.21), channel_id=1, source_target_pairs={{0,4},{1,5},{2,6},{3,7},{4,0},{5,1},{6,2},{7,3},{8,12},{9,13},{10,... | collective-permute-start | bytes 417800 | tf_op jit(solution)/shard_map/ppermute | solution.py:255
  6.9 1.4 %collective-permute-start.2 = (bf16[2,272,128]{2,1,0:T(8,128)(2,1)S(1)}, bf16[2,272,128]{2,1,0:T(8,128)(2,1)S(1)}, u32[]{:S(2)}, u32[]{:S(2)}) collective-permute-start(bf16[2,272,128]{2,1,0:T(8,128)(2,1)S(1)} %get-tuple-element.22), channel_id=1, source_target_pairs={{0,6},{1,7},{2,4},{3,5},{4,2},{5,3},{6,0},{7,1},{8,14},{9,15},{10,... | collective-permute-start | bytes 417800 | tf_op jit(solution)/shard_map/ppermute | solution.py:255
  8.3 0.1 collective-permute-start.3
  8.4 0.0 collective-permute-done.4.got_ref.refs_6_
  8.4 2.9 %collective-permute-done.1.refs_0_.refs_2_ = bf16[2,272,128]{2,1,0:T(8,128)(2,1)S(1)} collective-permute-done((bf16[2,272,128]{2,1,0:T(8,128)(2,1)S(1)}, bf16[2,272,128]{2,1,0:T(8,128)(2,1)S(1)}, u32[]{:S(2)}, u32[]{:S(2)}) %collective-permute-start.1) | collective-permute-done | bytes 139296 | tf_op jit(solution)/shard_map/ppermute | solution.py:255
  11.4 2.1 %collective-permute-start.5 = (bf16[2,192,128]{2,1,0:T(8,128)(2,1)S(1)}, bf16[2,192,128]{2,1,0:T(8,128)(2,1)S(1)}, u32[]{:S(2)}, u32[]{:S(2)}) collective-permute-start(bf16[2,192,128]{2,1,0:T(8,128)(2,1)S(1)} %get-tuple-element.26), channel_id=1, source_target_pairs={{0,4},{1,5},{2,6},{3,7},{4,0},{5,1},{6,2},{7,3},{8,12},{9,13},{10,... | collective-permute-start | bytes 294920 | tf_op jit(solution)/shard_map/ppermute | solution.py:255
  13.5 1.4 %collective-permute-start.6 = (bf16[2,192,128]{2,1,0:T(8,128)(2,1)S(1)}, bf16[2,192,128]{2,1,0:T(8,128)(2,1)S(1)}, u32[]{:S(2)}, u32[]{:S(2)}) collective-permute-start(bf16[2,192,128]{2,1,0:T(8,128)(2,1)S(1)} %get-tuple-element.27), channel_id=1, source_target_pairs={{0,6},{1,7},{2,4},{3,5},{4,2},{5,3},{6,0},{7,1},{8,14},{9,15},{10,... | collective-permute-start | bytes 294920 | tf_op jit(solution)/shard_map/ppermute | solution.py:255
  14.9 0.1 collective-permute-start.7
  15.0 0.8 %collective-permute-done.2.refs_3_ = bf16[2,272,128]{2,1,0:T(8,128)(2,1)S(1)} collective-permute-done((bf16[2,272,128]{2,1,0:T(8,128)(2,1)S(1)}, bf16[2,272,128]{2,1,0:T(8,128)(2,1)S(1)}, u32[]{:S(2)}, u32[]{:S(2)}) %collective-permute-start.2) | collective-permute-done | bytes 139296 | tf_op jit(solution)/shard_map/ppermute | solution.py:255
  15.8 2.9 %collective-permute-done.3.refs_4_ = bf16[2,272,128]{2,1,0:T(8,128)(2,1)S(1)} collective-permute-done((bf16[2,272,128]{2,1,0:T(8,128)(2,1)S(1)}, bf16[2,272,128]{2,1,0:T(8,128)(2,1)S(1)}, u32[]{:S(2)}, u32[]{:S(2)}) %collective-permute-start.3) | collective-permute-done | bytes 139296 | tf_op jit(solution)/shard_map/ppermute | solution.py:255
  18.7 0.4 %sum_offsets.3 = (f32[928,128]{1,0:T(8,128)S(1)}, f32[480,128]{1,0:T(8,128)S(1)}) custom-call(bf16[4,272,128]{2,1,0:T(8,128)(2,1)S(1)} %get-tuple-element.19.keep_ref.refs_0_, bf16[4,272,128]{2,1,0:T(8,128)(2,1)S(1)} %collective-permute-done.got_ref.refs_1_, bf16[2,272,128]{2,1,0:T(8,128)(2,1)S(1)} %collective-permute-done.1.refs_0_.refs_2_, ...), custom_call_target="tpu_custom_call" | custom-call | tf_op jit(solution)/shard_map/sum_offsets/pallas_call | solution.py:298
  19.1 2.2 %collective-permute-start.9 = (f16[480,128]{1,0:T(8,128)(2,1)S(1)}, f16[480,128]{1,0:T(8,128)(2,1)S(1)}, u32[]{:S(2)}, u32[]{:S(2)}) collective-permute-start(f16[480,128]{1,0:T(8,128)(2,1)S(1)} %convert_element_type.14), channel_id=1, source_target_pairs={{0,8},{1,9},{2,10},{3,11},{4,12},{5,13},{6,14},{7,15},{8,0},{9,1},... | collective-permute-start | bytes 368648 | tf_op jit(solution)/shard_map/ppermute | solution.py:255
  21.3 0.0 collective-permute-done.5.refs_7_
  21.3 0.0 collective-permute-done.6.refs_8_
  21.3 0.0 collective-permute-done.7.refs_9_
  21.3 0.4 %sum_offsets.2 = (f32[768,128]{1,0:T(8,128)S(1)}, f32[400,128]{1,0:T(8,128)S(1)}) custom-call(bf16[4,272,128]{2,1,0:T(8,128)(2,1)S(1)} %get-tuple-element.19.keep_ref.refs_0_, bf16[4,272,128]{2,1,0:T(8,128)(2,1)S(1)} %collective-permute-done.got_ref.refs_1_, bf16[2,272,128]{2,1,0:T(8,128)(2,1)S(1)} %collective-permute-done.1.refs_0_.refs_2_, ...), custom_call_target="tpu_custom_call" | custom-call | tf_op jit(solution)/shard_map/sum_offsets/pallas_call | solution.py:298
  21.7 2.0 %collective-permute-start.8 = (f16[400,128]{1,0:T(8,128)(2,1)S(1)}, f16[400,128]{1,0:T(8,128)(2,1)S(1)}, u32[]{:S(2)}, u32[]{:S(2)}) collective-permute-start(f16[400,128]{1,0:T(8,128)(2,1)S(1)} %convert_element_type.12), channel_id=1, source_target_pairs={{0,8},{1,9},{2,10},{3,11},{4,12},{5,13},{6,14},{7,15},{8,0},{9,1},... | collective-permute-start | bytes 307208 | tf_op jit(solution)/shard_map/ppermute | solution.py:255
  23.7 5.7 %collective-permute-done.9 = f16[480,128]{1,0:T(8,128)(2,1)S(1)} collective-permute-done((f16[480,128]{1,0:T(8,128)(2,1)S(1)}, f16[480,128]{1,0:T(8,128)(2,1)S(1)}, u32[]{:S(2)}, u32[]{:S(2)}) %collective-permute-start.9) | collective-permute-done | bytes 122912 | tf_op jit(solution)/shard_map/ppermute | solution.py:255
  29.4 0.9 %join_offsets.2.refs_0_ = f32[7,128,128]{2,1,0:T(8,128)} custom-call(f32[928,128]{1,0:T(8,128)S(1)} %get-tuple-element.31.sums_ref, f32[480,128]{1,0:T(8,128)S(1)} %convert_element_type.15.far_ref), custom_call_target="tpu_custom_call" | custom-call | tf_op jit(solution)/shard_map/join_offsets/pallas_call | solution.py:312
  30.4 0.3 collective-permute-done.8
  30.7 0.7 %join_offsets.3 = f32[7,128,128]{2,1,0:T(8,128)} custom-call(f32[768,128]{1,0:T(8,128)S(1)} %get-tuple-element.29.sums_ref, f32[400,128]{1,0:T(8,128)S(1)} %convert_element_type.13.far_ref, f32[7,128,128]{2,1,0:T(8,128)} %join_offsets.2.refs_0_), custom_call_target="tpu_custom_call", output_to_operand_aliasing={{}: (2, {})} | custom-call | tf_op jit(solution)/shard_map/join_offsets/pallas_call | solution.py:312
  (6 shorter events, 0.1 us)
Async XLA Ops:
  2.1 1.7 %collective-permute-start = (bf16[4,272,128]{2,1,0:T(8,128)(2,1)S(1)}, bf16[4,272,128]{2,1,0:T(8,128)(2,1)S(1)}, u32[]{:S(2)}, u32[]{:S(2)}) collective-permute-start(bf16[4,272,128]{2,1,0:T(8,128)(2,1)S(1)} %get-tuple-element.20), channel_id=1, source_target_pairs={{0,1},{1,0},{2,3},{3,2},{4,5},{5,4},{6,7},{7,6},{8,9},{9,8},{10,11... | collective-permute-start | bytes 835592 | tf_op jit(solution)/shard_map/ppermute | solution.py:255
  2.6 5.8 %collective-permute-start.4 = (bf16[4,192,128]{2,1,0:T(8,128)(2,1)S(1)}, bf16[4,192,128]{2,1,0:T(8,128)(2,1)S(1)}, u32[]{:S(2)}, u32[]{:S(2)}) collective-permute-start(bf16[4,192,128]{2,1,0:T(8,128)(2,1)S(1)} %get-tuple-element.25), channel_id=1, source_target_pairs={{0,1},{1,0},{2,3},{3,2},{4,5},{5,4},{6,7},{7,6},{8,9},{9,8},{10,11... | collective-permute-start | bytes 589832 | tf_op jit(solution)/shard_map/ppermute | solution.py:255
  3.9 7.5 %collective-permute-start.1 = (bf16[2,272,128]{2,1,0:T(8,128)(2,1)S(1)}, bf16[2,272,128]{2,1,0:T(8,128)(2,1)S(1)}, u32[]{:S(2)}, u32[]{:S(2)}) collective-permute-start(bf16[2,272,128]{2,1,0:T(8,128)(2,1)S(1)} %get-tuple-element.21), channel_id=1, source_target_pairs={{0,4},{1,5},{2,6},{3,7},{4,0},{5,1},{6,2},{7,3},{8,12},{9,13},{10,... | collective-permute-start | bytes 417800 | tf_op jit(solution)/shard_map/ppermute | solution.py:255
  6.9 8.9 %collective-permute-start.2 = (bf16[2,272,128]{2,1,0:T(8,128)(2,1)S(1)}, bf16[2,272,128]{2,1,0:T(8,128)(2,1)S(1)}, u32[]{:S(2)}, u32[]{:S(2)}) collective-permute-start(bf16[2,272,128]{2,1,0:T(8,128)(2,1)S(1)} %get-tuple-element.22), channel_id=1, source_target_pairs={{0,6},{1,7},{2,4},{3,5},{4,2},{5,3},{6,0},{7,1},{8,14},{9,15},{10,... | collective-permute-start | bytes 417800 | tf_op jit(solution)/shard_map/ppermute | solution.py:255
  8.3 10.4 %collective-permute-start.3 = (bf16[2,272,128]{2,1,0:T(8,128)(2,1)S(1)}, bf16[2,272,128]{2,1,0:T(8,128)(2,1)S(1)}, u32[]{:S(2)}, u32[]{:S(2)}) collective-permute-start(bf16[2,272,128]{2,1,0:T(8,128)(2,1)S(1)} %get-tuple-element.23), channel_id=1, source_target_pairs={{0,2},{1,3},{2,0},{3,1},{4,6},{5,7},{6,4},{7,5},{8,10},{9,11},{10,... | collective-permute-start | bytes 417800 | tf_op jit(solution)/shard_map/ppermute | solution.py:255
  11.4 9.9 %collective-permute-start.5 = (bf16[2,192,128]{2,1,0:T(8,128)(2,1)S(1)}, bf16[2,192,128]{2,1,0:T(8,128)(2,1)S(1)}, u32[]{:S(2)}, u32[]{:S(2)}) collective-permute-start(bf16[2,192,128]{2,1,0:T(8,128)(2,1)S(1)} %get-tuple-element.26), channel_id=1, source_target_pairs={{0,4},{1,5},{2,6},{3,7},{4,0},{5,1},{6,2},{7,3},{8,12},{9,13},{10,... | collective-permute-start | bytes 294920 | tf_op jit(solution)/shard_map/ppermute | solution.py:255
  13.5 7.8 %collective-permute-start.6 = (bf16[2,192,128]{2,1,0:T(8,128)(2,1)S(1)}, bf16[2,192,128]{2,1,0:T(8,128)(2,1)S(1)}, u32[]{:S(2)}, u32[]{:S(2)}) collective-permute-start(bf16[2,192,128]{2,1,0:T(8,128)(2,1)S(1)} %get-tuple-element.27), channel_id=1, source_target_pairs={{0,6},{1,7},{2,4},{3,5},{4,2},{5,3},{6,0},{7,1},{8,14},{9,15},{10,... | collective-permute-start | bytes 294920 | tf_op jit(solution)/shard_map/ppermute | solution.py:255
  14.9 6.4 %collective-permute-start.7 = (bf16[2,192,128]{2,1,0:T(8,128)(2,1)S(1)}, bf16[2,192,128]{2,1,0:T(8,128)(2,1)S(1)}, u32[]{:S(2)}, u32[]{:S(2)}) collective-permute-start(bf16[2,192,128]{2,1,0:T(8,128)(2,1)S(1)} %get-tuple-element.28), channel_id=1, source_target_pairs={{0,2},{1,3},{2,0},{3,1},{4,6},{5,7},{6,4},{7,5},{8,10},{9,11},{10,... | collective-permute-start | bytes 294920 | tf_op jit(solution)/shard_map/ppermute | solution.py:255
  19.1 10.3 %collective-permute-start.9 = (f16[480,128]{1,0:T(8,128)(2,1)S(1)}, f16[480,128]{1,0:T(8,128)(2,1)S(1)}, u32[]{:S(2)}, u32[]{:S(2)}) collective-permute-start(f16[480,128]{1,0:T(8,128)(2,1)S(1)} %convert_element_type.14), channel_id=1, source_target_pairs={{0,8},{1,9},{2,10},{3,11},{4,12},{5,13},{6,14},{7,15},{8,0},{9,1},... | collective-permute-start | bytes 368648 | tf_op jit(solution)/shard_map/ppermute | solution.py:255
  21.7 8.9 %collective-permute-start.8 = (f16[400,128]{1,0:T(8,128)(2,1)S(1)}, f16[400,128]{1,0:T(8,128)(2,1)S(1)}, u32[]{:S(2)}, u32[]{:S(2)}) collective-permute-start(f16[400,128]{1,0:T(8,128)(2,1)S(1)} %convert_element_type.12), channel_id=1, source_target_pairs={{0,8},{1,9},{2,10},{3,11},{4,12},{5,13},{6,14},{7,15},{8,0},{9,1},... | collective-permute-start | bytes 307208 | tf_op jit(solution)/shard_map/ppermute | solution.py:255

commit v9 on v7

--- a/solution.py
+++ b/solution.py
@@ -196,7 +196,10 @@
     largest = jnp.max(jnp.broadcast_to(tops, (8, width)), axis=1, keepdims=True)
     power = jnp.floor(jnp.log2(jnp.maximum(largest, 2.0**LEAST_POWER))) - TOP_POWER
     scaled_ref[:count] = sums_ref[count:] * jnp.exp2(-power)[0:1]
-    scaled_ref[count:] = jnp.broadcast_to(power[0:1], (TILE, width))
+    if chunk == 0:
+        scaled_ref[half:packed] = jnp.where(col < half, scaled_ref[half:packed], power[0:1])
+    else:
+        scaled_ref[count:] = jnp.broadcast_to(power[0:1], (TILE, width))
 
 
 def merge_kernel(keep_ref, got_ref, *refs):
@@ -210,8 +213,8 @@
     out_hbm, joined_ref, sems = refs[-3:]
     width = joined_ref.shape[2]
     half, packed = width // 2, packed_rows(width)
-    count = sum_rows(chunk, width, slot_count)
-    factor = jnp.exp2(far_ref[count : count + 1])
+    at = half if chunk == 0 else sum_rows(chunk, width, slot_count)
+    factor = jnp.exp2(far_ref[at : at + 8][:1, width - 1 :])
     copies = []
 
     def joined(first, size):
@@ -299,7 +302,7 @@
         tagged = tagged or gots
         count = sum_rows(chunk, width, slot_count)
         shape = jax.ShapeDtypeStruct((2 * count, width), jnp.float32)
-        scaled = jax.ShapeDtypeStruct((count + TILE, width), jnp.float32)
+        scaled = jax.ShapeDtypeStruct((count + TILE * chunk, width), jnp.float32)
         by_chip = dict(zip(order_of(0, pair_count), tagged[CORES:]))
         tags = tagged[:CORES] + [by_chip[pair] for pair in order_of(chunk, pair_count)]
         sums = ()

time: 28.8 us -> 28.8 us (level)
  transfers between devices with their start and end apart: 10 -> 10, of which waited for: 7 -> 7; matrix products, arithmetic and copies ran while one was open for 0% -> 0% of each run, Pallas kernels for 6% -> 7%
where the time goes in v9:
time: 28.8 us; the launch traced here: 28.6 us
  starting transfers between devices  14.2 us (49%)
  waiting for transfers between devices  9.4 us (33%)
  Pallas kernels  4.87 us (17%)
    ppermute x10, starting transfers between devices, permute(): return lax.ppermute(values, 'group', pairs)  14.2 us
    ppermute x10, waiting for transfers between devices, permute(): return lax.ppermute(values, 'group', pairs)  9.4 us
    pallas_call x1, Pallas kernels, shards(): pl.pallas_call(functools.partial(gram_kernel, total_groups, half), in_spe...  2.12 us
    pallas_call x2, Pallas kernels, shards(): pl.pallas_call(functools.partial(join_kernel, chunk, slot_count), in_spec...  1.85 us
    pallas_call x3, Pallas kernels, shards(): pl.pallas_call(functools.partial(sum_kernel, chunk, slot_count, first, la...  0.85 us
  transfers between devices with their start and end apart: 10, of which 7 were waited for; matrix products, arithmetic and copies ran while one was open for 0% of the time, Pallas kernels for 7%

profile of v9, /device:TPU:0, one launch (start us, length us, event | category | flops | bytes accessed | tf_op | source)
XLA Modules:
  0.0 28.6 jit_solution(11931674624335533531)
XLA Ops:
  0.0 2.1 %gram_rows.1 = (bf16[4,272,128]{2,1,0:T(8,128)(2,1)S(1)}, bf16[4,272,128]{2,1,0:T(8,128)(2,1)S(1)}, bf16[4,192,128]{2,1,0:T(8,128)(2,1)S(1)}, bf16[4,192,128]{2,1,0:T(8,128)(2,1)S(1)}) custom-call(s32[2,4]{1,0:T(2,128)} %groups_hbm.1, bf16[2,512,512]{2,1,0:T(8,128)(2,1)} %cols_hbm.1), custom_call_target="tpu_custom_call" | custom-call | tf_op jit(solution)/shard_map/gram_rows/pallas_call | solution.py:269
  2.1 0.5 %collective-permute-start = (bf16[4,272,128]{2,1,0:T(8,128)(2,1)S(1)}, bf16[4,272,128]{2,1,0:T(8,128)(2,1)S(1)}, u32[]{:S(2)}, u32[]{:S(2)}) collective-permute-start(bf16[4,272,128]{2,1,0:T(8,128)(2,1)S(1)} %get-tuple-element.20), channel_id=1, source_target_pairs={{0,1},{1,0},{2,3},{3,2},{4,5},{5,4},{6,7},{7,6},{8,9},{9,8},{10,11... | collective-permute-start | bytes 835592 | tf_op jit(solution)/shard_map/ppermute | solution.py:263
  2.6 0.1 collective-permute-start.4
  2.7 1.1 %collective-permute-done.got_ref.refs_1_ = bf16[4,272,128]{2,1,0:T(8,128)(2,1)S(1)} collective-permute-done((bf16[4,272,128]{2,1,0:T(8,128)(2,1)S(1)}, bf16[4,272,128]{2,1,0:T(8,128)(2,1)S(1)}, u32[]{:S(2)}, u32[]{:S(2)}) %collective-permute-start) | collective-permute-done | bytes 278560 | tf_op jit(solution)/shard_map/ppermute | solution.py:263
  3.9 3.0 %collective-permute-start.1 = (bf16[2,272,128]{2,1,0:T(8,128)(2,1)S(1)}, bf16[2,272,128]{2,1,0:T(8,128)(2,1)S(1)}, u32[]{:S(2)}, u32[]{:S(2)}) collective-permute-start(bf16[2,272,128]{2,1,0:T(8,128)(2,1)S(1)} %get-tuple-element.21), channel_id=1, source_target_pairs={{0,4},{1,5},{2,6},{3,7},{4,0},{5,1},{6,2},{7,3},{8,12},{9,13},{10,... | collective-permute-start | bytes 417800 | tf_op jit(solution)/shard_map/ppermute | solution.py:263
  6.9 1.5 %collective-permute-start.3 = (bf16[2,272,128]{2,1,0:T(8,128)(2,1)S(1)}, bf16[2,272,128]{2,1,0:T(8,128)(2,1)S(1)}, u32[]{:S(2)}, u32[]{:S(2)}) collective-permute-start(bf16[2,272,128]{2,1,0:T(8,128)(2,1)S(1)} %get-tuple-element.23), channel_id=1, source_target_pairs={{0,2},{1,3},{2,0},{3,1},{4,6},{5,7},{6,4},{7,5},{8,10},{9,11},{10,... | collective-permute-start | bytes 417800 | tf_op jit(solution)/shard_map/ppermute | solution.py:263
  8.4 0.0 collective-permute-start.2
  8.4 0.0 collective-permute-done.4.got_ref.refs_6_
  8.4 2.7 %collective-permute-done.1.refs_0_.refs_2_ = bf16[2,272,128]{2,1,0:T(8,128)(2,1)S(1)} collective-permute-done((bf16[2,272,128]{2,1,0:T(8,128)(2,1)S(1)}, bf16[2,272,128]{2,1,0:T(8,128)(2,1)S(1)}, u32[]{:S(2)}, u32[]{:S(2)}) %collective-permute-start.1) | collective-permute-done | bytes 139296 | tf_op jit(solution)/shard_map/ppermute | solution.py:263
  11.1 2.3 %collective-permute-start.5 = (bf16[2,192,128]{2,1,0:T(8,128)(2,1)S(1)}, bf16[2,192,128]{2,1,0:T(8,128)(2,1)S(1)}, u32[]{:S(2)}, u32[]{:S(2)}) collective-permute-start(bf16[2,192,128]{2,1,0:T(8,128)(2,1)S(1)} %get-tuple-element.26), channel_id=1, source_target_pairs={{0,4},{1,5},{2,6},{3,7},{4,0},{5,1},{6,2},{7,3},{8,12},{9,13},{10,... | collective-permute-start | bytes 294920 | tf_op jit(solution)/shard_map/ppermute | solution.py:263
  13.5 1.0 %collective-permute-start.6 = (bf16[2,192,128]{2,1,0:T(8,128)(2,1)S(1)}, bf16[2,192,128]{2,1,0:T(8,128)(2,1)S(1)}, u32[]{:S(2)}, u32[]{:S(2)}) collective-permute-start(bf16[2,192,128]{2,1,0:T(8,128)(2,1)S(1)} %get-tuple-element.27), channel_id=1, source_target_pairs={{0,6},{1,7},{2,4},{3,5},{4,2},{5,3},{6,0},{7,1},{8,14},{9,15},{10,... | collective-permute-start | bytes 294920 | tf_op jit(solution)/shard_map/ppermute | solution.py:263
  14.5 0.5 %collective-permute-start.7 = (bf16[2,192,128]{2,1,0:T(8,128)(2,1)S(1)}, bf16[2,192,128]{2,1,0:T(8,128)(2,1)S(1)}, u32[]{:S(2)}, u32[]{:S(2)}) collective-permute-start(bf16[2,192,128]{2,1,0:T(8,128)(2,1)S(1)} %get-tuple-element.28), channel_id=1, source_target_pairs={{0,2},{1,3},{2,0},{3,1},{4,6},{5,7},{6,4},{7,5},{8,10},{9,11},{10,... | collective-permute-start | bytes 294920 | tf_op jit(solution)/shard_map/ppermute | solution.py:263
  15.0 0.2 collective-permute-done.3.refs_4_.refs_3_
  15.3 0.2 sum_offsets.4.refs_0_
  15.5 0.5 %collective-permute-done.2.refs_3_.refs_1_ = bf16[2,272,128]{2,1,0:T(8,128)(2,1)S(1)} collective-permute-done((bf16[2,272,128]{2,1,0:T(8,128)(2,1)S(1)}, bf16[2,272,128]{2,1,0:T(8,128)(2,1)S(1)}, u32[]{:S(2)}, u32[]{:S(2)}) %collective-permute-start.2) | collective-permute-done | bytes 139296 | tf_op jit(solution)/shard_map/ppermute | solution.py:263
  15.9 0.3 sum_offsets.5
  16.3 2.7 %collective-permute-start.9 = (f16[464,128]{1,0:T(8,128)(2,1)S(1)}, f16[464,128]{1,0:T(8,128)(2,1)S(1)}, u32[]{:S(2)}, u32[]{:S(2)}) collective-permute-start(f16[464,128]{1,0:T(8,128)(2,1)S(1)} %convert_element_type.14), channel_id=1, source_target_pairs={{0,8},{1,9},{2,10},{3,11},{4,12},{5,13},{6,14},{7,15},{8,0},{9,1},... | collective-permute-start | bytes 356360 | tf_op jit(solution)/shard_map/ppermute | solution.py:263
  18.9 0.0 collective-permute-done.5.refs_7_
  18.9 1.5 %collective-permute-done.6.refs_8_ = bf16[2,192,128]{2,1,0:T(8,128)(2,1)S(1)} collective-permute-done((bf16[2,192,128]{2,1,0:T(8,128)(2,1)S(1)}, bf16[2,192,128]{2,1,0:T(8,128)(2,1)S(1)}, u32[]{:S(2)}, u32[]{:S(2)}) %collective-permute-start.6) | collective-permute-done | bytes 98336 | tf_op jit(solution)/shard_map/ppermute | solution.py:263
  20.4 0.0 collective-permute-done.7.refs_9_
  20.4 0.4 %sum_offsets.3 = (f32[768,128]{1,0:T(8,128)S(1)}, f32[400,128]{1,0:T(8,128)S(1)}) custom-call(bf16[4,272,128]{2,1,0:T(8,128)(2,1)S(1)} %get-tuple-element.19.keep_ref.refs_0_, bf16[4,272,128]{2,1,0:T(8,128)(2,1)S(1)} %collective-permute-done.got_ref.refs_1_, bf16[2,272,128]{2,1,0:T(8,128)(2,1)S(1)} %collective-permute-done.1.refs_0_.refs_2_, ...), custom_call_target="tpu_custom_call" | custom-call | tf_op jit(solution)/shard_map/sum_offsets/pallas_call | solution.py:312
  20.8 2.5 %collective-permute-start.8 = (f16[400,128]{1,0:T(8,128)(2,1)S(1)}, f16[400,128]{1,0:T(8,128)(2,1)S(1)}, u32[]{:S(2)}, u32[]{:S(2)}) collective-permute-start(f16[400,128]{1,0:T(8,128)(2,1)S(1)} %convert_element_type.12), channel_id=1, source_target_pairs={{0,8},{1,9},{2,10},{3,11},{4,12},{5,13},{6,14},{7,15},{8,0},{9,1},... | collective-permute-start | bytes 307208 | tf_op jit(solution)/shard_map/ppermute | solution.py:263
  23.4 1.5 %collective-permute-done.9 = f16[464,128]{1,0:T(8,128)(2,1)S(1)} collective-permute-done((f16[464,128]{1,0:T(8,128)(2,1)S(1)}, f16[464,128]{1,0:T(8,128)(2,1)S(1)}, u32[]{:S(2)}, u32[]{:S(2)}) %collective-permute-start.9) | collective-permute-done | bytes 118816 | tf_op jit(solution)/shard_map/ppermute | solution.py:263
  24.9 1.0 %join_offsets.2.refs_0_ = f32[7,128,128]{2,1,0:T(8,128)} custom-call(f32[928,128]{1,0:T(8,128)S(1)} %get-tuple-element.31.sums_ref, f32[464,128]{1,0:T(8,128)S(1)} %convert_element_type.15.far_ref), custom_call_target="tpu_custom_call" | custom-call | tf_op jit(solution)/shard_map/join_offsets/pallas_call | solution.py:327
  26.0 1.8 %collective-permute-done.8 = f16[400,128]{1,0:T(8,128)(2,1)S(1)} collective-permute-done((f16[400,128]{1,0:T(8,128)(2,1)S(1)}, f16[400,128]{1,0:T(8,128)(2,1)S(1)}, u32[]{:S(2)}, u32[]{:S(2)}) %collective-permute-start.8) | collective-permute-done | bytes 102432 | tf_op jit(solution)/shard_map/ppermute | solution.py:263
  27.8 0.8 %join_offsets.3 = f32[7,128,128]{2,1,0:T(8,128)} custom-call(f32[768,128]{1,0:T(8,128)S(1)} %get-tuple-element.29.sums_ref, f32[400,128]{1,0:T(8,128)S(1)} %convert_element_type.13.far_ref, f32[7,128,128]{2,1,0:T(8,128)} %join_offsets.2.refs_0_), custom_call_target="tpu_custom_call", output_to_operand_aliasing={{}: (2, {})} | custom-call | tf_op jit(solution)/shard_map/join_offsets/pallas_call | solution.py:327
  (6 shorter events, 0.1 us)
Async XLA Ops:
  2.1 1.7 %collective-permute-start = (bf16[4,272,128]{2,1,0:T(8,128)(2,1)S(1)}, bf16[4,272,128]{2,1,0:T(8,128)(2,1)S(1)}, u32[]{:S(2)}, u32[]{:S(2)}) collective-permute-start(bf16[4,272,128]{2,1,0:T(8,128)(2,1)S(1)} %get-tuple-element.20), channel_id=1, source_target_pairs={{0,1},{1,0},{2,3},{3,2},{4,5},{5,4},{6,7},{7,6},{8,9},{9,8},{10,11... | collective-permute-start | bytes 835592 | tf_op jit(solution)/shard_map/ppermute | solution.py:263
  2.6 5.8 %collective-permute-start.4 = (bf16[4,192,128]{2,1,0:T(8,128)(2,1)S(1)}, bf16[4,192,128]{2,1,0:T(8,128)(2,1)S(1)}, u32[]{:S(2)}, u32[]{:S(2)}) collective-permute-start(bf16[4,192,128]{2,1,0:T(8,128)(2,1)S(1)} %get-tuple-element.25), channel_id=1, source_target_pairs={{0,1},{1,0},{2,3},{3,2},{4,5},{5,4},{6,7},{7,6},{8,9},{9,8},{10,11... | collective-permute-start | bytes 589832 | tf_op jit(solution)/shard_map/ppermute | solution.py:263
  3.9 7.3 %collective-permute-start.1 = (bf16[2,272,128]{2,1,0:T(8,128)(2,1)S(1)}, bf16[2,272,128]{2,1,0:T(8,128)(2,1)S(1)}, u32[]{:S(2)}, u32[]{:S(2)}) collective-permute-start(bf16[2,272,128]{2,1,0:T(8,128)(2,1)S(1)} %get-tuple-element.21), channel_id=1, source_target_pairs={{0,4},{1,5},{2,6},{3,7},{4,0},{5,1},{6,2},{7,3},{8,12},{9,13},{10,... | collective-permute-start | bytes 417800 | tf_op jit(solution)/shard_map/ppermute | solution.py:263
  6.9 8.4 %collective-permute-start.3 = (bf16[2,272,128]{2,1,0:T(8,128)(2,1)S(1)}, bf16[2,272,128]{2,1,0:T(8,128)(2,1)S(1)}, u32[]{:S(2)}, u32[]{:S(2)}) collective-permute-start(bf16[2,272,128]{2,1,0:T(8,128)(2,1)S(1)} %get-tuple-element.23), channel_id=1, source_target_pairs={{0,2},{1,3},{2,0},{3,1},{4,6},{5,7},{6,4},{7,5},{8,10},{9,11},{10,... | collective-permute-start | bytes 417800 | tf_op jit(solution)/shard_map/ppermute | solution.py:263
  8.4 7.5 %collective-permute-start.2 = (bf16[2,272,128]{2,1,0:T(8,128)(2,1)S(1)}, bf16[2,272,128]{2,1,0:T(8,128)(2,1)S(1)}, u32[]{:S(2)}, u32[]{:S(2)}) collective-permute-start(bf16[2,272,128]{2,1,0:T(8,128)(2,1)S(1)} %get-tuple-element.22), channel_id=1, source_target_pairs={{0,6},{1,7},{2,4},{3,5},{4,2},{5,3},{6,0},{7,1},{8,14},{9,15},{10,... | collective-permute-start | bytes 417800 | tf_op jit(solution)/shard_map/ppermute | solution.py:263
  11.1 7.8 %collective-permute-start.5 = (bf16[2,192,128]{2,1,0:T(8,128)(2,1)S(1)}, bf16[2,192,128]{2,1,0:T(8,128)(2,1)S(1)}, u32[]{:S(2)}, u32[]{:S(2)}) collective-permute-start(bf16[2,192,128]{2,1,0:T(8,128)(2,1)S(1)} %get-tuple-element.26), channel_id=1, source_target_pairs={{0,4},{1,5},{2,6},{3,7},{4,0},{5,1},{6,2},{7,3},{8,12},{9,13},{10,... | collective-permute-start | bytes 294920 | tf_op jit(solution)/shard_map/ppermute | solution.py:263
  13.5 7.0 %collective-permute-start.6 = (bf16[2,192,128]{2,1,0:T(8,128)(2,1)S(1)}, bf16[2,192,128]{2,1,0:T(8,128)(2,1)S(1)}, u32[]{:S(2)}, u32[]{:S(2)}) collective-permute-start(bf16[2,192,128]{2,1,0:T(8,128)(2,1)S(1)} %get-tuple-element.27), channel_id=1, source_target_pairs={{0,6},{1,7},{2,4},{3,5},{4,2},{5,3},{6,0},{7,1},{8,14},{9,15},{10,... | collective-permute-start | bytes 294920 | tf_op jit(solution)/shard_map/ppermute | solution.py:263
  14.5 5.9 %collective-permute-start.7 = (bf16[2,192,128]{2,1,0:T(8,128)(2,1)S(1)}, bf16[2,192,128]{2,1,0:T(8,128)(2,1)S(1)}, u32[]{:S(2)}, u32[]{:S(2)}) collective-permute-start(bf16[2,192,128]{2,1,0:T(8,128)(2,1)S(1)} %get-tuple-element.28), channel_id=1, source_target_pairs={{0,2},{1,3},{2,0},{3,1},{4,6},{5,7},{6,4},{7,5},{8,10},{9,11},{10,... | collective-permute-start | bytes 294920 | tf_op jit(solution)/shard_map/ppermute | solution.py:263
  16.3 8.7 %collective-permute-start.9 = (f16[464,128]{1,0:T(8,128)(2,1)S(1)}, f16[464,128]{1,0:T(8,128)(2,1)S(1)}, u32[]{:S(2)}, u32[]{:S(2)}) collective-permute-start(f16[464,128]{1,0:T(8,128)(2,1)S(1)} %convert_element_type.14), channel_id=1, source_target_pairs={{0,8},{1,9},{2,10},{3,11},{4,12},{5,13},{6,14},{7,15},{8,0},{9,1},... | collective-permute-start | bytes 356360 | tf_op jit(solution)/shard_map/ppermute | solution.py:263
  20.8 7.0 %collective-permute-start.8 = (f16[400,128]{1,0:T(8,128)(2,1)S(1)}, f16[400,128]{1,0:T(8,128)(2,1)S(1)}, u32[]{:S(2)}, u32[]{:S(2)}) collective-permute-start(f16[400,128]{1,0:T(8,128)(2,1)S(1)} %convert_element_type.12), channel_id=1, source_target_pairs={{0,8},{1,9},{2,10},{3,11},{4,12},{5,13},{6,14},{7,15},{8,0},{9,1},... | collective-permute-start | bytes 307208 | tf_op jit(solution)/shard_map/ppermute | solution.py:263

commit v10 on v9

--- a/solution.py
+++ b/solution.py
@@ -145,7 +145,7 @@
 
 def order_of(chunk, pair_count):
     def key(pair):
-        return (0 if chunk == 0 else -pair.bit_length(), pair.bit_count(), -pair)
+        return (pair.bit_count(), -pair)
 
     return sorted(range(1, pair_count), key=key)
 

time: 28.8 us -> 28.9 us (level)
  waiting for transfers between devices: 9.4 us -> 10.1 us
  starting transfers between devices: 14.2 us -> 13.6 us
    ppermute x10, waiting for transfers between devices: 9.4 us -> 10.1 us  [permute(): return lax.ppermute(values, 'group', pairs)]
    ppermute x10, starting transfers between devices: 14.2 us -> 13.6 us  [permute(): return lax.ppermute(values, 'group', pairs)]
where the time goes in v10:
time: 28.9 us; the launch traced here: 28.7 us
  starting transfers between devices  13.6 us (47%)
  waiting for transfers between devices  10.1 us (35%)
  Pallas kernels  4.87 us (17%)
    ppermute x10, starting transfers between devices, permute(): return lax.ppermute(values, 'group', pairs)  13.6 us
    ppermute x10, waiting for transfers between devices, permute(): return lax.ppermute(values, 'group', pairs)  10.1 us
    pallas_call x1, Pallas kernels, shards(): pl.pallas_call(functools.partial(gram_kernel, total_groups, half), in_spe...  2.12 us
    pallas_call x2, Pallas kernels, shards(): pl.pallas_call(functools.partial(join_kernel, chunk, slot_count), in_spec...  1.85 us
    pallas_call x3, Pallas kernels, shards(): pl.pallas_call(functools.partial(sum_kernel, chunk, slot_count, first, la...  0.85 us
  transfers between devices with their start and end apart: 10, of which 7 were waited for; matrix products, arithmetic and copies ran while one was open for 0% of the time, Pallas kernels for 7%

profile of v10, /device:TPU:0, one launch (start us, length us, event | category | flops | bytes accessed | tf_op | source)
XLA Modules:
  0.0 28.7 jit_solution(15325138419930928780)
XLA Ops:
  0.0 2.1 %gram_rows.1 = (bf16[4,272,128]{2,1,0:T(8,128)(2,1)S(1)}, bf16[4,272,128]{2,1,0:T(8,128)(2,1)S(1)}, bf16[4,192,128]{2,1,0:T(8,128)(2,1)S(1)}, bf16[4,192,128]{2,1,0:T(8,128)(2,1)S(1)}) custom-call(s32[2,4]{1,0:T(2,128)} %groups_hbm.1, bf16[2,512,512]{2,1,0:T(8,128)(2,1)} %cols_hbm.1), custom_call_target="tpu_custom_call" | custom-call | tf_op jit(solution)/shard_map/gram_rows/pallas_call | solution.py:269
  2.1 0.5 %collective-permute-start = (bf16[4,272,128]{2,1,0:T(8,128)(2,1)S(1)}, bf16[4,272,128]{2,1,0:T(8,128)(2,1)S(1)}, u32[]{:S(2)}, u32[]{:S(2)}) collective-permute-start(bf16[4,272,128]{2,1,0:T(8,128)(2,1)S(1)} %get-tuple-element.20), channel_id=1, source_target_pairs={{0,1},{1,0},{2,3},{3,2},{4,5},{5,4},{6,7},{7,6},{8,9},{9,8},{10,11... | collective-permute-start | bytes 835592 | tf_op jit(solution)/shard_map/ppermute | solution.py:263
  2.6 0.1 collective-permute-start.4
  2.7 1.1 %collective-permute-done.got_ref.refs_1_ = bf16[4,272,128]{2,1,0:T(8,128)(2,1)S(1)} collective-permute-done((bf16[4,272,128]{2,1,0:T(8,128)(2,1)S(1)}, bf16[4,272,128]{2,1,0:T(8,128)(2,1)S(1)}, u32[]{:S(2)}, u32[]{:S(2)}) %collective-permute-start) | collective-permute-done | bytes 278560 | tf_op jit(solution)/shard_map/ppermute | solution.py:263
  3.9 3.0 %collective-permute-start.1 = (bf16[2,272,128]{2,1,0:T(8,128)(2,1)S(1)}, bf16[2,272,128]{2,1,0:T(8,128)(2,1)S(1)}, u32[]{:S(2)}, u32[]{:S(2)}) collective-permute-start(bf16[2,272,128]{2,1,0:T(8,128)(2,1)S(1)} %get-tuple-element.21), channel_id=1, source_target_pairs={{0,4},{1,5},{2,6},{3,7},{4,0},{5,1},{6,2},{7,3},{8,12},{9,13},{10,... | collective-permute-start | bytes 417800 | tf_op jit(solution)/shard_map/ppermute | solution.py:263
  6.9 1.5 %collective-permute-start.2 = (bf16[2,272,128]{2,1,0:T(8,128)(2,1)S(1)}, bf16[2,272,128]{2,1,0:T(8,128)(2,1)S(1)}, u32[]{:S(2)}, u32[]{:S(2)}) collective-permute-start(bf16[2,272,128]{2,1,0:T(8,128)(2,1)S(1)} %get-tuple-element.22), channel_id=1, source_target_pairs={{0,2},{1,3},{2,0},{3,1},{4,6},{5,7},{6,4},{7,5},{8,10},{9,11},{10,... | collective-permute-start | bytes 417800 | tf_op jit(solution)/shard_map/ppermute | solution.py:263
  8.4 0.0 collective-permute-start.3
  8.4 0.0 collective-permute-done.4.got_ref.refs_6_
  8.4 2.7 %collective-permute-done.1.refs_0_.refs_2_ = bf16[2,272,128]{2,1,0:T(8,128)(2,1)S(1)} collective-permute-done((bf16[2,272,128]{2,1,0:T(8,128)(2,1)S(1)}, bf16[2,272,128]{2,1,0:T(8,128)(2,1)S(1)}, u32[]{:S(2)}, u32[]{:S(2)}) %collective-permute-start.1) | collective-permute-done | bytes 139296 | tf_op jit(solution)/shard_map/ppermute | solution.py:263
  11.2 2.3 %collective-permute-start.5 = (bf16[2,192,128]{2,1,0:T(8,128)(2,1)S(1)}, bf16[2,192,128]{2,1,0:T(8,128)(2,1)S(1)}, u32[]{:S(2)}, u32[]{:S(2)}) collective-permute-start(bf16[2,192,128]{2,1,0:T(8,128)(2,1)S(1)} %get-tuple-element.26), channel_id=1, source_target_pairs={{0,4},{1,5},{2,6},{3,7},{4,0},{5,1},{6,2},{7,3},{8,12},{9,13},{10,... | collective-permute-start | bytes 294920 | tf_op jit(solution)/shard_map/ppermute | solution.py:263
  13.5 1.5 %collective-permute-start.6 = (bf16[2,192,128]{2,1,0:T(8,128)(2,1)S(1)}, bf16[2,192,128]{2,1,0:T(8,128)(2,1)S(1)}, u32[]{:S(2)}, u32[]{:S(2)}) collective-permute-start(bf16[2,192,128]{2,1,0:T(8,128)(2,1)S(1)} %get-tuple-element.27), channel_id=1, source_target_pairs={{0,2},{1,3},{2,0},{3,1},{4,6},{5,7},{6,4},{7,5},{8,10},{9,11},{10,... | collective-permute-start | bytes 294920 | tf_op jit(solution)/shard_map/ppermute | solution.py:263
  15.0 0.0 collective-permute-start.7
  15.0 0.4 %collective-permute-done.2.refs_3_ = bf16[2,272,128]{2,1,0:T(8,128)(2,1)S(1)} collective-permute-done((bf16[2,272,128]{2,1,0:T(8,128)(2,1)S(1)}, bf16[2,272,128]{2,1,0:T(8,128)(2,1)S(1)}, u32[]{:S(2)}, u32[]{:S(2)}) %collective-permute-start.2) | collective-permute-done | bytes 139296 | tf_op jit(solution)/shard_map/ppermute | solution.py:263
  15.4 0.2 sum_offsets.4.refs_0_
  15.6 0.3 %collective-permute-done.3.refs_4_.refs_1_ = bf16[2,272,128]{2,1,0:T(8,128)(2,1)S(1)} collective-permute-done((bf16[2,272,128]{2,1,0:T(8,128)(2,1)S(1)}, bf16[2,272,128]{2,1,0:T(8,128)(2,1)S(1)}, u32[]{:S(2)}, u32[]{:S(2)}) %collective-permute-start.3) | collective-permute-done | bytes 139296 | tf_op jit(solution)/shard_map/ppermute | solution.py:263
  15.9 0.3 sum_offsets.5
  16.3 2.6 %collective-permute-start.9 = (f16[464,128]{1,0:T(8,128)(2,1)S(1)}, f16[464,128]{1,0:T(8,128)(2,1)S(1)}, u32[]{:S(2)}, u32[]{:S(2)}) collective-permute-start(f16[464,128]{1,0:T(8,128)(2,1)S(1)} %convert_element_type.14), channel_id=1, source_target_pairs={{0,8},{1,9},{2,10},{3,11},{4,12},{5,13},{6,14},{7,15},{8,0},{9,1},... | collective-permute-start | bytes 356360 | tf_op jit(solution)/shard_map/ppermute | solution.py:263
  18.9 0.0 collective-permute-done.5.refs_7_
  18.9 0.0 collective-permute-done.6.refs_8_
  18.9 2.4 %collective-permute-done.7.refs_9_ = bf16[2,192,128]{2,1,0:T(8,128)(2,1)S(1)} collective-permute-done((bf16[2,192,128]{2,1,0:T(8,128)(2,1)S(1)}, bf16[2,192,128]{2,1,0:T(8,128)(2,1)S(1)}, u32[]{:S(2)}, u32[]{:S(2)}) %collective-permute-start.7) | collective-permute-done | bytes 98336 | tf_op jit(solution)/shard_map/ppermute | solution.py:263
  21.3 0.4 %sum_offsets.3 = (f32[768,128]{1,0:T(8,128)S(1)}, f32[400,128]{1,0:T(8,128)S(1)}) custom-call(bf16[4,272,128]{2,1,0:T(8,128)(2,1)S(1)} %get-tuple-element.19.keep_ref.refs_0_, bf16[4,272,128]{2,1,0:T(8,128)(2,1)S(1)} %collective-permute-done.got_ref.refs_1_, bf16[2,272,128]{2,1,0:T(8,128)(2,1)S(1)} %collective-permute-done.1.refs_0_.refs_2_, ...), custom_call_target="tpu_custom_call" | custom-call | tf_op jit(solution)/shard_map/sum_offsets/pallas_call | solution.py:312
  21.7 1.9 %collective-permute-start.8 = (f16[400,128]{1,0:T(8,128)(2,1)S(1)}, f16[400,128]{1,0:T(8,128)(2,1)S(1)}, u32[]{:S(2)}, u32[]{:S(2)}) collective-permute-start(f16[400,128]{1,0:T(8,128)(2,1)S(1)} %convert_element_type.12), channel_id=1, source_target_pairs={{0,8},{1,9},{2,10},{3,11},{4,12},{5,13},{6,14},{7,15},{8,0},{9,1},... | collective-permute-start | bytes 307208 | tf_op jit(solution)/shard_map/ppermute | solution.py:263
  23.7 1.1 %collective-permute-done.9 = f16[464,128]{1,0:T(8,128)(2,1)S(1)} collective-permute-done((f16[464,128]{1,0:T(8,128)(2,1)S(1)}, f16[464,128]{1,0:T(8,128)(2,1)S(1)}, u32[]{:S(2)}, u32[]{:S(2)}) %collective-permute-start.9) | collective-permute-done | bytes 118816 | tf_op jit(solution)/shard_map/ppermute | solution.py:263
  24.8 1.0 %join_offsets.2.refs_0_ = f32[7,128,128]{2,1,0:T(8,128)} custom-call(f32[928,128]{1,0:T(8,128)S(1)} %get-tuple-element.31.sums_ref, f32[464,128]{1,0:T(8,128)S(1)} %convert_element_type.15.far_ref), custom_call_target="tpu_custom_call" | custom-call | tf_op jit(solution)/shard_map/join_offsets/pallas_call | solution.py:327
  25.8 2.1 %collective-permute-done.8 = f16[400,128]{1,0:T(8,128)(2,1)S(1)} collective-permute-done((f16[400,128]{1,0:T(8,128)(2,1)S(1)}, f16[400,128]{1,0:T(8,128)(2,1)S(1)}, u32[]{:S(2)}, u32[]{:S(2)}) %collective-permute-start.8) | collective-permute-done | bytes 102432 | tf_op jit(solution)/shard_map/ppermute | solution.py:263
  27.9 0.8 %join_offsets.3 = f32[7,128,128]{2,1,0:T(8,128)} custom-call(f32[768,128]{1,0:T(8,128)S(1)} %get-tuple-element.29.sums_ref, f32[400,128]{1,0:T(8,128)S(1)} %convert_element_type.13.far_ref, f32[7,128,128]{2,1,0:T(8,128)} %join_offsets.2.refs_0_), custom_call_target="tpu_custom_call", output_to_operand_aliasing={{}: (2, {})} | custom-call | tf_op jit(solution)/shard_map/join_offsets/pallas_call | solution.py:327
  (6 shorter events, 0.1 us)
Async XLA Ops:
  2.1 1.7 %collective-permute-start = (bf16[4,272,128]{2,1,0:T(8,128)(2,1)S(1)}, bf16[4,272,128]{2,1,0:T(8,128)(2,1)S(1)}, u32[]{:S(2)}, u32[]{:S(2)}) collective-permute-start(bf16[4,272,128]{2,1,0:T(8,128)(2,1)S(1)} %get-tuple-element.20), channel_id=1, source_target_pairs={{0,1},{1,0},{2,3},{3,2},{4,5},{5,4},{6,7},{7,6},{8,9},{9,8},{10,11... | collective-permute-start | bytes 835592 | tf_op jit(solution)/shard_map/ppermute | solution.py:263
  2.6 5.8 %collective-permute-start.4 = (bf16[4,192,128]{2,1,0:T(8,128)(2,1)S(1)}, bf16[4,192,128]{2,1,0:T(8,128)(2,1)S(1)}, u32[]{:S(2)}, u32[]{:S(2)}) collective-permute-start(bf16[4,192,128]{2,1,0:T(8,128)(2,1)S(1)} %get-tuple-element.25), channel_id=1, source_target_pairs={{0,1},{1,0},{2,3},{3,2},{4,5},{5,4},{6,7},{7,6},{8,9},{9,8},{10,11... | collective-permute-start | bytes 589832 | tf_op jit(solution)/shard_map/ppermute | solution.py:263
  3.9 7.3 %collective-permute-start.1 = (bf16[2,272,128]{2,1,0:T(8,128)(2,1)S(1)}, bf16[2,272,128]{2,1,0:T(8,128)(2,1)S(1)}, u32[]{:S(2)}, u32[]{:S(2)}) collective-permute-start(bf16[2,272,128]{2,1,0:T(8,128)(2,1)S(1)} %get-tuple-element.21), channel_id=1, source_target_pairs={{0,4},{1,5},{2,6},{3,7},{4,0},{5,1},{6,2},{7,3},{8,12},{9,13},{10,... | collective-permute-start | bytes 417800 | tf_op jit(solution)/shard_map/ppermute | solution.py:263
  6.9 8.5 %collective-permute-start.2 = (bf16[2,272,128]{2,1,0:T(8,128)(2,1)S(1)}, bf16[2,272,128]{2,1,0:T(8,128)(2,1)S(1)}, u32[]{:S(2)}, u32[]{:S(2)}) collective-permute-start(bf16[2,272,128]{2,1,0:T(8,128)(2,1)S(1)} %get-tuple-element.22), channel_id=1, source_target_pairs={{0,2},{1,3},{2,0},{3,1},{4,6},{5,7},{6,4},{7,5},{8,10},{9,11},{10,... | collective-permute-start | bytes 417800 | tf_op jit(solution)/shard_map/ppermute | solution.py:263
  8.4 7.5 %collective-permute-start.3 = (bf16[2,272,128]{2,1,0:T(8,128)(2,1)S(1)}, bf16[2,272,128]{2,1,0:T(8,128)(2,1)S(1)}, u32[]{:S(2)}, u32[]{:S(2)}) collective-permute-start(bf16[2,272,128]{2,1,0:T(8,128)(2,1)S(1)} %get-tuple-element.23), channel_id=1, source_target_pairs={{0,6},{1,7},{2,4},{3,5},{4,2},{5,3},{6,0},{7,1},{8,14},{9,15},{10,... | collective-permute-start | bytes 417800 | tf_op jit(solution)/shard_map/ppermute | solution.py:263
  11.2 7.8 %collective-permute-start.5 = (bf16[2,192,128]{2,1,0:T(8,128)(2,1)S(1)}, bf16[2,192,128]{2,1,0:T(8,128)(2,1)S(1)}, u32[]{:S(2)}, u32[]{:S(2)}) collective-permute-start(bf16[2,192,128]{2,1,0:T(8,128)(2,1)S(1)} %get-tuple-element.26), channel_id=1, source_target_pairs={{0,4},{1,5},{2,6},{3,7},{4,0},{5,1},{6,2},{7,3},{8,12},{9,13},{10,... | collective-permute-start | bytes 294920 | tf_op jit(solution)/shard_map/ppermute | solution.py:263
  13.5 5.4 %collective-permute-start.6 = (bf16[2,192,128]{2,1,0:T(8,128)(2,1)S(1)}, bf16[2,192,128]{2,1,0:T(8,128)(2,1)S(1)}, u32[]{:S(2)}, u32[]{:S(2)}) collective-permute-start(bf16[2,192,128]{2,1,0:T(8,128)(2,1)S(1)} %get-tuple-element.27), channel_id=1, source_target_pairs={{0,2},{1,3},{2,0},{3,1},{4,6},{5,7},{6,4},{7,5},{8,10},{9,11},{10,... | collective-permute-start | bytes 294920 | tf_op jit(solution)/shard_map/ppermute | solution.py:263
  15.0 6.3 %collective-permute-start.7 = (bf16[2,192,128]{2,1,0:T(8,128)(2,1)S(1)}, bf16[2,192,128]{2,1,0:T(8,128)(2,1)S(1)}, u32[]{:S(2)}, u32[]{:S(2)}) collective-permute-start(bf16[2,192,128]{2,1,0:T(8,128)(2,1)S(1)} %get-tuple-element.28), channel_id=1, source_target_pairs={{0,6},{1,7},{2,4},{3,5},{4,2},{5,3},{6,0},{7,1},{8,14},{9,15},{10,... | collective-permute-start | bytes 294920 | tf_op jit(solution)/shard_map/ppermute | solution.py:263
  16.3 8.5 %collective-permute-start.9 = (f16[464,128]{1,0:T(8,128)(2,1)S(1)}, f16[464,128]{1,0:T(8,128)(2,1)S(1)}, u32[]{:S(2)}, u32[]{:S(2)}) collective-permute-start(f16[464,128]{1,0:T(8,128)(2,1)S(1)} %convert_element_type.14), channel_id=1, source_target_pairs={{0,8},{1,9},{2,10},{3,11},{4,12},{5,13},{6,14},{7,15},{8,0},{9,1},... | collective-permute-start | bytes 356360 | tf_op jit(solution)/shard_map/ppermute | solution.py:263
  21.7 6.2 %collective-permute-start.8 = (f16[400,128]{1,0:T(8,128)(2,1)S(1)}, f16[400,128]{1,0:T(8,128)(2,1)S(1)}, u32[]{:S(2)}, u32[]{:S(2)}) collective-permute-start(f16[400,128]{1,0:T(8,128)(2,1)S(1)} %convert_element_type.12), channel_id=1, source_target_pairs={{0,8},{1,9},{2,10},{3,11},{4,12},{5,13},{6,14},{7,15},{8,0},{9,1},... | collective-permute-start | bytes 307208 | tf_op jit(solution)/shard_map/ppermute | solution.py:263
